TPU v7x, 128 devices: a whole 4x4x4 slice. The times are simulated.
128 devices in a mesh: ctx: 64 (over x, y, z), tp: 2 (over core).
Axes of the slice: x: 4, y: 4, z: 4, core: 2. Of those that a mesh axis runs over, the one named last changes fastest.
Arguments:
- hidden: bfloat16 [8192, 2048], P('ctx', 'tp'), may hold values from -60 to 60
- grad_out: bfloat16 [8192, 2048], P('ctx', 'tp'), may hold values from -6 to 6
- expert_ids: int32 [8192, 4], P('ctx'), may hold values from 0 to 63, all different within a row; in each aligned block of 128 rows (0 to 127, 128 to 255, ...) at most 10 rows name the same one
- gate_weights: float32 [8192, 4], P('ctx'), may hold values from 0.1 to 1
- norm_gain: float32 [2048], P('tp'), may hold values from 0.25 to 1.75
- w_gate: bfloat16 [64, 2048, 1536], P('ctx', None, 'tp'), may hold values from -0.125 to 0.125
- w_up: bfloat16 [64, 2048, 1536], P('ctx', None, 'tp'), may hold values from -0.125 to 0.125
- w_down: bfloat16 [64, 1536, 2048], P('ctx', 'tp'), may hold values from -0.15625 to 0.15625
- queries: bfloat16 [8192, 2048], P('ctx', 'tp'), may hold values from -6 to 6
- forget_logits: bfloat16 [8192, 2048], P('ctx', 'tp'), may hold values from -1 to 16
- values: bfloat16 [8192, 2048], P('ctx', 'tp'), may hold values from -6 to 6
Outputs:
- grad_hidden: bfloat16 [8192, 2048], P('ctx', 'tp')
- grad_queries: bfloat16 [8192, 2048], P('ctx', 'tp')
- grad_logits: bfloat16 [8192, 2048], P('ctx', 'tp')
- grad_values: bfloat16 [8192, 2048], P('ctx', 'tp')
Inputs may be any that keep to these rules, and one draw needn't show every extreme that they name: `expert_ids`: in the 128 rows of one block no expert is named more than 10 times; in some block one expert is named exactly 10 times.
All inputs are finite; a program needn't handle non-finite values.
Results may differ from a plain program's by a relative error of at most 0.0069.
Values may be sent and summed in bfloat16 or wider, within the bound.
No kernel may reach another device: no remote copies, remote signals or barrier semaphores. Data moves between devices by JAX's collectives and lax.ppermute only.
A program may use at most 192 MiB of HBM per device.

v0:
```python
import functools

import jax
import jax.numpy as jnp
from jax import lax
from jax.experimental import pallas as pl
from jax.experimental.pallas import tpu as pltpu
from jax.sharding import PartitionSpec as P

HEAD_DIM = 64
NORM_EPS = 1e-06
LANES = 128
BF16 = jnp.bfloat16
F32 = jnp.float32
EXACT = lax.Precision.HIGHEST
NT = (((1,), (1,)), ((), ()))
TN = (((0,), (0,)), ((), ()))
NN = (((1,), (0,)), ((), ()))


def iota(shape, dim):
    return lax.broadcasted_iota(jnp.int32, shape, dim)


def exact_dot(a, b, dims=NN):
    return lax.dot_general(a, b, dims, precision=EXACT, preferred_element_type=F32)


def fast_dot(a, b, dims=NN):
    return lax.dot_general(a, b, dims, preferred_element_type=F32)


def call(kernel, out_shape, *args, scratch=(), in_specs=None, mib=48, flops=0, nbytes=0):
    return pl.pallas_call(
        kernel,
        out_shape=out_shape,
        in_specs=in_specs or [pl.BlockSpec(memory_space=pltpu.VMEM)] * len(args),
        out_specs=jax.tree.map(lambda _: pl.BlockSpec(memory_space=pltpu.VMEM), out_shape),
        scratch_shapes=list(scratch),
        compiler_params=pltpu.CompilerParams(vmem_limit_bytes=mib << 20),
        cost_estimate=pl.CostEstimate(flops=flops, bytes_accessed=nbytes, transcendentals=0),
    )(*args)


def shape_of(shape, dtype):
    return jax.ShapeDtypeStruct(shape, dtype)


def ranked(ids_ref):
    rows = ids_ref.shape[0]
    lane = iota((rows, LANES), 1)
    named = jnp.zeros((rows, LANES), F32)
    for choice in range(ids_ref.shape[1]):
        named = named + (ids_ref[:, choice : choice + 1] == lane).astype(F32)
    before = (iota((rows, rows), 1) < iota((rows, rows), 0)).astype(BF16)
    rank = fast_dot(before, named.astype(BF16))
    return jnp.where(named > 0.0, rank, -1.0)


def dispatch_kernel(hidden_ref, cot_ref, squares_ref, gain_ref, ids_ref, weight_ref, width, out_ref, rhs, rhs_rem):
    rows = hidden_ref.shape[0]
    row_scale = lax.rsqrt(squares_ref[...] / width + NORM_EPS)
    normed = (hidden_ref[...].astype(F32) * row_scale * gain_ref[...]).astype(BF16)
    rhs[0:rows, :] = normed
    rhs[rows : 2 * rows, :] = cot_ref[...]
    for j in range(8):
        lo, col = 2 * rows * (j % 4), LANES * (j // 4)
        rhs_rem[lo : lo + rows, col : col + LANES] = normed[:, j * LANES : (j + 1) * LANES]
        rhs_rem[lo + rows : lo + 2 * rows, col : col + LANES] = cot_ref[:, j * LANES : (j + 1) * LANES]
    rank = ranked(ids_ref).T
    lane = iota((rows, LANES), 1)
    weight = jnp.zeros((rows, LANES), F32)
    for choice in range(ids_ref.shape[1]):
        weight = weight + jnp.where(
            ids_ref[:, choice : choice + 1] == lane, weight_ref[:, choice : choice + 1], 0.0
        )
    weight = weight.T
    rank_b = rank.astype(BF16)
    for group in range(8):
        expand = (iota((128, LANES), 0) // 16 + group * 8 == iota((128, LANES), 1)).astype(BF16)
        ranks = fast_dot(expand, rank_b)
        weights = exact_dot(expand.astype(F32), weight)
        inner = iota((128, LANES), 0) % 16
        hit = ranks == (inner % 8).astype(F32)
        is_cot = inner >= 8
        left = jnp.concatenate([hit & ~is_cot, hit & is_cot], axis=1).astype(BF16)
        scale = jnp.sum(jnp.where(hit & is_cot, weights, 0.0), axis=1, keepdims=True)
        scale = jnp.where(is_cot[:, :1], scale, 1.0)
        main = (fast_dot(left, rhs[...]) * scale).astype(BF16)
        for j in range(8):
            out_ref[group * 8 : group * 8 + 8, j * 16 : (j + 1) * 16, :] = main[
                :, j * LANES : (j + 1) * LANES
            ].reshape(8, 16, LANES)
        hit = ranks == (8 + inner % 2).astype(F32)
        is_cot = (inner // 2) % 2 == 1
        parts = []
        for j in range(4):
            here = hit & (inner // 4 == j)
            parts += [here & ~is_cot, here & is_cot]
        left = jnp.concatenate(parts, axis=1).astype(BF16)
        scale = jnp.sum(jnp.where(hit & is_cot, weights, 0.0), axis=1, keepdims=True)
        scale = jnp.where(is_cot[:, :1], scale, 1.0)
        rest = (fast_dot(left, rhs_rem[...]) * scale).astype(BF16)
        for half in range(2):
            out_ref[group * 8 : group * 8 + 8, 128 + 16 * half : 144 + 16 * half, :] = rest[
                :, half * LANES : (half + 1) * LANES
            ].reshape(8, 16, LANES)


def table_kernel(ids_ref, main_ref, rest_ref):
    rank = ranked(ids_ref).astype(BF16)
    count = main_ref.shape[1]
    expand = (iota((LANES, count), 1) // 16 == iota((LANES, count), 0)).astype(BF16)
    ranks = fast_dot(rank, expand)
    inner = iota(ranks.shape, 1) % 16
    hit = ranks == (inner % 8).astype(F32)
    rows = ranks.shape[0]
    main_ref[0:rows, :] = (hit & (inner < 8)).astype(BF16)
    main_ref[rows : 2 * rows, :] = (hit & (inner >= 8)).astype(BF16)
    hit = ranks == (8 + inner % 2).astype(F32)
    for j in range(8):
        rest_ref[j * rows : (j + 1) * rows, :] = (hit & (inner // 2 == j)).astype(BF16)


def unpack(raw_ref, x_ref, c_ref, offset):
    count = raw_ref.shape[0]
    for j in range(8):
        tile = raw_ref[:, j * 16 : (j + 1) * 16, :].astype(F32).reshape(count, 2, 8, LANES)
        cols = pl.ds(pl.multiple_of(offset + j * LANES, LANES), LANES)
        x_ref[0 : count * 8, cols] = tile[:, 0].reshape(count * 8, LANES).astype(BF16)
        c_ref[0 : count * 8, cols] = tile[:, 1].reshape(count * 8, LANES).astype(BF16)
    row = iota((128, 128), 0)
    source = (row // 2) % 4 * 32 + row // 16 * 4 + (row // 8) % 2 * 2 + row % 2
    perm = (iota((128, 128), 1) == source).astype(BF16)
    groups = count // 4
    rest = jnp.concatenate(
        [raw_ref[g * 4 : (g + 1) * 4, 128:160, :].reshape(128, LANES) for g in range(groups)], axis=1
    )
    rest = fast_dot(perm, rest)
    for j in range(8):
        cols = pl.ds(pl.multiple_of(offset + j * LANES, LANES), LANES)
        for kind, ref in enumerate((x_ref, c_ref)):
            lo = j * 16 + kind * 8
            ref[count * 8 : count * 10, cols] = jnp.concatenate(
                [rest[lo : lo + 8, g * LANES : (g + 1) * LANES] for g in range(groups)], axis=0
            ).astype(BF16)


def expert_kernel(
    core_ref, own_ref, peer_ref, gate_hbm, up_hbm, down_hbm, keep_ref, send_ref, x, c, gate, up, down, dg, du, sems
):
    copies = [
        pltpu.make_async_copy(source, target, sems.at[number])
        for number, (source, target) in enumerate(((gate_hbm, gate), (up_hbm, up), (down_hbm, down)))
    ]
    for copy in copies:
        copy.start()
    core = core_ref[0]
    half = keep_ref.shape[1]
    unpack(own_ref, x, c, core * half)
    unpack(peer_ref, x, c, (1 - core) * half)
    for copy in copies:
        copy.wait()

    @pl.loop(0, gate.shape[1] // 256)
    def _(step):
        cols = pl.ds(pl.multiple_of(step * 256, 256), 256)
        pre_gate = fast_dot(x[...], gate[:, cols])
        pre_up = fast_dot(x[...], up[:, cols])
        d_act = fast_dot(c[...], down[cols, :], NT)
        sig = jax.nn.sigmoid(pre_gate)
        dg[:, cols] = (d_act * pre_up * sig * (1.0 + pre_gate * (1.0 - sig))).astype(BF16)
        du[:, cols] = (d_act * pre_gate * sig).astype(BF16)

    @pl.loop(0, half // 256)
    def _(step):
        cols = pl.ds(pl.multiple_of(step * 256, 256), 256)
        for ref, first in ((send_ref, (1 - core) * half), (keep_ref, core * half)):
            feats = pl.ds(pl.multiple_of(first + step * 256, 256), 256)
            value = fast_dot(dg[...], gate[feats, :], NT) + fast_dot(du[...], up[feats, :], NT)
            ref[:, cols] = value.astype(ref.dtype)


def pack_kernel(keep_ref, got_ref, out_ref):
    count = out_ref.shape[0]
    for pair in range(4):
        tiles = []
        for j in (2 * pair, 2 * pair + 1):
            cols = slice(j * LANES, (j + 1) * LANES)
            value = keep_ref[0 : count * 8, cols] + got_ref[0 : count * 8, cols].astype(F32)
            tiles.append(value.reshape(count, 8, LANES))
        out_ref[:, pair * 16 : (pair + 1) * 16, :] = jnp.concatenate(tiles, axis=1).astype(BF16)
    rest = (keep_ref[count * 8 :, :] + got_ref[count * 8 :, :].astype(F32)).astype(BF16)
    row = iota((128, 128), 0)
    source = (row // 2) % 8 * 16 + row // 16 * 2 + row % 2
    perm = (iota((128, 128), 1) == source).astype(BF16)
    groups = count // 8
    stacked = jnp.concatenate(
        [
            jnp.concatenate(
                [rest[g * 16 : (g + 1) * 16, j * LANES : (j + 1) * LANES] for j in range(8)], axis=0
            )
            for g in range(groups)
        ],
        axis=1,
    )
    moved = fast_dot(perm, stacked).astype(BF16)
    for g in range(groups):
        out_ref[g * 8 : (g + 1) * 8, 64:80, :] = moved[:, g * LANES : (g + 1) * LANES].reshape(8, 16, LANES)


def combine_kernel(back_ref, main_ref, rest_ref, hidden_ref, gain_ref, gained_ref, dot_ref):
    count = back_ref.shape[0]
    rows = hidden_ref.shape[0]
    main = jnp.concatenate(
        [back_ref[:, m * 16 : (m + 1) * 16, :].reshape(count * 16, LANES) for m in range(4)], axis=1
    )
    main = fast_dot(main_ref[...], main)
    rest = fast_dot(rest_ref[...], back_ref[:, 64:80, :].reshape(count * 16, LANES))
    total = jnp.zeros((rows, LANES), F32)
    for j in range(8):
        cols = slice(j * LANES, (j + 1) * LANES)
        value = main[j % 2 * rows : (j % 2 + 1) * rows, j // 2 * LANES : (j // 2 + 1) * LANES]
        value = (value + rest[j * rows : (j + 1) * rows, :]) * gain_ref[:, cols]
        gained_ref[:, cols] = value
        total = total + value * hidden_ref[:, cols].astype(F32)
    dot_ref[...] = jnp.sum(total, axis=1, keepdims=True)


def log_sigmoid(x):
    return -(jnp.maximum(-x, 0.0) + jnp.log1p(jnp.exp(-jnp.abs(x))))


def decay_kernel(logit_ref, value_ref, total_ref, state_ref):
    rows, feats = logit_ref.shape
    logits = logit_ref[...].astype(F32)
    key = jax.nn.sigmoid(-logits)
    lower = (iota((rows, rows), 0) >= iota((rows, rows), 1)).astype(F32)
    running = exact_dot(lower, log_sigmoid(logits))
    total_ref[...] = running
    end = running[rows - 1 : rows, :]
    key_end = key * jnp.exp(end - running)
    decay = jnp.exp(end)
    same = iota((LANES, LANES), 0) // HEAD_DIM == iota((LANES, LANES), 1) // HEAD_DIM
    pick = iota((HEAD_DIM, LANES), 0) == iota((HEAD_DIM, LANES), 1) % HEAD_DIM
    for pair in range(feats // LANES):
        cols = slice(pair * LANES, (pair + 1) * LANES)
        local = exact_dot(key_end[:, cols], value_ref[:, cols].astype(F32), TN)
        local = jnp.where(same, local, 0.0)
        local = local[:HEAD_DIM] + local[HEAD_DIM:]
        spread = exact_dot(jnp.where(pick, decay[:, cols], 0.0), same.astype(F32))
        for part in range(8):
            state_ref[pair * 8 + part, 0:8, :] = local[part * 8 : (part + 1) * 8, :]
            state_ref[pair * 8 + part, 8:16, :] = spread[part * 8 : (part + 1) * 8, :]


def forward_kernel(piece_ref, out_ref):
    count = piece_ref.shape[0]
    state = jnp.zeros((8, LANES), F32)
    for block in range(count):
        out_ref[block] = state
        state = piece_ref[block, 8:16, :] * state + piece_ref[block, 0:8, :]


def backward_kernel(piece_ref, decay_ref, out_ref):
    count = piece_ref.shape[0]
    state = jnp.zeros((8, LANES), F32)
    for block in range(count - 1, -1, -1):
        out_ref[block] = state
        state = decay_ref[block, 8:16, :] * state + piece_ref[block]


def hidden_kernel(
    hidden_ref, cot_ref, squares_ref, gained_ref, dot_ref, query_ref, total_ref, width, out_ref, piece_ref
):
    row_scale = lax.rsqrt(squares_ref[...] / width + NORM_EPS)
    back = row_scale * gained_ref[...] - hidden_ref[...].astype(F32) * (
        row_scale * row_scale * row_scale * dot_ref[...] / width
    )
    upstream = (cot_ref[...].astype(F32) + back).astype(BF16)
    out_ref[...] = upstream
    query = query_ref[...].astype(F32) * jnp.exp(total_ref[...])
    same = iota((LANES, LANES), 0) // HEAD_DIM == iota((LANES, LANES), 1) // HEAD_DIM
    for pair in range(hidden_ref.shape[1] // LANES):
        cols = slice(pair * LANES, (pair + 1) * LANES)
        elem = exact_dot(query[:, cols], upstream[:, cols].astype(F32), TN)
        elem = jnp.where(same, elem, 0.0)
        elem = elem[:HEAD_DIM] + elem[HEAD_DIM:]
        piece_ref[pair * 8 : (pair + 1) * 8] = elem.reshape(8, 8, LANES)


def final_kernel(
    query_ref,
    logit_ref,
    value_ref,
    total_ref,
    upstream_ref,
    start_ref,
    incoming_ref,
    state_ref,
    query_out,
    logit_out,
    value_out,
):
    rows, feats = query_ref.shape
    lower = iota((rows, rows), 0) >= iota((rows, rows), 1)
    upper = iota((rows, rows), 0) <= iota((rows, rows), 1)
    same = iota((LANES, LANES), 0) // HEAD_DIM == iota((LANES, LANES), 1) // HEAD_DIM
    first = iota((rows, LANES), 1) < HEAD_DIM

    def split(array):
        zero = jnp.zeros_like(array)
        return jnp.where(first, array, zero), jnp.where(first, zero, array)

    def spread(array):
        return jnp.where(same, jnp.concatenate([array, array], axis=0), 0.0)

    for pair in range(feats // LANES):
        cols = slice(pair * LANES, (pair + 1) * LANES)
        eight = slice(pair * 8, (pair + 1) * 8)
        query = query_ref[:, cols].astype(F32)
        logits = logit_ref[:, cols].astype(F32)
        key = jax.nn.sigmoid(-logits)
        running = total_ref[:, cols]
        end = running[rows - 1 : rows, :]
        centre = 0.5 * end
        grow = jnp.exp(running - centre)
        shrink = jnp.exp(centre - running)
        value = value_ref[:, cols]
        upstream = upstream_ref[:, cols]
        value_f, upstream_f = value.astype(F32), upstream.astype(F32)
        start = start_ref[eight].reshape(HEAD_DIM, LANES)
        incoming = incoming_ref[eight].reshape(HEAD_DIM, LANES)
        local = state_ref[eight, 0:8, :].reshape(HEAD_DIM, LANES)
        decay = state_ref[eight, 8:16, :].reshape(HEAD_DIM, LANES)
        start_2, incoming_2 = spread(start), spread(incoming)
        query_s, key_s = query * grow, key * shrink
        up_split, value_split = split(upstream), split(value)
        query_split, key_split = split(query_s), split(key_s)
        raw = [fast_dot(u, v, NT) for u, v in zip(up_split, value_split)]
        pairs = jnp.concatenate([jnp.where(lower, r, 0.0) for r in raw], axis=1)
        query_grad = jnp.exp(running) * exact_dot(upstream_f, start_2, NT) + grow * exact_dot(
            pairs, jnp.concatenate(key_split, axis=0)
        )
        raw = [fast_dot(v, u, NT) for u, v in zip(up_split, value_split)]
        pairs = jnp.concatenate([jnp.where(upper, r, 0.0) for r in raw], axis=1)
        tail = jnp.exp(end - running)
        key_grad = tail * exact_dot(value_f, incoming_2, NT) + shrink * exact_dot(
            pairs, jnp.concatenate(query_split, axis=0)
        )
        raw = [exact_dot(k, q, NT) for k, q in zip(key_split, query_split)]
        pairs = jnp.concatenate([jnp.where(upper, r, 0.0) for r in raw], axis=1)
        value_grad = exact_dot(
            pairs, jnp.concatenate([u.astype(F32) for u in up_split], axis=0)
        ) + exact_dot(key * tail, incoming_2)
        past = spread((decay * start + local) * incoming)
        past = exact_dot(jnp.ones((8, LANES), F32), past, NT)[0:1, :]
        suffix = exact_dot(upper.astype(F32), query * query_grad - key * key_grad) + past
        logit_grad = suffix * key - key_grad * key * (1.0 - key)
        query_out[:, cols] = query_grad.astype(BF16)
        logit_out[:, cols] = logit_grad.astype(BF16)
        value_out[:, cols] = value_grad.astype(BF16)


def on_device(
    hidden, grad_out, expert_ids, gate_weights, norm_gain, w_gate, w_up, w_down, queries, forget_logits, values
):
    rows, feats = hidden.shape
    ctx = lax.axis_size("ctx")
    width = w_gate.shape[1]
    units = w_gate.shape[2]
    slots = ctx * 10
    core = lax.axis_index("tp")
    swap = [(0, 1), (1, 0)]
    gain = norm_gain.reshape(1, feats)

    def exchange(array):
        return lax.all_to_all(array, "ctx", split_axis=0, concat_axis=0, tiled=True)

    hidden_f = hidden.astype(F32)
    squares = lax.psum(jnp.sum(hidden_f * hidden_f, axis=1), "tp").reshape(rows, 1)

    sent = call(
        lambda h, g, s, n, i, w, o, a, b: dispatch_kernel(h, g, s, n, i, w, width, o, a, b),
        shape_of((ctx, 160, LANES), BF16),
        hidden,
        grad_out,
        squares,
        gain,
        expert_ids,
        gate_weights,
        scratch=(pltpu.VMEM((2 * rows, feats), BF16), pltpu.VMEM((8 * rows, 2 * LANES), BF16)),
        flops=1 << 30,
        nbytes=4 << 20,
    )
    own = exchange(sent)
    main_table, rest_table = call(
        table_kernel,
        (shape_of((2 * rows, ctx * 16), BF16), shape_of((8 * rows, ctx * 16), BF16)),
        expert_ids,
        flops=1 << 26,
        nbytes=3 << 20,
    )
    total, state = call(
        decay_kernel,
        (shape_of((rows, feats), F32), shape_of((ctx, 16, LANES), F32)),
        forget_logits,
        values,
        flops=1 << 30,
        nbytes=2 << 20,
    )
    pieces = exchange(state)
    starts = exchange(call(forward_kernel, shape_of((ctx, 8, LANES), F32), pieces, nbytes=1 << 20))

    peer = lax.ppermute(own, "tp", swap)
    vmem, hbm = pl.BlockSpec(memory_space=pltpu.VMEM), pl.BlockSpec(memory_space=pl.ANY)
    keep, send = call(
        expert_kernel,
        (shape_of((slots, feats), F32), shape_of((slots, feats), BF16)),
        core.reshape(1).astype(jnp.int32),
        own,
        peer,
        w_gate[0],
        w_up[0],
        w_down[0],
        in_specs=[pl.BlockSpec(memory_space=pltpu.SMEM), vmem, vmem, hbm, hbm, hbm],
        scratch=(
            pltpu.VMEM((slots, width), BF16),
            pltpu.VMEM((slots, width), BF16),
            pltpu.VMEM((width, units), BF16),
            pltpu.VMEM((width, units), BF16),
            pltpu.VMEM((units, width), BF16),
            pltpu.VMEM((slots, units), BF16),
            pltpu.VMEM((slots, units), BF16),
            pltpu.SemaphoreType.DMA((3,)),
        ),
        flops=10 * slots * width * units,
        nbytes=20 << 20,
    )
    got = lax.ppermute(send, "tp", swap)
    packed = call(pack_kernel, shape_of((ctx, 80, LANES), BF16), keep, got, flops=1 << 26, nbytes=6 << 20)
    back = exchange(packed)
    gained, dots = call(
        combine_kernel,
        (shape_of((rows, feats), F32), shape_of((rows, 1), F32)),
        back,
        main_table,
        rest_table,
        hidden,
        gain,
        flops=1 << 29,
        nbytes=6 << 20,
    )
    dots = lax.psum(dots, "tp")
    grad_hidden, piece = call(
        lambda h, g, s, a, d, q, t, o, p: hidden_kernel(h, g, s, a, d, q, t, width, o, p),
        (shape_of((rows, feats), BF16), shape_of((ctx, 8, LANES), F32)),
        hidden,
        grad_out,
        squares,
        gained,
        dots,
        queries,
        total,
        flops=1 << 28,
        nbytes=3 << 20,
    )
    incoming = exchange(
        call(backward_kernel, shape_of((ctx, 8, LANES), F32), exchange(piece), pieces, nbytes=1 << 20)
    )
    grad_queries, grad_logits, grad_values = call(
        final_kernel,
        (shape_of((rows, feats), BF16),) * 3,
        queries,
        forget_logits,
        values,
        total,
        grad_hidden,
        starts,
        incoming,
        state,
        flops=1 << 30,
        nbytes=4 << 20,
    )
    return grad_hidden, grad_queries, grad_logits, grad_values


def solution(mesh):
    rows = P("ctx", "tp")
    in_specs = (
        rows,
        rows,
        P("ctx", None),
        P("ctx", None),
        P("tp"),
        P("ctx", None, "tp"),
        P("ctx", None, "tp"),
        P("ctx", "tp", None),
        rows,
        rows,
        rows,
    )
    return jax.shard_map(on_device, mesh=mesh, in_specs=in_specs, out_specs=(rows,) * 4, check_vma=False)
```

profile of v0, /device:TPU:0, one launch (start us, length us, event | category | flops | bytes accessed | tf_op | source)
XLA Modules:
  0.0 192.9 jit_solution(16447677416450917648)
XLA Ops:
  0.6 1.1 multiply_reduce_fusion
  1.7 0.1 copy.15
  1.8 3.6 %psum.14.s = f32[128,1]{1,0:T(8,128)S(1)} all-reduce(f32[128,1]{1,0:T(8,128)S(1)} %copy.15), channel_id=1, replica_groups=mesh['ctx'=64,'tp'=2] {'tp'}, use_global_device_ids=true, to_apply=%region_1.0 | all-reduce | flops 128 | bytes 1024 | tf_op jit(solution)/shard_map/psum | solution.py:381
  5.4 0.8 copy.16.i.ids_ref
  6.2 0.8 copy.17.w
  7.0 0.9 copy-done
  7.9 0.0 copy-start.2
  8.0 0.9 copy-done.2
  8.9 0.7 copy-done.6
  9.6 2.9 %shard_map.138 = bf16[64,160,128]{2,1,0:T(8,128)(2,1)S(1)} custom-call(bf16[128,1024]{1,0:T(8,128)(2,1)S(1)} %copy-done, bf16[128,1024]{1,0:T(8,128)(2,1)S(1)} %copy-done.2, f32[128,1]{1,0:T(8,128)S(1)} %psum.14.s, f32[1,1024]{1,0:T(1,128)S(1)} %bitcast.6, s32[128,4]{1,0:T(8,128)S(1)} %copy.16.i.ids_ref, f32[128,4]{1,0:T(8,128)S(1)} %copy.17.w), custom_call_target="tpu_custom_call" | custom-call | flops 1073741824 | bytes 4194304 | tf_op jit(solution)/shard_map/pallas_call | solution.py:34
  12.5 47.4 %all_to_all.30.own_ref = bf16[64,160,128]{2,1,0:T(8,128)(2,1)S(1)} all-to-all(bf16[64,160,128]{2,1,0:T(8,128)(2,1)S(1)} %shard_map.138), channel_id=1, replica_groups=mesh['ctx'=64,'tp'=2] {'ctx'}, dimensions={0} | all-to-all | bytes 5242880 | tf_op jit(solution)/shard_map/all_to_all | solution.py:378
  59.9 0.0 collective-permute-start
  59.9 5.0 %collective-permute-done.peer_ref = bf16[64,160,128]{2,1,0:T(8,128)(2,1)} collective-permute-done((bf16[64,160,128]{2,1,0:T(8,128)(2,1)S(1)}, bf16[64,160,128]{2,1,0:T(8,128)(2,1)}, u32[]{:S(2)}, u32[]{:S(2)}) %collective-permute-start) | collective-permute-done | bytes 2621472 | tf_op jit(solution)/shard_map/ppermute | solution.py:415
  64.9 0.0 copy-done.13
  64.9 19.1 %shard_map.139 = (f32[640,1024]{1,0:T(8,128)S(1)}, bf16[640,1024]{1,0:T(8,128)(2,1)S(1)}) custom-call(s32[1]{0:T(128)} %bitcast.1.core_ref, bf16[64,160,128]{2,1,0:T(8,128)(2,1)} %copy-done.13, bf16[64,160,128]{2,1,0:T(8,128)(2,1)} %collective-permute-done.peer_ref, bf16[2048,768]{1,0:T(8,128)(2,1)} %bitcast.9, bf16[2048,768]{1,0:T(8,128)(2,1)} %bitcast.10, ...), custom_call_target="tpu_custom_call" | custom-call | flops 10066329600 | bytes 20971520 | tf_op jit(solution)/shard_map/pallas_call | solution.py:34
  84.0 0.2 collective-permute-start.1
  84.3 2.9 %collective-permute-done.1.got_ref = bf16[640,1024]{1,0:T(8,128)(2,1)S(1)} collective-permute-done((bf16[640,1024]{1,0:T(8,128)(2,1)S(1)}, bf16[640,1024]{1,0:T(8,128)(2,1)S(1)}, u32[]{:S(2)}, u32[]{:S(2)}) %collective-permute-start.1) | collective-permute-done | bytes 1310752 | tf_op jit(solution)/shard_map/ppermute | solution.py:440
  87.1 1.7 shard_map.140
  88.8 5.3 %all-to-all-start.1 = ((bf16[64,80,128]{2,1,0:T(8,128)(2,1)}), bf16[64,80,128]{2,1,0:T(8,128)(2,1)S(1)}, u32[]{:S(2)}, u32[]{:S(2)}) async-start(bf16[64,80,128]{2,1,0:T(8,128)(2,1)} %shard_map.140), calls=%async_computation.1 | async-start | bytes 2621440 | tf_op jit(solution)/shard_map/all_to_all | solution.py:378
  94.2 0.0 copy-done.8
  94.2 0.0 copy-done.10
  94.2 0.0 copy-start.1
  94.2 0.0 copy-start.7
  94.2 2.5 %shard_map.143 = (f32[128,1024]{1,0:T(8,128)S(1)}, f32[64,16,128]{2,1,0:T(8,128)}) custom-call(bf16[128,1024]{1,0:T(8,128)(2,1)S(1)} %copy-done.8, bf16[128,1024]{1,0:T(8,128)(2,1)S(1)} %copy-done.10), custom_call_target="tpu_custom_call" | custom-call | flops 1073741824 | bytes 2097152 | tf_op jit(solution)/shard_map/pallas_call | solution.py:34
  96.7 19.2 %all-to-all-done.1.back_ref = bf16[64,80,128]{2,1,0:T(8,128)(2,1)S(1)} async-done(((bf16[64,80,128]{2,1,0:T(8,128)(2,1)}), bf16[64,80,128]{2,1,0:T(8,128)(2,1)S(1)}, u32[]{:S(2)}, u32[]{:S(2)}) %all-to-all-start.1) | async-done | bytes 1310752 | tf_op jit(solution)/shard_map/all_to_all | solution.py:378
  116.0 4.9 %all-to-all-start.2 = ((f32[64,16,128]{2,1,0:T(8,128)}), f32[64,16,128]{2,1,0:T(8,128)S(1)}, u32[]{:S(2)}, u32[]{:S(2)}) async-start(f32[64,16,128]{2,1,0:T(8,128)} %get-tuple-element.25.state_ref), calls=%async_computation.2 | async-start | bytes 1048576 | tf_op jit(solution)/shard_map/all_to_all | solution.py:378
  120.9 0.8 shard_map.141
  121.7 0.0 copy-done.1
  121.7 0.0 copy-done.7
  121.7 1.1 shard_map.142
  122.8 3.6 %psum.15.d = f32[128,1]{1,0:T(8,128)S(1)} all-reduce(f32[128,1]{1,0:T(8,128)S(1)} %get-tuple-element.22), channel_id=1, replica_groups=mesh['ctx'=64,'tp'=2] {'tp'}, use_global_device_ids=true, to_apply=%region_2.0 | all-reduce | flops 128 | bytes 1024 | tf_op jit(solution)/shard_map/psum | solution.py:454
  126.4 0.0 copy-done.3
  126.4 0.0 copy-start.4
  126.4 0.9 copy-done.4
  127.3 1.5 shard_map.144
  128.9 4.3 %all-to-all-done.2.piece_ref.decay_ref = f32[64,16,128]{2,1,0:T(8,128)S(1)} async-done(((f32[64,16,128]{2,1,0:T(8,128)}), f32[64,16,128]{2,1,0:T(8,128)S(1)}, u32[]{:S(2)}, u32[]{:S(2)}) %all-to-all-start.2) | async-done | bytes 524320 | tf_op jit(solution)/shard_map/all_to_all | solution.py:378
  133.1 6.2 %all-to-all-start.4 = ((f32[64,8,128]{2,1,0:T(8,128)}), f32[64,8,128]{2,1,0:T(8,128)S(1)}, u32[]{:S(2)}, u32[]{:S(2)}) async-start(f32[64,8,128]{2,1,0:T(8,128)} %get-tuple-element.26), calls=%async_computation.4 | async-start | bytes 524288 | tf_op jit(solution)/shard_map/all_to_all | solution.py:378
  139.3 0.8 shard_map.145
  140.2 10.1 %all-to-all-done.4.piece_ref = f32[64,8,128]{2,1,0:T(8,128)S(1)} async-done(((f32[64,8,128]{2,1,0:T(8,128)}), f32[64,8,128]{2,1,0:T(8,128)S(1)}, u32[]{:S(2)}, u32[]{:S(2)}) %all-to-all-start.4) | async-done | bytes 262176 | tf_op jit(solution)/shard_map/all_to_all | solution.py:378
  150.3 5.0 %all-to-all-start.3 = ((f32[64,8,128]{2,1,0:T(8,128)}), f32[64,8,128]{2,1,0:T(8,128)S(1)}, u32[]{:S(2)}, u32[]{:S(2)}) async-start(f32[64,8,128]{2,1,0:T(8,128)} %shard_map.145), calls=%async_computation.3 | async-start | bytes 524288 | tf_op jit(solution)/shard_map/all_to_all | solution.py:378
  155.3 0.1 shard_map.146
  155.4 10.3 %all-to-all-done.3.start_ref = f32[64,8,128]{2,1,0:T(8,128)S(1)} async-done(((f32[64,8,128]{2,1,0:T(8,128)}), f32[64,8,128]{2,1,0:T(8,128)S(1)}, u32[]{:S(2)}, u32[]{:S(2)}) %all-to-all-start.3) | async-done | bytes 262176 | tf_op jit(solution)/shard_map/all_to_all | solution.py:378
  165.7 15.2 %all_to_all.31.incoming_ref = f32[64,8,128]{2,1,0:T(8,128)S(1)} all-to-all(f32[64,8,128]{2,1,0:T(8,128)S(1)} %shard_map.146), channel_id=1, replica_groups=mesh['ctx'=64,'tp'=2] {'ctx'}, dimensions={0} | all-to-all | bytes 524288 | tf_op jit(solution)/shard_map/all_to_all | solution.py:378
  180.9 0.0 copy-done.5
  180.9 0.0 copy-done.9
  180.9 0.0 copy-done.11
  180.9 0.0 copy-done.12
  180.9 12.0 %shard_map.147 = (bf16[128,1024]{1,0:T(8,128)(2,1)}, bf16[128,1024]{1,0:T(8,128)(2,1)}, bf16[128,1024]{1,0:T(8,128)(2,1)}) custom-call(bf16[128,1024]{1,0:T(8,128)(2,1)S(1)} %copy-done.5, bf16[128,1024]{1,0:T(8,128)(2,1)S(1)} %copy-done.9, bf16[128,1024]{1,0:T(8,128)(2,1)S(1)} %copy-done.11, f32[128,1024]{1,0:T(8,128)S(1)} %get-tuple-element.23.t.total_ref, ...), custom_call_target="tpu_custom_call" | custom-call | flops 1073741824 | bytes 4194304 | tf_op jit(solution)/shard_map/pallas_call | solution.py:34
  (10 shorter events, 0.0 us)
Async XLA Ops:
  7.0 0.9 copy-start
  7.9 0.9 copy-start.2
  8.9 0.7 copy-start.6
  59.8 5.0 %copy-start.13 = (bf16[64,160,128]{2,1,0:T(8,128)(2,1)}, bf16[64,160,128]{2,1,0:T(8,128)(2,1)S(1)}, u32[]{:S(2)}) copy-start(bf16[64,160,128]{2,1,0:T(8,128)(2,1)S(1)} %all_to_all.30.own_ref) | copy-start | bytes 7864324
  59.9 5.0 %collective-permute-start = (bf16[64,160,128]{2,1,0:T(8,128)(2,1)S(1)}, bf16[64,160,128]{2,1,0:T(8,128)(2,1)}, u32[]{:S(2)}, u32[]{:S(2)}) collective-permute-start(bf16[64,160,128]{2,1,0:T(8,128)(2,1)S(1)} %all_to_all.30.own_ref), channel_id=1, source_target_pairs={{0,1},{1,0},{2,3},{3,2},{4,5},{5,4},{6,7},{7,6},{8,9},{9,8},{10,11... | collective-permute-start | bytes 7864328 | tf_op jit(solution)/shard_map/ppermute | solution.py:415
  84.0 3.1 %collective-permute-start.1 = (bf16[640,1024]{1,0:T(8,128)(2,1)S(1)}, bf16[640,1024]{1,0:T(8,128)(2,1)S(1)}, u32[]{:S(2)}, u32[]{:S(2)}) collective-permute-start(bf16[640,1024]{1,0:T(8,128)(2,1)S(1)} %get-tuple-element.18), channel_id=1, source_target_pairs={{0,1},{1,0},{2,3},{3,2},{4,5},{5,4},{6,7},{7,6},{8,9},{9,8},{10,11... | collective-permute-start | bytes 3932168 | tf_op jit(solution)/shard_map/ppermute | solution.py:440
  88.8 5.3 %copy-start.8 = (bf16[128,1024]{1,0:T(8,128)(2,1)S(1)}, bf16[128,1024]{1,0:T(8,128)(2,1)}, u32[]{:S(2)}) copy-start(bf16[128,1024]{1,0:T(8,128)(2,1)} %logit_ref.3) | copy-start | bytes 786436
  88.8 5.4 %copy-start.10 = (bf16[128,1024]{1,0:T(8,128)(2,1)S(1)}, bf16[128,1024]{1,0:T(8,128)(2,1)}, u32[]{:S(2)}) copy-start(bf16[128,1024]{1,0:T(8,128)(2,1)} %value_ref.3) | copy-start | bytes 786436
  88.8 27.1 %all-to-all-start.1 = ((bf16[64,80,128]{2,1,0:T(8,128)(2,1)}), bf16[64,80,128]{2,1,0:T(8,128)(2,1)S(1)}, u32[]{:S(2)}, u32[]{:S(2)}) async-start(bf16[64,80,128]{2,1,0:T(8,128)(2,1)} %shard_map.140), calls=%async_computation.1 | async-start | bytes 2621440 | tf_op jit(solution)/shard_map/all_to_all | solution.py:378
  94.2 27.5 %copy-start.1 = (bf16[128,1024]{1,0:T(8,128)(2,1)S(1)}, bf16[128,1024]{1,0:T(8,128)(2,1)}, u32[]{:S(2)}) copy-start(bf16[128,1024]{1,0:T(8,128)(2,1)} %h.3) | copy-start | bytes 786436
  94.2 27.5 %copy-start.7 = (f32[1024]{0:T(1024)S(1)}, f32[1024]{0:T(1024)}, u32[]{:S(2)}) copy-start(f32[1024]{0:T(1024)} %param.15) | copy-start | bytes 12292
  116.0 10.4 %copy-start.3 = (bf16[128,1024]{1,0:T(8,128)(2,1)S(1)}, bf16[128,1024]{1,0:T(8,128)(2,1)}, u32[]{:S(2)}) copy-start(bf16[128,1024]{1,0:T(8,128)(2,1)} %g.3) | copy-start | bytes 786436
  116.0 17.2 %all-to-all-start.2 = ((f32[64,16,128]{2,1,0:T(8,128)}), f32[64,16,128]{2,1,0:T(8,128)S(1)}, u32[]{:S(2)}, u32[]{:S(2)}) async-start(f32[64,16,128]{2,1,0:T(8,128)} %get-tuple-element.25.state_ref), calls=%async_computation.2 | async-start | bytes 1048576 | tf_op jit(solution)/shard_map/all_to_all | solution.py:378
  126.4 1.0 copy-start.4
  127.3 53.6 %copy-start.5 = (bf16[128,1024]{1,0:T(8,128)(2,1)S(1)}, bf16[128,1024]{1,0:T(8,128)(2,1)}, u32[]{:S(2)}) copy-start(bf16[128,1024]{1,0:T(8,128)(2,1)} %query_ref.1) | copy-start | bytes 786436
  127.3 53.6 %copy-start.9 = (bf16[128,1024]{1,0:T(8,128)(2,1)S(1)}, bf16[128,1024]{1,0:T(8,128)(2,1)}, u32[]{:S(2)}) copy-start(bf16[128,1024]{1,0:T(8,128)(2,1)} %logit_ref.3) | copy-start | bytes 786436
  127.3 53.6 %copy-start.11 = (bf16[128,1024]{1,0:T(8,128)(2,1)S(1)}, bf16[128,1024]{1,0:T(8,128)(2,1)}, u32[]{:S(2)}) copy-start(bf16[128,1024]{1,0:T(8,128)(2,1)} %value_ref.3) | copy-start | bytes 786436
  128.9 52.1 %copy-start.12 = (bf16[128,1024]{1,0:T(8,128)(2,1)S(1)}, bf16[128,1024]{1,0:T(8,128)(2,1)}, u32[]{:S(2)}) copy-start(bf16[128,1024]{1,0:T(8,128)(2,1)} %get-tuple-element.13.upstream_ref) | copy-start | bytes 786436
  133.1 17.1 %all-to-all-start.4 = ((f32[64,8,128]{2,1,0:T(8,128)}), f32[64,8,128]{2,1,0:T(8,128)S(1)}, u32[]{:S(2)}, u32[]{:S(2)}) async-start(f32[64,8,128]{2,1,0:T(8,128)} %get-tuple-element.26), calls=%async_computation.4 | async-start | bytes 524288 | tf_op jit(solution)/shard_map/all_to_all | solution.py:378
  150.3 15.4 %all-to-all-start.3 = ((f32[64,8,128]{2,1,0:T(8,128)}), f32[64,8,128]{2,1,0:T(8,128)S(1)}, u32[]{:S(2)}, u32[]{:S(2)}) async-start(f32[64,8,128]{2,1,0:T(8,128)} %shard_map.145), calls=%async_computation.3 | async-start | bytes 524288 | tf_op jit(solution)/shard_map/all_to_all | solution.py:378
where the time goes:
time: 194 us; the launch traced here: 193 us
  blocking collectives  69.7 us (36%)
  waiting for transfers between devices  51.8 us (27%)
  Pallas kernels  42.5 us (22%)
  starting transfers between devices  21.7 us (11%)
  local copies, waits for them, and re-layouts  5.26 us (3%)
    all_to_all x2, blocking collectives, exchange(): return lax.all_to_all(array, 'ctx', split_axis=0, concat_axis=0, tiled=True)  62.6 us
    all_to_all x4, waiting for transfers between devices, exchange(): return lax.all_to_all(array, 'ctx', split_axis=0, concat_axis=0, tiled=True)  43.9 us
    pallas_call x10, Pallas kernels, call(): pl.pallas_call(kernel, out_shape=out_shape, in_specs=in_specs or [pl.Bloc...  42.5 us
    all_to_all x4, starting transfers between devices, exchange(): return lax.all_to_all(array, 'ctx', split_axis=0, concat_axis=0, tiled=True)  21.5 us
    unnamed x30, local copies, waits for them, and re-layouts  5.15 us
    ppermute x1, waiting for transfers between devices, on_device(): peer = lax.ppermute(own, 'tp', swap)  5.04 us
  transfers between devices with their start and end apart: 6, of which 6 were waited for; matrix products, arithmetic and copies ran while one was open for 0% of the time, Pallas kernels for 4%

commit v1 on v0

--- a/solution.py
+++ b/solution.py
@@ -46,20 +46,39 @@
     return jax.ShapeDtypeStruct(shape, dtype)
 
 
-def ranked(ids_ref):
-    rows = ids_ref.shape[0]
-    lane = iota((rows, LANES), 1)
-    named = jnp.zeros((rows, LANES), F32)
-    for choice in range(ids_ref.shape[1]):
-        named = named + (ids_ref[:, choice : choice + 1] == lane).astype(F32)
-    before = (iota((rows, rows), 1) < iota((rows, rows), 0)).astype(BF16)
-    rank = fast_dot(before, named.astype(BF16))
+def ranked(ids_ref, count):
+    rows = ids_ref.shape[1]
+    named = named_by(ids_ref, count)
+    before = (iota((rows, rows), 0) < iota((rows, rows), 1)).astype(BF16)
+    rank = fast_dot(named.astype(BF16), before)
     return jnp.where(named > 0.0, rank, -1.0)
 
 
-def dispatch_kernel(hidden_ref, cot_ref, squares_ref, gain_ref, ids_ref, weight_ref, width, out_ref, rhs, rhs_rem):
+def named_by(ids_ref, count, weight_ref=None):
+    expert = iota((count, ids_ref.shape[1]), 0)
+    total = jnp.zeros(expert.shape, F32)
+    for choice in range(ids_ref.shape[0]):
+        level = 1.0 if weight_ref is None else weight_ref[choice : choice + 1, :]
+        total = total + jnp.where(ids_ref[choice : choice + 1, :] == expert, level, 0.0)
+    return total
+
+
+def column(row):
+    count = row.shape[1]
+    eye = iota((count, count), 0) == iota((count, count), 1)
+    return jnp.sum(jnp.where(eye, row, 0.0), axis=1, keepdims=True)
+
+
+def row_scale_of(own_ref, peer_ref, width):
+    return lax.rsqrt(column(own_ref[...] + peer_ref[...]) / width + NORM_EPS)
+
+
+def dispatch_kernel(
+    hidden_ref, cot_ref, own_sq_ref, peer_sq_ref, gain_ref, ids_ref, weight_ref, width, out_ref, rhs, rhs_rem
+):
     rows = hidden_ref.shape[0]
-    row_scale = lax.rsqrt(squares_ref[...] / width + NORM_EPS)
+    count = out_ref.shape[0]
+    row_scale = row_scale_of(own_sq_ref, peer_sq_ref, width)
     normed = (hidden_ref[...].astype(F32) * row_scale * gain_ref[...]).astype(BF16)
     rhs[0:rows, :] = normed
     rhs[rows : 2 * rows, :] = cot_ref[...]
@@ -67,17 +86,10 @@
         lo, col = 2 * rows * (j % 4), LANES * (j // 4)
         rhs_rem[lo : lo + rows, col : col + LANES] = normed[:, j * LANES : (j + 1) * LANES]
         rhs_rem[lo + rows : lo + 2 * rows, col : col + LANES] = cot_ref[:, j * LANES : (j + 1) * LANES]
-    rank = ranked(ids_ref).T
-    lane = iota((rows, LANES), 1)
-    weight = jnp.zeros((rows, LANES), F32)
-    for choice in range(ids_ref.shape[1]):
-        weight = weight + jnp.where(
-            ids_ref[:, choice : choice + 1] == lane, weight_ref[:, choice : choice + 1], 0.0
-        )
-    weight = weight.T
-    rank_b = rank.astype(BF16)
-    for group in range(8):
-        expand = (iota((128, LANES), 0) // 16 + group * 8 == iota((128, LANES), 1)).astype(BF16)
+    rank_b = ranked(ids_ref, count).astype(BF16)
+    weight = named_by(ids_ref, count, weight_ref)
+    for group in range(count // 8):
+        expand = (iota((128, count), 0) // 16 + group * 8 == iota((128, count), 1)).astype(BF16)
         ranks = fast_dot(expand, rank_b)
         weights = exact_dot(expand.astype(F32), weight)
         inner = iota((128, LANES), 0) % 16
@@ -108,10 +120,11 @@
 
 
 def table_kernel(ids_ref, main_ref, rest_ref):
-    rank = ranked(ids_ref).astype(BF16)
-    count = main_ref.shape[1]
-    expand = (iota((LANES, count), 1) // 16 == iota((LANES, count), 0)).astype(BF16)
-    ranks = fast_dot(rank, expand)
+    slots = main_ref.shape[1]
+    count = slots // 16
+    rank = ranked(ids_ref, count).astype(BF16)
+    expand = (iota((count, slots), 1) // 16 == iota((count, slots), 0)).astype(BF16)
+    ranks = fast_dot(rank, expand, TN)
     inner = iota(ranks.shape, 1) % 16
     hit = ranks == (inner % 8).astype(F32)
     rows = ranks.shape[0]
@@ -224,14 +237,24 @@
         value = (value + rest[j * rows : (j + 1) * rows, :]) * gain_ref[:, cols]
         gained_ref[:, cols] = value
         total = total + value * hidden_ref[:, cols].astype(F32)
-    dot_ref[...] = jnp.sum(total, axis=1, keepdims=True)
+    eye = iota((rows, rows), 0) == iota((rows, rows), 1)
+    dot_ref[...] = jnp.sum(jnp.where(eye, jnp.sum(total, axis=1, keepdims=True), 0.0), axis=0, keepdims=True)
 
 
 def log_sigmoid(x):
     return -(jnp.maximum(-x, 0.0) + jnp.log1p(jnp.exp(-jnp.abs(x))))
 
 
-def decay_kernel(logit_ref, value_ref, total_ref, state_ref):
+def two_parts(array):
+    high = array.astype(BF16)
+    return high, (array - high.astype(F32)).astype(BF16)
+
+
+def head_mask():
+    return iota((LANES, LANES), 0) // HEAD_DIM == iota((LANES, LANES), 1) // HEAD_DIM
+
+
+def decay_kernel(logit_ref, value_ref, total_ref, state_ref, parts_ref):
     rows, feats = logit_ref.shape
     logits = logit_ref[...].astype(F32)
     key = jax.nn.sigmoid(-logits)
@@ -241,52 +264,102 @@
     end = running[rows - 1 : rows, :]
     key_end = key * jnp.exp(end - running)
     decay = jnp.exp(end)
-    same = iota((LANES, LANES), 0) // HEAD_DIM == iota((LANES, LANES), 1) // HEAD_DIM
+    same = head_mask()
     pick = iota((HEAD_DIM, LANES), 0) == iota((HEAD_DIM, LANES), 1) % HEAD_DIM
     for pair in range(feats // LANES):
         cols = slice(pair * LANES, (pair + 1) * LANES)
+        eight = slice(pair * 8, (pair + 1) * 8)
         local = exact_dot(key_end[:, cols], value_ref[:, cols].astype(F32), TN)
         local = jnp.where(same, local, 0.0)
-        local = local[:HEAD_DIM] + local[HEAD_DIM:]
-        spread = exact_dot(jnp.where(pick, decay[:, cols], 0.0), same.astype(F32))
-        for part in range(8):
-            state_ref[pair * 8 + part, 0:8, :] = local[part * 8 : (part + 1) * 8, :]
-            state_ref[pair * 8 + part, 8:16, :] = spread[part * 8 : (part + 1) * 8, :]
-
-
-def forward_kernel(piece_ref, out_ref):
+        local = (local[:HEAD_DIM] + local[HEAD_DIM:]).reshape(8, 8, LANES)
+        spread = exact_dot(jnp.where(pick, decay[:, cols], 0.0), same.astype(F32)).reshape(8, 8, LANES)
+        state_ref[eight, 0:8, :] = local
+        state_ref[eight, 8:16, :] = spread
+        rest = spread - spread.astype(BF16).astype(F32)
+        parts_ref[eight] = jnp.concatenate([spread, rest], axis=1).astype(BF16)
+
+
+def chain_kernel(piece_ref, out_ref, decay, both):
     count = piece_ref.shape[0]
-    state = jnp.zeros((8, LANES), F32)
+    decay[...] = piece_ref[:, 16:32, :].astype(F32)
+    both[...] = piece_ref[:, 0:16, :].astype(F32)
+    later = jnp.zeros((8, LANES), F32)
+    earlier = jnp.zeros((8, LANES), F32)
     for block in range(count):
-        out_ref[block] = state
-        state = piece_ref[block, 8:16, :] * state + piece_ref[block, 0:8, :]
-
-
-def backward_kernel(piece_ref, decay_ref, out_ref):
-    count = piece_ref.shape[0]
-    state = jnp.zeros((8, LANES), F32)
-    for block in range(count - 1, -1, -1):
-        out_ref[block] = state
-        state = decay_ref[block, 8:16, :] * state + piece_ref[block]
+        piece = both[block, 8:16, :]
+        both[block, 8:16, :] = earlier
+        earlier = (decay[block, 0:8, :] + decay[block, 8:16, :]) * earlier + piece
+        other = count - 1 - block
+        piece = both[other, 0:8, :]
+        both[other, 0:8, :] = later
+        later = (decay[other, 0:8, :] + decay[other, 8:16, :]) * later + piece
+    out_ref[...] = both[...].astype(BF16)
 
 
 def hidden_kernel(
-    hidden_ref, cot_ref, squares_ref, gained_ref, dot_ref, query_ref, total_ref, width, out_ref, piece_ref
+    hidden_ref,
+    cot_ref,
+    own_sq_ref,
+    peer_sq_ref,
+    gained_ref,
+    own_dot_ref,
+    peer_dot_ref,
+    query_ref,
+    total_ref,
+    state_ref,
+    parts_ref,
+    width,
+    out_ref,
+    piece_ref,
 ):
-    row_scale = lax.rsqrt(squares_ref[...] / width + NORM_EPS)
+    row_scale = row_scale_of(own_sq_ref, peer_sq_ref, width)
+    dot = column(own_dot_ref[...] + peer_dot_ref[...])
     back = row_scale * gained_ref[...] - hidden_ref[...].astype(F32) * (
-        row_scale * row_scale * row_scale * dot_ref[...] / width
+        row_scale * row_scale * row_scale * dot / width
     )
     upstream = (cot_ref[...].astype(F32) + back).astype(BF16)
     out_ref[...] = upstream
     query = query_ref[...].astype(F32) * jnp.exp(total_ref[...])
-    same = iota((LANES, LANES), 0) // HEAD_DIM == iota((LANES, LANES), 1) // HEAD_DIM
+    same = head_mask()
+    piece_ref[:, 16:32, :] = parts_ref[...]
     for pair in range(hidden_ref.shape[1] // LANES):
         cols = slice(pair * LANES, (pair + 1) * LANES)
+        eight = slice(pair * 8, (pair + 1) * 8)
         elem = exact_dot(query[:, cols], upstream[:, cols].astype(F32), TN)
         elem = jnp.where(same, elem, 0.0)
-        elem = elem[:HEAD_DIM] + elem[HEAD_DIM:]
-        piece_ref[pair * 8 : (pair + 1) * 8] = elem.reshape(8, 8, LANES)
+        elem = (elem[:HEAD_DIM] + elem[HEAD_DIM:]).reshape(8, 8, LANES)
+        piece_ref[eight, 0:16, :] = jnp.concatenate([elem, state_ref[eight, 0:8, :]], axis=1).astype(BF16)
+
+
+def block_kernel(query_ref, logit_ref, value_ref, total_ref, upstream_ref, query_out, key_out, value_out):
+    rows, feats = query_ref.shape
+    lower = iota((rows, rows), 0) >= iota((rows, rows), 1)
+    upper = iota((rows, rows), 0) <= iota((rows, rows), 1)
+    first = iota((rows, LANES), 1) < HEAD_DIM
+
+    def split(array):
+        zero = jnp.zeros_like(array)
+        return jnp.where(first, array, zero), jnp.where(first, zero, array)
+
+    for pair in range(feats // LANES):
+        cols = slice(pair * LANES, (pair + 1) * LANES)
+        query = query_ref[:, cols].astype(F32)
+        key = jax.nn.sigmoid(-logit_ref[:, cols].astype(F32))
+        running = total_ref[:, cols]
+        centre = 0.5 * running[rows - 1 : rows, :]
+        grow = jnp.exp(running - centre)
+        shrink = jnp.exp(centre - running)
+        up_split, value_split = split(upstream_ref[:, cols]), split(value_ref[:, cols])
+        query_split, key_split = split(query * grow), split(key * shrink)
+        raw = [fast_dot(u, v, NT) for u, v in zip(up_split, value_split)]
+        pairs = jnp.concatenate([jnp.where(lower, r, 0.0) for r in raw], axis=1)
+        query_out[:, cols] = grow * exact_dot(pairs, jnp.concatenate(key_split, axis=0))
+        raw = [fast_dot(v, u, NT) for u, v in zip(up_split, value_split)]
+        pairs = jnp.concatenate([jnp.where(upper, r, 0.0) for r in raw], axis=1)
+        key_out[:, cols] = shrink * exact_dot(pairs, jnp.concatenate(query_split, axis=0))
+        raw = [exact_dot(k, q, NT) for k, q in zip(key_split, query_split)]
+        pairs = jnp.concatenate([jnp.where(upper, r, 0.0) for r in raw], axis=1)
+        value_out[:, cols] = exact_dot(pairs, jnp.concatenate([u.astype(F32) for u in up_split], axis=0))
 
 
 def final_kernel(
@@ -295,22 +368,18 @@
     value_ref,
     total_ref,
     upstream_ref,
-    start_ref,
-    incoming_ref,
+    query_in,
+    key_in,
+    value_in,
+    carried_ref,
     state_ref,
     query_out,
     logit_out,
     value_out,
 ):
     rows, feats = query_ref.shape
-    lower = iota((rows, rows), 0) >= iota((rows, rows), 1)
-    upper = iota((rows, rows), 0) <= iota((rows, rows), 1)
-    same = iota((LANES, LANES), 0) // HEAD_DIM == iota((LANES, LANES), 1) // HEAD_DIM
-    first = iota((rows, LANES), 1) < HEAD_DIM
-
-    def split(array):
-        zero = jnp.zeros_like(array)
-        return jnp.where(first, array, zero), jnp.where(first, zero, array)
+    upper = (iota((rows, rows), 0) <= iota((rows, rows), 1)).astype(BF16)
+    same = head_mask()
 
     def spread(array):
         return jnp.where(same, jnp.concatenate([array, array], axis=0), 0.0)
@@ -318,44 +387,25 @@
     for pair in range(feats // LANES):
         cols = slice(pair * LANES, (pair + 1) * LANES)
         eight = slice(pair * 8, (pair + 1) * 8)
-        query = query_ref[:, cols].astype(F32)
-        logits = logit_ref[:, cols].astype(F32)
-        key = jax.nn.sigmoid(-logits)
+        key = jax.nn.sigmoid(-logit_ref[:, cols].astype(F32))
         running = total_ref[:, cols]
-        end = running[rows - 1 : rows, :]
-        centre = 0.5 * end
-        grow = jnp.exp(running - centre)
-        shrink = jnp.exp(centre - running)
-        value = value_ref[:, cols]
-        upstream = upstream_ref[:, cols]
-        value_f, upstream_f = value.astype(F32), upstream.astype(F32)
-        start = start_ref[eight].reshape(HEAD_DIM, LANES)
-        incoming = incoming_ref[eight].reshape(HEAD_DIM, LANES)
+        tail = jnp.exp(running[rows - 1 : rows, :] - running)
+        carried = carried_ref[eight].astype(F32)
+        incoming = carried[:, 0:8].reshape(HEAD_DIM, LANES)
+        start = carried[:, 8:16].reshape(HEAD_DIM, LANES)
         local = state_ref[eight, 0:8, :].reshape(HEAD_DIM, LANES)
         decay = state_ref[eight, 8:16, :].reshape(HEAD_DIM, LANES)
-        start_2, incoming_2 = spread(start), spread(incoming)
-        query_s, key_s = query * grow, key * shrink
-        up_split, value_split = split(upstream), split(value)
-        query_split, key_split = split(query_s), split(key_s)
-        raw = [fast_dot(u, v, NT) for u, v in zip(up_split, value_split)]
-        pairs = jnp.concatenate([jnp.where(lower, r, 0.0) for r in raw], axis=1)
-        query_grad = jnp.exp(running) * exact_dot(upstream_f, start_2, NT) + grow * exact_dot(
-            pairs, jnp.concatenate(key_split, axis=0)
-        )
-        raw = [fast_dot(v, u, NT) for u, v in zip(up_split, value_split)]
-        pairs = jnp.concatenate([jnp.where(upper, r, 0.0) for r in raw], axis=1)
-        tail = jnp.exp(end - running)
-        key_grad = tail * exact_dot(value_f, incoming_2, NT) + shrink * exact_dot(
-            pairs, jnp.concatenate(query_split, axis=0)
-        )
-        raw = [exact_dot(k, q, NT) for k, q in zip(key_split, query_split)]
-        pairs = jnp.concatenate([jnp.where(upper, r, 0.0) for r in raw], axis=1)
-        value_grad = exact_dot(
-            pairs, jnp.concatenate([u.astype(F32) for u in up_split], axis=0)
-        ) + exact_dot(key * tail, incoming_2)
+        start_b, incoming_b = spread(start).astype(BF16), spread(incoming).astype(BF16)
+        query_grad = query_in[:, cols] + jnp.exp(running) * fast_dot(upstream_ref[:, cols], start_b, NT)
+        key_grad = key_in[:, cols] + tail * fast_dot(value_ref[:, cols], incoming_b, NT)
+        high, low = two_parts(key * tail)
+        value_grad = value_in[:, cols] + fast_dot(high, incoming_b) + fast_dot(low, incoming_b)
         past = spread((decay * start + local) * incoming)
         past = exact_dot(jnp.ones((8, LANES), F32), past, NT)[0:1, :]
-        suffix = exact_dot(upper.astype(F32), query * query_grad - key * key_grad) + past
+        cumul = query_ref[:, cols].astype(F32) * query_grad - key * key_grad
+        high, rest = two_parts(cumul)
+        middle, low = two_parts(cumul - high.astype(F32))
+        suffix = fast_dot(upper, high) + fast_dot(upper, middle) + fast_dot(upper, low) + past
         logit_grad = suffix * key - key_grad * key * (1.0 - key)
         query_out[:, cols] = query_grad.astype(BF16)
         logit_out[:, cols] = logit_grad.astype(BF16)
@@ -377,18 +427,21 @@
     def exchange(array):
         return lax.all_to_all(array, "ctx", split_axis=0, concat_axis=0, tiled=True)
 
+    ids, weights = expert_ids.T, gate_weights.T
+
     hidden_f = hidden.astype(F32)
-    squares = lax.psum(jnp.sum(hidden_f * hidden_f, axis=1), "tp").reshape(rows, 1)
+    squares = jnp.sum(hidden_f * hidden_f, axis=1)
+    squares = (squares.reshape(1, rows), lax.ppermute(squares, "tp", swap).reshape(1, rows))
 
     sent = call(
-        lambda h, g, s, n, i, w, o, a, b: dispatch_kernel(h, g, s, n, i, w, width, o, a, b),
+        lambda h, g, s, z, n, i, w, o, a, b: dispatch_kernel(h, g, s, z, n, i, w, width, o, a, b),
         shape_of((ctx, 160, LANES), BF16),
         hidden,
         grad_out,
-        squares,
+        *squares,
         gain,
-        expert_ids,
-        gate_weights,
+        ids,
+        weights,
         scratch=(pltpu.VMEM((2 * rows, feats), BF16), pltpu.VMEM((8 * rows, 2 * LANES), BF16)),
         flops=1 << 30,
         nbytes=4 << 20,
@@ -397,20 +450,18 @@
     main_table, rest_table = call(
         table_kernel,
         (shape_of((2 * rows, ctx * 16), BF16), shape_of((8 * rows, ctx * 16), BF16)),
-        expert_ids,
+        ids,
         flops=1 << 26,
         nbytes=3 << 20,
     )
-    total, state = call(
+    total, state, parts = call(
         decay_kernel,
-        (shape_of((rows, feats), F32), shape_of((ctx, 16, LANES), F32)),
+        (shape_of((rows, feats), F32), shape_of((ctx, 16, LANES), F32), shape_of((ctx, 16, LANES), BF16)),
         forget_logits,
         values,
         flops=1 << 30,
         nbytes=2 << 20,
     )
-    pieces = exchange(state)
-    starts = exchange(call(forward_kernel, shape_of((ctx, 8, LANES), F32), pieces, nbytes=1 << 20))
 
     peer = lax.ppermute(own, "tp", swap)
     vmem, hbm = pl.BlockSpec(memory_space=pltpu.VMEM), pl.BlockSpec(memory_space=pl.ANY)
@@ -442,7 +493,7 @@
     back = exchange(packed)
     gained, dots = call(
         combine_kernel,
-        (shape_of((rows, feats), F32), shape_of((rows, 1), F32)),
+        (shape_of((rows, feats), F32), shape_of((1, rows), F32)),
         back,
         main_table,
         rest_table,
@@ -451,23 +502,44 @@
         flops=1 << 29,
         nbytes=6 << 20,
     )
-    dots = lax.psum(dots, "tp")
+    dots = (dots, lax.ppermute(dots, "tp", swap))
     grad_hidden, piece = call(
-        lambda h, g, s, a, d, q, t, o, p: hidden_kernel(h, g, s, a, d, q, t, width, o, p),
-        (shape_of((rows, feats), BF16), shape_of((ctx, 8, LANES), F32)),
+        lambda h, g, s, z, a, d, e, q, t, x, y, o, p: hidden_kernel(
+            h, g, s, z, a, d, e, q, t, x, y, width, o, p
+        ),
+        (shape_of((rows, feats), BF16), shape_of((ctx, 32, LANES), BF16)),
         hidden,
         grad_out,
-        squares,
+        *squares,
         gained,
-        dots,
+        *dots,
         queries,
         total,
+        state,
+        parts,
         flops=1 << 28,
         nbytes=3 << 20,
     )
-    incoming = exchange(
-        call(backward_kernel, shape_of((ctx, 8, LANES), F32), exchange(piece), pieces, nbytes=1 << 20)
-    )
+    pieces = exchange(piece)
+    inner = call(
+        block_kernel,
+        (shape_of((rows, feats), F32),) * 3,
+        queries,
+        forget_logits,
+        values,
+        total,
+        grad_hidden,
+        flops=1 << 32,
+        nbytes=4 << 20,
+    )
+    chained = call(
+        chain_kernel,
+        shape_of((ctx, 16, LANES), BF16),
+        pieces,
+        scratch=(pltpu.VMEM((ctx, 16, LANES), F32), pltpu.VMEM((ctx, 16, LANES), F32)),
+        nbytes=1 << 20,
+    )
+    carried = exchange(chained)
     grad_queries, grad_logits, grad_values = call(
         final_kernel,
         (shape_of((rows, feats), BF16),) * 3,
@@ -476,8 +548,8 @@
         values,
         total,
         grad_hidden,
-        starts,
-        incoming,
+        *inner,
+        carried,
         state,
         flops=1 << 30,
         nbytes=4 << 20,

time: 194 us -> 159 us (0.82)
  waiting for transfers between devices: 51.8 us -> 29 us
  starting transfers between devices: 21.7 us -> 10.9 us
  local copies, waits for them, and re-layouts: 5.26 us -> 11.6 us
  blocking collectives: 69.7 us -> 65.4 us
  Pallas kernels: 42.5 us -> 39.2 us
    all_to_all x4 -> x2, waiting for transfers between devices: 43.9 us -> 19.8 us  [exchange(): return lax.all_to_all(array, 'ctx', split_axis=0, concat_axis=0, tiled=True)]
    all_to_all x4 -> x2, starting transfers between devices: 21.5 us -> 10.3 us  [exchange(): return lax.all_to_all(array, 'ctx', split_axis=0, concat_axis=0, tiled=True)]
    psum x2 -> x0, blocking collectives: 7.17 us -> none  [the longest x1 3.58 us: on_device(): dots = lax.psum(dots, 'tp')]
    unnamed x30 -> x38, local copies, waits for them, and re-layouts: 5.15 us -> 11.6 us
    pallas_call x10, Pallas kernels: 42.5 us -> 39.2 us  [call(): pl.pallas_call(kernel, out_shape=out_shape, in_specs=in_specs or [pl.Bloc...]
    all_to_all x2, blocking collectives: 62.6 us -> 65.4 us  [exchange(): return lax.all_to_all(array, 'ctx', split_axis=0, concat_axis=0, tiled=True)]
  transfers between devices with their start and end apart: 6 -> 6, of which waited for: 6 -> 4; matrix products, arithmetic and copies ran while one was open for 0% -> 0% of each run, Pallas kernels for 4% -> 6%
where the time goes in v1:
time: 159 us; the launch traced here: 158 us
  blocking collectives  65.4 us (41%)
  Pallas kernels  39.2 us (25%)
  waiting for transfers between devices  29 us (18%)
  local copies, waits for them, and re-layouts  11.6 us (7%)
  starting transfers between devices  10.9 us (7%)
    all_to_all x2, blocking collectives, exchange(): return lax.all_to_all(array, 'ctx', split_axis=0, concat_axis=0, tiled=True)  65.4 us
    pallas_call x10, Pallas kernels, call(): pl.pallas_call(kernel, out_shape=out_shape, in_specs=in_specs or [pl.Bloc...  39.2 us
    all_to_all x2, waiting for transfers between devices, exchange(): return lax.all_to_all(array, 'ctx', split_axis=0, concat_axis=0, tiled=True)  19.8 us
    unnamed x38, local copies, waits for them, and re-layouts  11.6 us
    all_to_all x2, starting transfers between devices, exchange(): return lax.all_to_all(array, 'ctx', split_axis=0, concat_axis=0, tiled=True)  10.3 us
    ppermute x1, waiting for transfers between devices, on_device(): peer = lax.ppermute(own, 'tp', swap)  5.25 us
  transfers between devices with their start and end apart: 6, of which 4 were waited for; matrix products, arithmetic and copies ran while one was open for 0% of the time, Pallas kernels for 6%

profile of v1, /device:TPU:0, one launch (start us, length us, event | category | flops | bytes accessed | tf_op | source)
XLA Modules:
  0.0 158.0 jit_solution(16428278567785534096)
XLA Ops:
  0.6 1.1 multiply_reduce_fusion
  1.7 0.1 collective-permute-start
  1.8 1.1 collective-permute-done
  2.9 0.9 copy-done
  3.9 0.9 copy-done.4
  4.8 0.7 copy-done.7
  5.5 0.7 copy-done.12
  6.2 0.7 copy-done.13
  6.9 2.1 %shard_map.138 = bf16[64,160,128]{2,1,0:T(8,128)(2,1)S(1)} custom-call(bf16[128,1024]{1,0:T(8,128)(2,1)S(1)} %copy-done, bf16[128,1024]{1,0:T(8,128)(2,1)S(1)} %copy-done.4, f32[1,128]{1,0:T(1,128)S(1)} %bitcast.11, f32[1,128]{1,0:T(1,128)S(1)} %bitcast.13, f32[1,1024]{1,0:T(1,128)S(1)} %bitcast.9, s32[4,128]{1,0:T(4,128)S(1)} %bitcast.16, f32[4,128]{1,0:T(4,128)S(1)} %bitcast.15), custom_call_target="tpu_custom_call" | custom-call | flops 1073741824 | bytes 4194304 | tf_op jit(solution)/shard_map/pallas_call | solution.py:34
  9.0 47.3 %all_to_all.20.own_ref = bf16[64,160,128]{2,1,0:T(8,128)(2,1)} all-to-all(bf16[64,160,128]{2,1,0:T(8,128)(2,1)S(1)} %shard_map.138), channel_id=1, replica_groups=mesh['ctx'=64,'tp'=2] {'ctx'}, dimensions={0} | all-to-all | bytes 5242880 | tf_op jit(solution)/shard_map/all_to_all | solution.py:428
  56.3 0.0 collective-permute-start.1
  56.3 5.2 %collective-permute-done.1.peer_ref = bf16[64,160,128]{2,1,0:T(8,128)(2,1)} collective-permute-done((bf16[64,160,128]{2,1,0:T(8,128)(2,1)}, bf16[64,160,128]{2,1,0:T(8,128)(2,1)}, u32[]{:S(2)}, u32[]{:S(2)}) %collective-permute-start.1) | collective-permute-done | bytes 2621472 | tf_op jit(solution)/shard_map/ppermute | solution.py:466
  61.6 19.1 %shard_map.139 = (f32[640,1024]{1,0:T(8,128)S(1)}, bf16[640,1024]{1,0:T(8,128)(2,1)S(1)}) custom-call(s32[1]{0:T(128)} %bitcast.2.core_ref, bf16[64,160,128]{2,1,0:T(8,128)(2,1)} %all_to_all.20.own_ref, bf16[64,160,128]{2,1,0:T(8,128)(2,1)} %collective-permute-done.1.peer_ref, bf16[2048,768]{1,0:T(8,128)(2,1)} %bitcast.18, bf16[2048,768]{1,0:T(8,128)(2,1)} %bitcast.19, ...), custom_call_target="tpu_custom_call" | custom-call | flops 10066329600 | bytes 20971520 | tf_op jit(solution)/shard_map/pallas_call | solution.py:34
  80.7 0.2 collective-permute-start.2
  81.0 2.9 %collective-permute-done.2.got_ref = bf16[640,1024]{1,0:T(8,128)(2,1)S(1)} collective-permute-done((bf16[640,1024]{1,0:T(8,128)(2,1)S(1)}, bf16[640,1024]{1,0:T(8,128)(2,1)S(1)}, u32[]{:S(2)}, u32[]{:S(2)}) %collective-permute-start.2) | collective-permute-done | bytes 1310752 | tf_op jit(solution)/shard_map/ppermute | solution.py:491
  83.8 1.7 %shard_map.140 = bf16[64,80,128]{2,1,0:T(8,128)(2,1)} custom-call(f32[640,1024]{1,0:T(8,128)S(1)} %get-tuple-element.21.keep_ref, bf16[640,1024]{1,0:T(8,128)(2,1)S(1)} %collective-permute-done.2.got_ref), custom_call_target="tpu_custom_call" | custom-call | flops 67108864 | bytes 6291456 | tf_op jit(solution)/shard_map/pallas_call | solution.py:34
  85.6 0.0 copy-start.10
  85.6 5.4 %all-to-all-start.1 = ((bf16[64,80,128]{2,1,0:T(8,128)(2,1)}), bf16[64,80,128]{2,1,0:T(8,128)(2,1)S(1)}, u32[]{:S(2)}, u32[]{:S(2)}) async-start(bf16[64,80,128]{2,1,0:T(8,128)(2,1)} %shard_map.140), calls=%async_computation.1 | async-start | bytes 2621440 | tf_op jit(solution)/shard_map/all_to_all | solution.py:428
  91.0 0.0 copy-done.14
  91.0 0.7 shard_map.141
  91.6 0.0 copy-start.2
  91.6 1.3 copy-done.2
  93.0 19.7 %all-to-all-done.1.back_ref = bf16[64,80,128]{2,1,0:T(8,128)(2,1)S(1)} async-done(((bf16[64,80,128]{2,1,0:T(8,128)(2,1)}), bf16[64,80,128]{2,1,0:T(8,128)(2,1)S(1)}, u32[]{:S(2)}, u32[]{:S(2)}) %all-to-all-start.1) | async-done | bytes 1310752 | tf_op jit(solution)/shard_map/all_to_all | solution.py:428
  112.7 0.0 copy-done.1
  112.7 0.0 copy-done.8
  112.7 1.6 %copy-done.3 = bf16[1024,1024]{1,0:T(8,128)(2,1)S(1)} copy-done((bf16[1024,1024]{1,0:T(8,128)(2,1)S(1)}, bf16[1024,1024]{1,0:T(8,128)(2,1)}, u32[]{:S(2)}) %copy-start.3) | copy-done | bytes 2097176
  114.3 1.1 shard_map.142
  115.4 0.0 copy-start.5
  115.4 0.0 copy-start.6
  115.4 0.3 collective-permute-start.3
  115.7 0.0 copy-done.9
  115.7 0.0 copy-done.10
  115.7 1.7 %shard_map.143 = (f32[128,1024]{1,0:T(8,128)S(1)}, f32[64,16,128]{2,1,0:T(8,128)S(1)}, bf16[64,16,128]{2,1,0:T(8,128)(2,1)S(1)}) custom-call(bf16[128,1024]{1,0:T(8,128)(2,1)S(1)} %copy-done.9, bf16[128,1024]{1,0:T(8,128)(2,1)S(1)} %copy-done.10), custom_call_target="tpu_custom_call" | custom-call | flops 1073741824 | bytes 2097152 | tf_op jit(solution)/shard_map/pallas_call | solution.py:34
  117.4 0.0 collective-permute-done.3.e
  117.4 0.0 copy-done.5
  117.5 1.1 shard_map.144
  118.6 18.0 %all_to_all.21.piece_ref = bf16[64,32,128]{2,1,0:T(8,128)(2,1)S(1)} all-to-all(bf16[64,32,128]{2,1,0:T(8,128)(2,1)S(1)} %get-tuple-element.34), channel_id=1, replica_groups=mesh['ctx'=64,'tp'=2] {'ctx'}, dimensions={0} | all-to-all | bytes 1048576 | tf_op jit(solution)/shard_map/all_to_all | solution.py:428
  136.6 0.8 shard_map.146
  137.5 4.9 %all-to-all-start.3 = ((bf16[64,16,128]{2,1,0:T(8,128)(2,1)}), bf16[64,16,128]{2,1,0:T(8,128)(2,1)S(1)}, u32[]{:S(2)}, u32[]{:S(2)}) async-start(bf16[64,16,128]{2,1,0:T(8,128)(2,1)} %shard_map.146), calls=%async_computation.3 | async-start | bytes 524288 | tf_op jit(solution)/shard_map/all_to_all | solution.py:428
  142.4 0.0 copy-start.11
  142.4 0.9 copy-done.11
  143.3 7.8 %shard_map.145 = (f32[128,1024]{1,0:T(8,128)S(1)}, f32[128,1024]{1,0:T(8,128)S(1)}, f32[128,1024]{1,0:T(8,128)S(1)}) custom-call(bf16[128,1024]{1,0:T(8,128)(2,1)S(1)} %copy-done.6, bf16[128,1024]{1,0:T(8,128)(2,1)S(1)} %copy-done.9, bf16[128,1024]{1,0:T(8,128)(2,1)S(1)} %copy-done.10, f32[128,1024]{1,0:T(8,128)S(1)} %get-tuple-element.27.t.total_ref, ...), custom_call_target="tpu_custom_call" | custom-call | flops 4294967296 | bytes 4194304 | tf_op jit(solution)/shard_map/pallas_call | solution.py:34
  151.2 0.8 copy-done.15
  152.0 0.8 copy-done.17
  152.8 0.0 all-to-all-done.3.carried_ref
  152.8 1.0 copy-done.16
  153.9 1.0 copy-done.18
  154.9 3.1 %shard_map.147 = (bf16[128,1024]{1,0:T(8,128)(2,1)}, bf16[128,1024]{1,0:T(8,128)(2,1)}, bf16[128,1024]{1,0:T(8,128)(2,1)}) custom-call(bf16[128,1024]{1,0:T(8,128)(2,1)S(1)} %copy-done.6, bf16[128,1024]{1,0:T(8,128)(2,1)S(1)} %copy-done.9, bf16[128,1024]{1,0:T(8,128)(2,1)S(1)} %copy-done.10, f32[128,1024]{1,0:T(8,128)S(1)} %get-tuple-element.27.t.total_ref, ...), custom_call_target="tpu_custom_call" | custom-call | flops 1073741824 | bytes 4194304 | tf_op jit(solution)/shard_map/pallas_call | solution.py:34
  (15 shorter events, 0.0 us)
Async XLA Ops:
  1.7 1.2 collective-permute-start
  2.9 1.0 copy-start
  3.9 0.9 copy-start.4
  4.8 0.7 copy-start.7
  5.5 0.7 copy-start.12
  6.2 0.7 copy-start.13
  56.3 5.3 %collective-permute-start.1 = (bf16[64,160,128]{2,1,0:T(8,128)(2,1)}, bf16[64,160,128]{2,1,0:T(8,128)(2,1)}, u32[]{:S(2)}, u32[]{:S(2)}) collective-permute-start(bf16[64,160,128]{2,1,0:T(8,128)(2,1)} %all_to_all.20.own_ref), channel_id=1, source_target_pairs={{0,1},{1,0},{2,3},{3,2},{4,5},{5,4},{6,7},{7,6},{8,9},{9,8},{10,11... | collective-permute-start | bytes 7864328 | tf_op jit(solution)/shard_map/ppermute | solution.py:466
  80.7 3.1 %collective-permute-start.2 = (bf16[640,1024]{1,0:T(8,128)(2,1)S(1)}, bf16[640,1024]{1,0:T(8,128)(2,1)S(1)}, u32[]{:S(2)}, u32[]{:S(2)}) collective-permute-start(bf16[640,1024]{1,0:T(8,128)(2,1)S(1)} %get-tuple-element.22), channel_id=1, source_target_pairs={{0,1},{1,0},{2,3},{3,2},{4,5},{5,4},{6,7},{7,6},{8,9},{9,8},{10,11... | collective-permute-start | bytes 3932168 | tf_op jit(solution)/shard_map/ppermute | solution.py:491
  85.5 5.4 %copy-start.14 = (s32[128,4]{0,1:T(4,128)S(1)}, s32[128,4]{0,1:T(4,128)}, u32[]{:S(2)}) copy-start(s32[128,4]{0,1:T(4,128)} %param.13) | copy-start | bytes 6148
  85.6 27.2 %copy-start.1 = (bf16[128,1024]{1,0:T(8,128)(2,1)S(1)}, bf16[128,1024]{1,0:T(8,128)(2,1)}, u32[]{:S(2)}) copy-start(bf16[128,1024]{1,0:T(8,128)(2,1)} %h.3) | copy-start | bytes 786436
  85.6 27.2 %copy-start.8 = (f32[1024]{0:T(1024)S(1)}, f32[1024]{0:T(1024)}, u32[]{:S(2)}) copy-start(f32[1024]{0:T(1024)} %param.15) | copy-start | bytes 12292
  85.6 30.1 %copy-start.9 = (bf16[128,1024]{1,0:T(8,128)(2,1)S(1)}, bf16[128,1024]{1,0:T(8,128)(2,1)}, u32[]{:S(2)}) copy-start(bf16[128,1024]{1,0:T(8,128)(2,1)} %logit_ref.5) | copy-start | bytes 786436
  85.6 30.1 %copy-start.10 = (bf16[128,1024]{1,0:T(8,128)(2,1)S(1)}, bf16[128,1024]{1,0:T(8,128)(2,1)}, u32[]{:S(2)}) copy-start(bf16[128,1024]{1,0:T(8,128)(2,1)} %value_ref.5) | copy-start | bytes 786436
  85.6 27.2 %all-to-all-start.1 = ((bf16[64,80,128]{2,1,0:T(8,128)(2,1)}), bf16[64,80,128]{2,1,0:T(8,128)(2,1)S(1)}, u32[]{:S(2)}, u32[]{:S(2)}) async-start(bf16[64,80,128]{2,1,0:T(8,128)(2,1)} %shard_map.140), calls=%async_computation.1 | async-start | bytes 2621440 | tf_op jit(solution)/shard_map/all_to_all | solution.py:428
  91.6 1.3 copy-start.2
  112.7 1.6 %copy-start.3 = (bf16[1024,1024]{1,0:T(8,128)(2,1)S(1)}, bf16[1024,1024]{1,0:T(8,128)(2,1)}, u32[]{:S(2)}) copy-start(bf16[1024,1024]{1,0:T(8,128)(2,1)} %copy-done.2) | copy-start | bytes 6291460
  115.4 2.0 %copy-start.5 = (bf16[128,1024]{1,0:T(8,128)(2,1)S(1)}, bf16[128,1024]{1,0:T(8,128)(2,1)}, u32[]{:S(2)}) copy-start(bf16[128,1024]{1,0:T(8,128)(2,1)} %g.3) | copy-start | bytes 786436
  115.4 2.0 %copy-start.6 = (bf16[128,1024]{1,0:T(8,128)(2,1)S(1)}, bf16[128,1024]{1,0:T(8,128)(2,1)}, u32[]{:S(2)}) copy-start(bf16[128,1024]{1,0:T(8,128)(2,1)} %query_ref.3) | copy-start | bytes 786436
  115.4 2.0 %collective-permute-start.3 = (f32[1,128]{1,0:T(1,128)S(1)}, f32[1,128]{1,0:T(1,128)S(1)}, u32[]{:S(2)}, u32[]{:S(2)}) collective-permute-start(f32[1,128]{1,0:T(1,128)S(1)} %get-tuple-element.26.d), channel_id=1, source_target_pairs={{0,1},{1,0},{2,3},{3,2},{4,5},{5,4},{6,7},{7,6},{8,9},{9,8},{10,11... | collective-permute-start | bytes 1544 | tf_op jit(solution)/shard_map/ppermute | solution.py:505
  137.5 15.3 %all-to-all-start.3 = ((bf16[64,16,128]{2,1,0:T(8,128)(2,1)}), bf16[64,16,128]{2,1,0:T(8,128)(2,1)S(1)}, u32[]{:S(2)}, u32[]{:S(2)}) async-start(bf16[64,16,128]{2,1,0:T(8,128)(2,1)} %shard_map.146), calls=%async_computation.3 | async-start | bytes 524288 | tf_op jit(solution)/shard_map/all_to_all | solution.py:428
  142.4 1.0 copy-start.11
  151.1 0.8 copy-start.15
  152.0 0.8 copy-start.17
  152.8 1.0 copy-start.16
  153.9 1.0 copy-start.18

commit v2 on v1

--- a/solution.py
+++ b/solution.py
@@ -30,12 +30,12 @@
     return lax.dot_general(a, b, dims, preferred_element_type=F32)
 
 
-def call(kernel, out_shape, *args, scratch=(), in_specs=None, mib=48, flops=0, nbytes=0):
+def call(kernel, out_shape, *args, scratch=(), in_specs=None, out_specs=None, mib=16, flops=0, nbytes=0):
     return pl.pallas_call(
         kernel,
         out_shape=out_shape,
         in_specs=in_specs or [pl.BlockSpec(memory_space=pltpu.VMEM)] * len(args),
-        out_specs=jax.tree.map(lambda _: pl.BlockSpec(memory_space=pltpu.VMEM), out_shape),
+        out_specs=out_specs or jax.tree.map(lambda _: pl.BlockSpec(memory_space=pltpu.VMEM), out_shape),
         scratch_shapes=list(scratch),
         compiler_params=pltpu.CompilerParams(vmem_limit_bytes=mib << 20),
         cost_estimate=pl.CostEstimate(flops=flops, bytes_accessed=nbytes, transcendentals=0),
@@ -131,15 +131,14 @@
     main_ref[0:rows, :] = (hit & (inner < 8)).astype(BF16)
     main_ref[rows : 2 * rows, :] = (hit & (inner >= 8)).astype(BF16)
     hit = ranks == (8 + inner % 2).astype(F32)
-    for j in range(8):
-        rest_ref[j * rows : (j + 1) * rows, :] = (hit & (inner // 2 == j)).astype(BF16)
-
-
-def unpack(raw_ref, x_ref, c_ref, offset):
+    rest_ref[...] = hit.astype(BF16)
+
+
+def unpack(raw_ref, x_ref, c_ref):
     count = raw_ref.shape[0]
     for j in range(8):
         tile = raw_ref[:, j * 16 : (j + 1) * 16, :].astype(F32).reshape(count, 2, 8, LANES)
-        cols = pl.ds(pl.multiple_of(offset + j * LANES, LANES), LANES)
+        cols = slice(j * LANES, (j + 1) * LANES)
         x_ref[0 : count * 8, cols] = tile[:, 0].reshape(count * 8, LANES).astype(BF16)
         c_ref[0 : count * 8, cols] = tile[:, 1].reshape(count * 8, LANES).astype(BF16)
     row = iota((128, 128), 0)
@@ -151,7 +150,7 @@
     )
     rest = fast_dot(perm, rest)
     for j in range(8):
-        cols = pl.ds(pl.multiple_of(offset + j * LANES, LANES), LANES)
+        cols = slice(j * LANES, (j + 1) * LANES)
         for kind, ref in enumerate((x_ref, c_ref)):
             lo = j * 16 + kind * 8
             ref[count * 8 : count * 10, cols] = jnp.concatenate(
@@ -159,39 +158,84 @@
             ).astype(BF16)
 
 
-def expert_kernel(
-    core_ref, own_ref, peer_ref, gate_hbm, up_hbm, down_hbm, keep_ref, send_ref, x, c, gate, up, down, dg, du, sems
-):
-    copies = [
-        pltpu.make_async_copy(source, target, sems.at[number])
-        for number, (source, target) in enumerate(((gate_hbm, gate), (up_hbm, up), (down_hbm, down)))
-    ]
+def start_copies(pairs, sems):
+    copies = [pltpu.make_async_copy(source, target, sems.at[number]) for number, (source, target) in enumerate(pairs)]
     for copy in copies:
         copy.start()
-    core = core_ref[0]
-    half = keep_ref.shape[1]
-    unpack(own_ref, x, c, core * half)
-    unpack(peer_ref, x, c, (1 - core) * half)
-    for copy in copies:
+    return copies
+
+
+def half_of(core, half):
+    return pl.ds(pl.multiple_of(core * half, half), half)
+
+
+def own_kernel(
+    core_ref,
+    raw_ref,
+    gate_hbm,
+    up_hbm,
+    down_hbm,
+    part_0,
+    part_1,
+    part_2,
+    gate,
+    up,
+    peer_gate,
+    peer_up,
+    peer_down,
+    x,
+    c,
+    down,
+    sems,
+    peer_sems,
+):
+    mine = half_of(core_ref[0], x.shape[1])
+    other = half_of(1 - core_ref[0], x.shape[1])
+    copies = start_copies(
+        ((gate_hbm.at[mine, :], gate), (up_hbm.at[mine, :], up), (down_hbm.at[:, mine], down)), sems
+    )
+    later = [
+        pltpu.make_async_copy(source, target, peer_sems.at[number])
+        for number, (source, target) in enumerate(
+            ((gate_hbm.at[other, :], peer_gate), (up_hbm.at[other, :], peer_up), (down_hbm.at[:, other], peer_down))
+        )
+    ]
+    unpack(raw_ref, x, c)
+    copies[0].wait()
+    later[0].start()
+    part_0[...] = fast_dot(x[...], gate[...])
+    copies[1].wait()
+    later[1].start()
+    part_1[...] = fast_dot(x[...], up[...])
+    copies[2].wait()
+    later[2].start()
+    part_2[...] = fast_dot(c[...], down[...], NT)
+    for copy in later:
         copy.wait()
 
-    @pl.loop(0, gate.shape[1] // 256)
-    def _(step):
-        cols = pl.ds(pl.multiple_of(step * 256, 256), 256)
-        pre_gate = fast_dot(x[...], gate[:, cols])
-        pre_up = fast_dot(x[...], up[:, cols])
-        d_act = fast_dot(c[...], down[cols, :], NT)
+
+def peer_kernel(raw_ref, part_0, part_1, part_2, gate, up, down, send_ref, dg, du, x, c):
+    unpack(raw_ref, x, c)
+    for step in range(part_0.shape[1] // 256):
+        cols = slice(step * 256, (step + 1) * 256)
+        pre_gate = part_0[:, cols] + fast_dot(x[...], gate[:, cols])
+        pre_up = part_1[:, cols] + fast_dot(x[...], up[:, cols])
+        d_act = part_2[:, cols] + fast_dot(c[...], down[cols, :], NT)
         sig = jax.nn.sigmoid(pre_gate)
         dg[:, cols] = (d_act * pre_up * sig * (1.0 + pre_gate * (1.0 - sig))).astype(BF16)
         du[:, cols] = (d_act * pre_gate * sig).astype(BF16)
-
-    @pl.loop(0, half // 256)
-    def _(step):
-        cols = pl.ds(pl.multiple_of(step * 256, 256), 256)
-        for ref, first in ((send_ref, (1 - core) * half), (keep_ref, core * half)):
-            feats = pl.ds(pl.multiple_of(first + step * 256, 256), 256)
-            value = fast_dot(dg[...], gate[feats, :], NT) + fast_dot(du[...], up[feats, :], NT)
-            ref[:, cols] = value.astype(ref.dtype)
+    project(dg, du, gate, up, send_ref)
+
+
+def project(dg, du, gate, up, out_ref):
+    for step in range(out_ref.shape[1] // 256):
+        cols = slice(step * 256, (step + 1) * 256)
+        value = fast_dot(dg[...], gate[cols, :], NT) + fast_dot(du[...], up[cols, :], NT)
+        out_ref[:, cols] = value.astype(out_ref.dtype)
+
+
+def keep_kernel(dg, du, gate, up, keep_ref):
+    project(dg, du, gate, up, keep_ref)
 
 
 def pack_kernel(keep_ref, got_ref, out_ref):
@@ -229,7 +273,9 @@
         [back_ref[:, m * 16 : (m + 1) * 16, :].reshape(count * 16, LANES) for m in range(4)], axis=1
     )
     main = fast_dot(main_ref[...], main)
-    rest = fast_dot(rest_ref[...], back_ref[:, 64:80, :].reshape(count * 16, LANES))
+    block = iota((1, count * 16), 1) % 16 // 2
+    left = jnp.concatenate([jnp.where(block == j, rest_ref[...], 0.0) for j in range(8)], axis=0)
+    rest = fast_dot(left.astype(BF16), back_ref[:, 64:80, :].reshape(count * 16, LANES))
     total = jnp.zeros((rows, LANES), F32)
     for j in range(8):
         cols = slice(j * LANES, (j + 1) * LANES)
@@ -443,18 +489,19 @@
         ids,
         weights,
         scratch=(pltpu.VMEM((2 * rows, feats), BF16), pltpu.VMEM((8 * rows, 2 * LANES), BF16)),
-        flops=1 << 30,
-        nbytes=4 << 20,
+        mib=60,
+        flops=1 << 24,
+        nbytes=1 << 12,
     )
     own = exchange(sent)
     main_table, rest_table = call(
         table_kernel,
-        (shape_of((2 * rows, ctx * 16), BF16), shape_of((8 * rows, ctx * 16), BF16)),
+        (shape_of((2 * rows, ctx * 16), BF16), shape_of((rows, ctx * 16), BF16)),
         ids,
         flops=1 << 26,
         nbytes=3 << 20,
     )
-    total, state, parts = call(
+    total, state, decays = call(
         decay_kernel,
         (shape_of((rows, feats), F32), shape_of((ctx, 16, LANES), F32), shape_of((ctx, 16, LANES), BF16)),
         forget_logits,
@@ -464,31 +511,54 @@
     )
 
     peer = lax.ppermute(own, "tp", swap)
-    vmem, hbm = pl.BlockSpec(memory_space=pltpu.VMEM), pl.BlockSpec(memory_space=pl.ANY)
-    keep, send = call(
-        expert_kernel,
-        (shape_of((slots, feats), F32), shape_of((slots, feats), BF16)),
-        core.reshape(1).astype(jnp.int32),
+    vmem = pl.BlockSpec(memory_space=pltpu.VMEM)
+    smem, hbm = pl.BlockSpec(memory_space=pltpu.SMEM), pl.BlockSpec(memory_space=pl.ANY)
+    which = core.reshape(1).astype(jnp.int32)
+    half_in, half_out = shape_of((feats, units), BF16), shape_of((units, feats), BF16)
+    *parts, gate, up, peer_gate, peer_up, peer_down = call(
+        own_kernel,
+        (*(shape_of((slots, units), F32),) * 3, half_in, half_in, half_in, half_in, half_out),
+        which,
         own,
-        peer,
         w_gate[0],
         w_up[0],
         w_down[0],
-        in_specs=[pl.BlockSpec(memory_space=pltpu.SMEM), vmem, vmem, hbm, hbm, hbm],
+        in_specs=[smem, vmem, hbm, hbm, hbm],
         scratch=(
-            pltpu.VMEM((slots, width), BF16),
-            pltpu.VMEM((slots, width), BF16),
-            pltpu.VMEM((width, units), BF16),
-            pltpu.VMEM((width, units), BF16),
-            pltpu.VMEM((units, width), BF16),
-            pltpu.VMEM((slots, units), BF16),
-            pltpu.VMEM((slots, units), BF16),
+            pltpu.VMEM((slots, feats), BF16),
+            pltpu.VMEM((slots, feats), BF16),
+            pltpu.VMEM((units, feats), BF16),
+            pltpu.SemaphoreType.DMA((3,)),
             pltpu.SemaphoreType.DMA((3,)),
         ),
-        flops=10 * slots * width * units,
-        nbytes=20 << 20,
+        mib=40,
+        flops=6 * slots * feats * units,
+        nbytes=13 << 20,
+    )
+    send, dg, du = call(
+        peer_kernel,
+        (shape_of((slots, feats), BF16), shape_of((slots, units), BF16), shape_of((slots, units), BF16)),
+        peer,
+        *parts,
+        peer_gate,
+        peer_up,
+        peer_down,
+        scratch=(pltpu.VMEM((slots, feats), BF16), pltpu.VMEM((slots, feats), BF16)),
+        mib=28,
+        flops=10 * slots * feats * units,
+        nbytes=16 << 20,
     )
     got = lax.ppermute(send, "tp", swap)
+    keep = call(
+        keep_kernel,
+        shape_of((slots, feats), F32),
+        dg,
+        du,
+        gate,
+        up,
+        flops=4 * slots * feats * units,
+        nbytes=8 << 20,
+    )
     packed = call(pack_kernel, shape_of((ctx, 80, LANES), BF16), keep, got, flops=1 << 26, nbytes=6 << 20)
     back = exchange(packed)
     gained, dots = call(
@@ -516,7 +586,7 @@
         queries,
         total,
         state,
-        parts,
+        decays,
         flops=1 << 28,
         nbytes=3 << 20,
     )
@@ -529,6 +599,7 @@
         values,
         total,
         grad_hidden,
+        mib=60,
         flops=1 << 32,
         nbytes=4 << 20,
     )
@@ -551,6 +622,7 @@
         *inner,
         carried,
         state,
+        mib=60,
         flops=1 << 30,
         nbytes=4 << 20,
     )

time: 159 us -> 147 us (0.925)
  local copies, waits for them, and re-layouts: 11.6 us -> 1.28 us
  waiting for transfers between devices: 29 us -> 23.3 us
  Pallas kernels: 39.2 us -> 42.8 us
    unnamed x38 -> x28, local copies, waits for them, and re-layouts: 11.6 us -> 1.28 us
    ppermute x1, waiting for transfers between devices: 5.25 us -> 0.01 us  [on_device(): peer = lax.ppermute(own, 'tp', swap)]
    pallas_call x10 -> x12, Pallas kernels: 39.2 us -> 42.8 us  [call(): pl.pallas_call(kernel, out_shape=out_shape, in_specs=in_specs or [pl.Bloc...]
    ppermute x1, waiting for transfers between devices: 2.89 us -> 0.44 us  [on_device(): got = lax.ppermute(send, 'tp', swap)]
    all_to_all x2, waiting for transfers between devices: 19.8 us -> 21.8 us  [exchange(): return lax.all_to_all(array, 'ctx', split_axis=0, concat_axis=0, tiled=True)]
  transfers between devices with their start and end apart: 6 -> 6, of which waited for: 4 -> 4; matrix products, arithmetic and copies ran while one was open for 0% -> 0% of each run, Pallas kernels for 6% -> 15%
where the time goes in v2:
time: 147 us; the launch traced here: 146 us
  blocking collectives  65.6 us (45%)
  Pallas kernels  42.8 us (29%)
  waiting for transfers between devices  23.3 us (16%)
  starting transfers between devices  11.3 us (8%)
    all_to_all x2, blocking collectives, exchange(): return lax.all_to_all(array, 'ctx', split_axis=0, concat_axis=0, tiled=True)  65.6 us
    pallas_call x12, Pallas kernels, call(): pl.pallas_call(kernel, out_shape=out_shape, in_specs=in_specs or [pl.Bloc...  42.8 us
    all_to_all x2, waiting for transfers between devices, exchange(): return lax.all_to_all(array, 'ctx', split_axis=0, concat_axis=0, tiled=True)  21.8 us
    all_to_all x2, starting transfers between devices, exchange(): return lax.all_to_all(array, 'ctx', split_axis=0, concat_axis=0, tiled=True)  10.5 us
  transfers between devices with their start and end apart: 6, of which 4 were waited for; matrix products, arithmetic and copies ran while one was open for 0% of the time, Pallas kernels for 15%

profile of v2, /device:TPU:0, one launch (start us, length us, event | category | flops | bytes accessed | tf_op | source)
XLA Modules:
  0.0 146.2 jit_solution(8225856381435120541)
XLA Ops:
  0.6 1.1 multiply_reduce_fusion
  1.7 0.1 collective-permute-start
  1.8 1.1 collective-permute-done
  2.9 0.0 copy-done.6
  2.9 0.5 copy-done.8
  3.4 4.7 %shard_map.138 = bf16[64,160,128]{2,1,0:T(8,128)(2,1)} custom-call(bf16[128,1024]{1,0:T(8,128)(2,1)} %h.3, bf16[128,1024]{1,0:T(8,128)(2,1)} %g.3, f32[1,128]{1,0:T(1,128)} %bitcast.11, f32[1,128]{1,0:T(1,128)} %bitcast.13, f32[1,1024]{1,0:T(1,128)} %bitcast.9, s32[4,128]{1,0:T(4,128)} %bitcast.15, f32[4,128]{1,0:T(4,128)} %bitcast.20), custom_call_target="tpu_custom_call" | custom-call | flops 16777216 | bytes 4096 | tf_op jit(solution)/shard_map/pallas_call | solution.py:34
  8.1 47.5 %all_to_all.20.raw_ref = bf16[64,160,128]{2,1,0:T(8,128)(2,1)} all-to-all(bf16[64,160,128]{2,1,0:T(8,128)(2,1)} %shard_map.138), channel_id=1, replica_groups=mesh['ctx'=64,'tp'=2] {'ctx'}, dimensions={0} | all-to-all | bytes 5242880 | tf_op jit(solution)/shard_map/all_to_all | solution.py:474
  55.7 0.0 collective-permute-start.1
  55.7 8.1 %shard_map.139 = (f32[640,768]{1,0:T(8,128)S(1)}, f32[640,768]{1,0:T(8,128)S(1)}, f32[640,768]{1,0:T(8,128)S(1)}, bf16[1024,768]{1,0:T(8,128)(2,1)S(1)}, bf16[10...) custom-call(s32[1]{0:T(128)} %bitcast.5.core_ref, ...), custom_call_target="tpu_custom_call" | custom-call | flops 3019898880 | bytes 13631488 | tf_op jit(solution)/shard_map/pallas_call | solution.py:34
  63.7 0.0 collective-permute-done.1.raw_ref
  63.8 5.9 %shard_map.140 = (bf16[640,1024]{1,0:T(8,128)(2,1)S(1)}, bf16[640,768]{1,0:T(8,128)(2,1)S(1)}, bf16[640,768]{1,0:T(8,128)(2,1)S(1)}) custom-call(bf16[64,160,128]{2,1,0:T(8,128)(2,1)S(1)} %collective-permute-done.1.raw_ref, f32[640,768]{1,0:T(8,128)S(1)} %get-tuple-element.30.part_0, f32[640,768]{1,0:T(8,128)S(1)} %get-tuple-element.31.part_1, ...), custom_call_target="tpu_custom_call" | custom-call | flops 5033164800 | bytes 16777216 | tf_op jit(solution)/shard_map/pallas_call | solution.py:34
  69.6 0.6 collective-permute-start.2
  70.2 2.2 %shard_map.141.keep_ref = f32[640,1024]{1,0:T(8,128)S(1)} custom-call(bf16[640,768]{1,0:T(8,128)(2,1)S(1)} %get-tuple-element.36.dg, bf16[640,768]{1,0:T(8,128)(2,1)S(1)} %get-tuple-element.37.du, bf16[1024,768]{1,0:T(8,128)(2,1)S(1)} %get-tuple-element.38.gate, bf16[1024,768]{1,0:T(8,128)(2,1)S(1)} %get-tuple-element.39.up), custom_call_target="tpu_custom_call" | custom-call | flops 2013265920 | bytes 8388608 | tf_op jit(solution)/shard_map/pallas_call | solution.py:34
  72.4 0.4 collective-permute-done.2.got_ref
  72.9 1.7 %shard_map.142 = bf16[64,80,128]{2,1,0:T(8,128)(2,1)} custom-call(f32[640,1024]{1,0:T(8,128)S(1)} %shard_map.141.keep_ref, bf16[640,1024]{1,0:T(8,128)(2,1)S(1)} %collective-permute-done.2.got_ref), custom_call_target="tpu_custom_call" | custom-call | flops 67108864 | bytes 6291456 | tf_op jit(solution)/shard_map/pallas_call | solution.py:34
  74.6 0.0 copy-start.12
  74.6 5.6 %all-to-all-start.1 = ((bf16[64,80,128]{2,1,0:T(8,128)(2,1)}), bf16[64,80,128]{2,1,0:T(8,128)(2,1)S(1)}, u32[]{:S(2)}, u32[]{:S(2)}) async-start(bf16[64,80,128]{2,1,0:T(8,128)(2,1)} %shard_map.142), calls=%async_computation.1 | async-start | bytes 2621440 | tf_op jit(solution)/shard_map/all_to_all | solution.py:474
  80.2 0.0 copy-done.10
  80.2 0.4 shard_map.143
  80.7 21.3 %all-to-all-done.1.back_ref = bf16[64,80,128]{2,1,0:T(8,128)(2,1)S(1)} async-done(((bf16[64,80,128]{2,1,0:T(8,128)(2,1)}), bf16[64,80,128]{2,1,0:T(8,128)(2,1)S(1)}, u32[]{:S(2)}, u32[]{:S(2)}) %all-to-all-start.1) | async-done | bytes 1310752 | tf_op jit(solution)/shard_map/all_to_all | solution.py:474
  102.0 0.0 copy-done
  102.0 0.0 copy-done.5
  102.0 1.1 shard_map.144
  103.1 0.0 copy-start.1
  103.1 0.0 copy-start.4
  103.1 0.0 copy-start.7
  103.1 0.0 copy-start.9
  103.1 0.1 collective-permute-start.3
  103.2 0.0 copy-done.11
  103.2 0.0 copy-done.12
  103.2 1.7 %shard_map.145 = (f32[128,1024]{1,0:T(8,128)S(1)}, f32[64,16,128]{2,1,0:T(8,128)S(1)}, bf16[64,16,128]{2,1,0:T(8,128)(2,1)S(1)}) custom-call(bf16[128,1024]{1,0:T(8,128)(2,1)S(1)} %copy-done.11, bf16[128,1024]{1,0:T(8,128)(2,1)S(1)} %copy-done.12), custom_call_target="tpu_custom_call" | custom-call | flops 1073741824 | bytes 2097152 | tf_op jit(solution)/shard_map/pallas_call | solution.py:34
  104.9 0.0 copy-start.2
  104.9 0.0 copy-start.3
  104.9 0.0 collective-permute-done.3.e
  105.0 0.0 copy-done.1
  105.0 0.0 copy-done.4
  105.0 0.0 copy-done.7
  105.0 0.0 copy-done.9
  105.0 1.1 shard_map.146
  106.1 18.0 %all_to_all.21.piece_ref = bf16[64,32,128]{2,1,0:T(8,128)(2,1)S(1)} all-to-all(bf16[64,32,128]{2,1,0:T(8,128)(2,1)S(1)} %get-tuple-element.52), channel_id=1, replica_groups=mesh['ctx'=64,'tp'=2] {'ctx'}, dimensions={0} | all-to-all | bytes 1048576 | tf_op jit(solution)/shard_map/all_to_all | solution.py:474
  124.2 0.8 shard_map.148
  125.0 0.0 copy-done.2
  125.0 0.0 copy-done.3
  125.1 4.9 %all-to-all-start.3 = ((bf16[64,16,128]{2,1,0:T(8,128)(2,1)}), bf16[64,16,128]{2,1,0:T(8,128)(2,1)S(1)}, u32[]{:S(2)}, u32[]{:S(2)}) async-start(bf16[64,16,128]{2,1,0:T(8,128)(2,1)} %shard_map.148), calls=%async_computation.3 | async-start | bytes 524288 | tf_op jit(solution)/shard_map/all_to_all | solution.py:474
  130.0 9.9 %shard_map.147 = (f32[128,1024]{1,0:T(8,128)}, f32[128,1024]{1,0:T(8,128)}, f32[128,1024]{1,0:T(8,128)}) custom-call(bf16[128,1024]{1,0:T(8,128)(2,1)} %query_ref.3, bf16[128,1024]{1,0:T(8,128)(2,1)} %logit_ref.5, bf16[128,1024]{1,0:T(8,128)(2,1)} %value_ref.5, f32[128,1024]{1,0:T(8,128)} %copy-done.2, bf16[128,1024]{1,0:T(8,128)(2,1)} %get-tuple-element.26.upstream_ref), custom_call_target="tpu_custom_call" | custom-call | flops 4294967296 | bytes 4194304 | tf_op jit(solution)/shard_map/pallas_call | solution.py:34
  139.9 0.5 all-to-all-done.3.carried_ref
  140.4 0.7 copy-done.13
  141.1 5.1 %shard_map.149 = (bf16[128,1024]{1,0:T(8,128)(2,1)}, bf16[128,1024]{1,0:T(8,128)(2,1)}, bf16[128,1024]{1,0:T(8,128)(2,1)}) custom-call(bf16[128,1024]{1,0:T(8,128)(2,1)} %query_ref.3, bf16[128,1024]{1,0:T(8,128)(2,1)} %logit_ref.5, bf16[128,1024]{1,0:T(8,128)(2,1)} %value_ref.5, f32[128,1024]{1,0:T(8,128)} %copy-done.2, ...), custom_call_target="tpu_custom_call" | custom-call | flops 1073741824 | bytes 4194304 | tf_op jit(solution)/shard_map/pallas_call | solution.py:34
  (7 shorter events, 0.0 us)
Async XLA Ops:
  1.7 1.2 copy-start.6
  1.7 1.2 collective-permute-start
  2.9 0.5 copy-start.8
  55.7 8.1 %collective-permute-start.1 = (bf16[64,160,128]{2,1,0:T(8,128)(2,1)}, bf16[64,160,128]{2,1,0:T(8,128)(2,1)S(1)}, u32[]{:S(2)}, u32[]{:S(2)}) collective-permute-start(bf16[64,160,128]{2,1,0:T(8,128)(2,1)} %all_to_all.20.raw_ref), channel_id=1, source_target_pairs={{0,1},{1,0},{2,3},{3,2},{4,5},{5,4},{6,7},{7,6},{8,9},{9,8},{10,11... | collective-permute-start | bytes 7864328 | tf_op jit(solution)/shard_map/ppermute | solution.py:513
  69.6 3.2 %collective-permute-start.2 = (bf16[640,1024]{1,0:T(8,128)(2,1)S(1)}, bf16[640,1024]{1,0:T(8,128)(2,1)S(1)}, u32[]{:S(2)}, u32[]{:S(2)}) collective-permute-start(bf16[640,1024]{1,0:T(8,128)(2,1)S(1)} %get-tuple-element.40), channel_id=1, source_target_pairs={{0,1},{1,0},{2,3},{3,2},{4,5},{5,4},{6,7},{7,6},{8,9},{9,8},{10,11... | collective-permute-start | bytes 3932168 | tf_op jit(solution)/shard_map/ppermute | solution.py:551
  74.6 5.6 %copy-start.10 = (s32[128,4]{0,1:T(4,128)S(1)}, s32[128,4]{0,1:T(4,128)}, u32[]{:S(2)}) copy-start(s32[128,4]{0,1:T(4,128)} %param.13) | copy-start | bytes 6148
  74.6 27.4 %copy-start = (bf16[128,1024]{1,0:T(8,128)(2,1)S(1)}, bf16[128,1024]{1,0:T(8,128)(2,1)}, u32[]{:S(2)}) copy-start(bf16[128,1024]{1,0:T(8,128)(2,1)} %h.3) | copy-start | bytes 786436
  74.6 27.4 %copy-start.5 = (f32[1024]{0:T(1024)S(1)}, f32[1024]{0:T(1024)}, u32[]{:S(2)}) copy-start(f32[1024]{0:T(1024)} %param.15) | copy-start | bytes 12292
  74.6 28.6 %copy-start.11 = (bf16[128,1024]{1,0:T(8,128)(2,1)S(1)}, bf16[128,1024]{1,0:T(8,128)(2,1)}, u32[]{:S(2)}) copy-start(bf16[128,1024]{1,0:T(8,128)(2,1)} %logit_ref.5) | copy-start | bytes 786436
  74.6 28.6 %copy-start.12 = (bf16[128,1024]{1,0:T(8,128)(2,1)S(1)}, bf16[128,1024]{1,0:T(8,128)(2,1)}, u32[]{:S(2)}) copy-start(bf16[128,1024]{1,0:T(8,128)(2,1)} %value_ref.5) | copy-start | bytes 786436
  74.6 27.4 %all-to-all-start.1 = ((bf16[64,80,128]{2,1,0:T(8,128)(2,1)}), bf16[64,80,128]{2,1,0:T(8,128)(2,1)S(1)}, u32[]{:S(2)}, u32[]{:S(2)}) async-start(bf16[64,80,128]{2,1,0:T(8,128)(2,1)} %shard_map.142), calls=%async_computation.1 | async-start | bytes 2621440 | tf_op jit(solution)/shard_map/all_to_all | solution.py:474
  103.1 1.9 %copy-start.1 = (bf16[128,1024]{1,0:T(8,128)(2,1)S(1)}, bf16[128,1024]{1,0:T(8,128)(2,1)}, u32[]{:S(2)}) copy-start(bf16[128,1024]{1,0:T(8,128)(2,1)} %g.3) | copy-start | bytes 786436
  103.1 1.9 %copy-start.4 = (bf16[128,1024]{1,0:T(8,128)(2,1)S(1)}, bf16[128,1024]{1,0:T(8,128)(2,1)}, u32[]{:S(2)}) copy-start(bf16[128,1024]{1,0:T(8,128)(2,1)} %query_ref.3) | copy-start | bytes 786436
  103.1 1.9 %copy-start.7 = (f32[128]{0:T(128)S(1)}, f32[128]{0:T(128)}, u32[]{:S(2)}) copy-start(f32[128]{0:T(128)} %copy-done.6) | copy-start | bytes 1540
  103.1 1.9 %copy-start.9 = (f32[128]{0:T(128)S(1)}, f32[128]{0:T(128)}, u32[]{:S(2)}) copy-start(f32[128]{0:T(128)} %copy-done.8) | copy-start | bytes 1540
  103.1 1.8 %collective-permute-start.3 = (f32[1,128]{1,0:T(1,128)S(1)}, f32[1,128]{1,0:T(1,128)S(1)}, u32[]{:S(2)}, u32[]{:S(2)}) collective-permute-start(f32[1,128]{1,0:T(1,128)S(1)} %get-tuple-element.44.d), channel_id=1, source_target_pairs={{0,1},{1,0},{2,3},{3,2},{4,5},{5,4},{6,7},{7,6},{8,9},{9,8},{10,11... | collective-permute-start | bytes 1544 | tf_op jit(solution)/shard_map/ppermute | solution.py:575
  104.9 20.1 %copy-start.2 = (f32[128,1024]{1,0:T(8,128)}, f32[128,1024]{1,0:T(8,128)S(1)}, u32[]{:S(2)}) copy-start(f32[128,1024]{1,0:T(8,128)S(1)} %get-tuple-element.45.t.total_ref) | copy-start | bytes 1572868
  104.9 20.1 %copy-start.3 = (f32[64,16,128]{2,1,0:T(8,128)}, f32[64,16,128]{2,1,0:T(8,128)S(1)}, u32[]{:S(2)}) copy-start(f32[64,16,128]{2,1,0:T(8,128)S(1)} %get-tuple-element.46.x.state_ref) | copy-start | bytes 1572868
  125.1 15.3 %all-to-all-start.3 = ((bf16[64,16,128]{2,1,0:T(8,128)(2,1)}), bf16[64,16,128]{2,1,0:T(8,128)(2,1)S(1)}, u32[]{:S(2)}, u32[]{:S(2)}) async-start(bf16[64,16,128]{2,1,0:T(8,128)(2,1)} %shard_map.148), calls=%async_computation.3 | async-start | bytes 524288 | tf_op jit(solution)/shard_map/all_to_all | solution.py:474
  140.4 0.7 copy-start.13

commit v3 on v2

--- a/solution.py
+++ b/solution.py
@@ -74,7 +74,7 @@
 
 
 def dispatch_kernel(
-    hidden_ref, cot_ref, own_sq_ref, peer_sq_ref, gain_ref, ids_ref, weight_ref, width, out_ref, rhs, rhs_rem
+    hidden_ref, cot_ref, own_sq_ref, peer_sq_ref, gain_ref, ids_ref, weight_ref, width, out_hbm, out_ref, rhs, rhs_rem, sems
 ):
     rows = hidden_ref.shape[0]
     count = out_ref.shape[0]
@@ -88,6 +88,7 @@
         rhs_rem[lo + rows : lo + 2 * rows, col : col + LANES] = cot_ref[:, j * LANES : (j + 1) * LANES]
     rank_b = ranked(ids_ref, count).astype(BF16)
     weight = named_by(ids_ref, count, weight_ref)
+    copies = []
     for group in range(count // 8):
         expand = (iota((128, count), 0) // 16 + group * 8 == iota((128, count), 1)).astype(BF16)
         ranks = fast_dot(expand, rank_b)
@@ -117,9 +118,19 @@
             out_ref[group * 8 : group * 8 + 8, 128 + 16 * half : 144 + 16 * half, :] = rest[
                 :, half * LANES : (half + 1) * LANES
             ].reshape(8, 16, LANES)
-
-
-def table_kernel(ids_ref, main_ref, rest_ref):
+        eight = slice(group * 8, group * 8 + 8)
+        copies.append(pltpu.make_async_copy(out_ref.at[eight], out_hbm.at[eight], sems.at[group]))
+        copies[-1].start()
+    for copy in copies:
+        copy.wait()
+
+
+def early_kernel(ids_ref, logit_ref, value_ref, main_ref, rest_ref, total_ref, local_ref, parts_ref):
+    tables(ids_ref, main_ref, rest_ref)
+    decays(logit_ref, value_ref, total_ref, local_ref, parts_ref)
+
+
+def tables(ids_ref, main_ref, rest_ref):
     slots = main_ref.shape[1]
     count = slots // 16
     rank = ranked(ids_ref, count).astype(BF16)
@@ -201,14 +212,13 @@
         )
     ]
     unpack(raw_ref, x, c)
+    for copy in later:
+        copy.start()
     copies[0].wait()
-    later[0].start()
     part_0[...] = fast_dot(x[...], gate[...])
     copies[1].wait()
-    later[1].start()
     part_1[...] = fast_dot(x[...], up[...])
     copies[2].wait()
-    later[2].start()
     part_2[...] = fast_dot(c[...], down[...], NT)
     for copy in later:
         copy.wait()
@@ -300,7 +310,7 @@
     return iota((LANES, LANES), 0) // HEAD_DIM == iota((LANES, LANES), 1) // HEAD_DIM
 
 
-def decay_kernel(logit_ref, value_ref, total_ref, state_ref, parts_ref):
+def decays(logit_ref, value_ref, total_ref, local_ref, parts_ref):
     rows, feats = logit_ref.shape
     logits = logit_ref[...].astype(F32)
     key = jax.nn.sigmoid(-logits)
@@ -319,8 +329,7 @@
         local = jnp.where(same, local, 0.0)
         local = (local[:HEAD_DIM] + local[HEAD_DIM:]).reshape(8, 8, LANES)
         spread = exact_dot(jnp.where(pick, decay[:, cols], 0.0), same.astype(F32)).reshape(8, 8, LANES)
-        state_ref[eight, 0:8, :] = local
-        state_ref[eight, 8:16, :] = spread
+        local_ref[eight] = local
         rest = spread - spread.astype(BF16).astype(F32)
         parts_ref[eight] = jnp.concatenate([spread, rest], axis=1).astype(BF16)
 
@@ -352,7 +361,7 @@
     peer_dot_ref,
     query_ref,
     total_ref,
-    state_ref,
+    local_ref,
     parts_ref,
     width,
     out_ref,
@@ -374,7 +383,7 @@
         elem = exact_dot(query[:, cols], upstream[:, cols].astype(F32), TN)
         elem = jnp.where(same, elem, 0.0)
         elem = (elem[:HEAD_DIM] + elem[HEAD_DIM:]).reshape(8, 8, LANES)
-        piece_ref[eight, 0:16, :] = jnp.concatenate([elem, state_ref[eight, 0:8, :]], axis=1).astype(BF16)
+        piece_ref[eight, 0:16, :] = jnp.concatenate([elem, local_ref[eight]], axis=1).astype(BF16)
 
 
 def block_kernel(query_ref, logit_ref, value_ref, total_ref, upstream_ref, query_out, key_out, value_out):
@@ -405,53 +414,56 @@
         key_out[:, cols] = shrink * exact_dot(pairs, jnp.concatenate(query_split, axis=0))
         raw = [exact_dot(k, q, NT) for k, q in zip(key_split, query_split)]
         pairs = jnp.concatenate([jnp.where(upper, r, 0.0) for r in raw], axis=1)
-        value_out[:, cols] = exact_dot(pairs, jnp.concatenate([u.astype(F32) for u in up_split], axis=0))
+        value = exact_dot(pairs, jnp.concatenate([u.astype(F32) for u in up_split], axis=0))
+        value_out[:, cols] = value.astype(BF16)
 
 
 def final_kernel(
     query_ref,
     logit_ref,
     value_ref,
-    total_ref,
     upstream_ref,
     query_in,
     key_in,
     value_in,
     carried_ref,
-    state_ref,
     query_out,
     logit_out,
     value_out,
 ):
     rows, feats = query_ref.shape
     upper = (iota((rows, rows), 0) <= iota((rows, rows), 1)).astype(BF16)
+    lower = (iota((rows, rows), 0) >= iota((rows, rows), 1)).astype(BF16)
     same = head_mask()
 
     def spread(array):
         return jnp.where(same, jnp.concatenate([array, array], axis=0), 0.0)
+
+    def summed(mask, array):
+        high, rest = two_parts(array)
+        middle, low = two_parts(array - high.astype(F32))
+        return fast_dot(mask, high) + fast_dot(mask, middle) + fast_dot(mask, low)
 
     for pair in range(feats // LANES):
         cols = slice(pair * LANES, (pair + 1) * LANES)
         eight = slice(pair * 8, (pair + 1) * 8)
-        key = jax.nn.sigmoid(-logit_ref[:, cols].astype(F32))
-        running = total_ref[:, cols]
-        tail = jnp.exp(running[rows - 1 : rows, :] - running)
+        logits = logit_ref[:, cols].astype(F32)
+        key = jax.nn.sigmoid(-logits)
+        running = summed(lower, log_sigmoid(logits))
+        end = running[rows - 1 : rows, :]
+        tail = jnp.exp(end - running)
         carried = carried_ref[eight].astype(F32)
         incoming = carried[:, 0:8].reshape(HEAD_DIM, LANES)
         start = carried[:, 8:16].reshape(HEAD_DIM, LANES)
-        local = state_ref[eight, 0:8, :].reshape(HEAD_DIM, LANES)
-        decay = state_ref[eight, 8:16, :].reshape(HEAD_DIM, LANES)
         start_b, incoming_b = spread(start).astype(BF16), spread(incoming).astype(BF16)
         query_grad = query_in[:, cols] + jnp.exp(running) * fast_dot(upstream_ref[:, cols], start_b, NT)
-        key_grad = key_in[:, cols] + tail * fast_dot(value_ref[:, cols], incoming_b, NT)
+        key_back = tail * fast_dot(value_ref[:, cols], incoming_b, NT)
+        key_grad = key_in[:, cols] + key_back
         high, low = two_parts(key * tail)
-        value_grad = value_in[:, cols] + fast_dot(high, incoming_b) + fast_dot(low, incoming_b)
-        past = spread((decay * start + local) * incoming)
-        past = exact_dot(jnp.ones((8, LANES), F32), past, NT)[0:1, :]
-        cumul = query_ref[:, cols].astype(F32) * query_grad - key * key_grad
-        high, rest = two_parts(cumul)
-        middle, low = two_parts(cumul - high.astype(F32))
-        suffix = fast_dot(upper, high) + fast_dot(upper, middle) + fast_dot(upper, low) + past
+        value_grad = value_in[:, cols].astype(F32) + fast_dot(high, incoming_b) + fast_dot(low, incoming_b)
+        past = exact_dot(jnp.ones((8, LANES), F32), spread(start * incoming), NT)[0:1, :]
+        past = jnp.exp(end) * past + jnp.sum(key * key_back, axis=0, keepdims=True)
+        suffix = summed(upper, query_ref[:, cols].astype(F32) * query_grad - key * key_grad) + past
         logit_grad = suffix * key - key_grad * key * (1.0 - key)
         query_out[:, cols] = query_grad.astype(BF16)
         logit_out[:, cols] = logit_grad.astype(BF16)
@@ -474,13 +486,15 @@
         return lax.all_to_all(array, "ctx", split_axis=0, concat_axis=0, tiled=True)
 
     ids, weights = expert_ids.T, gate_weights.T
+    vmem, hbm = pl.BlockSpec(memory_space=pltpu.VMEM), pl.BlockSpec(memory_space=pl.ANY)
+    smem = pl.BlockSpec(memory_space=pltpu.SMEM)
 
     hidden_f = hidden.astype(F32)
     squares = jnp.sum(hidden_f * hidden_f, axis=1)
     squares = (squares.reshape(1, rows), lax.ppermute(squares, "tp", swap).reshape(1, rows))
 
     sent = call(
-        lambda h, g, s, z, n, i, w, o, a, b: dispatch_kernel(h, g, s, z, n, i, w, width, o, a, b),
+        lambda h, g, s, z, n, i, w, o, v, a, b, m: dispatch_kernel(h, g, s, z, n, i, w, width, o, v, a, b, m),
         shape_of((ctx, 160, LANES), BF16),
         hidden,
         grad_out,
@@ -488,31 +502,35 @@
         gain,
         ids,
         weights,
-        scratch=(pltpu.VMEM((2 * rows, feats), BF16), pltpu.VMEM((8 * rows, 2 * LANES), BF16)),
+        out_specs=hbm,
+        scratch=(
+            pltpu.VMEM((ctx, 160, LANES), BF16),
+            pltpu.VMEM((2 * rows, feats), BF16),
+            pltpu.VMEM((8 * rows, 2 * LANES), BF16),
+            pltpu.SemaphoreType.DMA((ctx // 8,)),
+        ),
         mib=60,
         flops=1 << 24,
         nbytes=1 << 12,
     )
     own = exchange(sent)
-    main_table, rest_table = call(
-        table_kernel,
-        (shape_of((2 * rows, ctx * 16), BF16), shape_of((rows, ctx * 16), BF16)),
+    main_table, rest_table, total, local, decay = call(
+        early_kernel,
+        (
+            shape_of((2 * rows, ctx * 16), BF16),
+            shape_of((rows, ctx * 16), BF16),
+            shape_of((rows, feats), F32),
+            shape_of((ctx, 8, LANES), F32),
+            shape_of((ctx, 16, LANES), BF16),
+        ),
         ids,
-        flops=1 << 26,
-        nbytes=3 << 20,
-    )
-    total, state, decays = call(
-        decay_kernel,
-        (shape_of((rows, feats), F32), shape_of((ctx, 16, LANES), F32), shape_of((ctx, 16, LANES), BF16)),
         forget_logits,
         values,
         flops=1 << 30,
-        nbytes=2 << 20,
+        nbytes=4 << 20,
     )
 
     peer = lax.ppermute(own, "tp", swap)
-    vmem = pl.BlockSpec(memory_space=pltpu.VMEM)
-    smem, hbm = pl.BlockSpec(memory_space=pltpu.SMEM), pl.BlockSpec(memory_space=pl.ANY)
     which = core.reshape(1).astype(jnp.int32)
     half_in, half_out = shape_of((feats, units), BF16), shape_of((units, feats), BF16)
     *parts, gate, up, peer_gate, peer_up, peer_down = call(
@@ -585,21 +603,20 @@
         *dots,
         queries,
         total,
-        state,
-        decays,
+        local,
+        decay,
         flops=1 << 28,
         nbytes=3 << 20,
     )
     pieces = exchange(piece)
     inner = call(
         block_kernel,
-        (shape_of((rows, feats), F32),) * 3,
+        (shape_of((rows, feats), F32), shape_of((rows, feats), F32), shape_of((rows, feats), BF16)),
         queries,
         forget_logits,
         values,
         total,
         grad_hidden,
-        mib=60,
         flops=1 << 32,
         nbytes=4 << 20,
     )
@@ -617,12 +634,9 @@
         queries,
         forget_logits,
         values,
-        total,
         grad_hidden,
         *inner,
         carried,
-        state,
-        mib=60,
         flops=1 << 30,
         nbytes=4 << 20,
     )

time: 147 us -> 143 us (0.973)
  Pallas kernels: 42.8 us -> 38.2 us
  local copies, waits for them, and re-layouts: 1.28 us -> 3.85 us
  waiting for transfers between devices: 23.3 us -> 21.7 us
    pallas_call x12 -> x11, Pallas kernels: 42.8 us -> 38.2 us  [call(): pl.pallas_call(kernel, out_shape=out_shape, in_specs=in_specs or [pl.Bloc...]
    all_to_all x2, waiting for transfers between devices: 21.8 us -> 19.1 us  [exchange(): return lax.all_to_all(array, 'ctx', split_axis=0, concat_axis=0, tiled=True)]
    unnamed x28 -> x36, local copies, waits for them, and re-layouts: 1.28 us -> 3.85 us
  transfers between devices with their start and end apart: 6 -> 6, of which waited for: 4 -> 5; matrix products, arithmetic and copies ran while one was open for 0% -> 0% of each run, Pallas kernels for 15% -> 14%
where the time goes in v3:
time: 143 us; the launch traced here: 142 us
  blocking collectives  65.5 us (46%)
  Pallas kernels  38.2 us (27%)
  waiting for transfers between devices  21.7 us (15%)
  starting transfers between devices  11.3 us (8%)
  local copies, waits for them, and re-layouts  3.85 us (3%)
    all_to_all x2, blocking collectives, exchange(): return lax.all_to_all(array, 'ctx', split_axis=0, concat_axis=0, tiled=True)  65.5 us
    pallas_call x11, Pallas kernels, call(): pl.pallas_call(kernel, out_shape=out_shape, in_specs=in_specs or [pl.Bloc...  38.2 us
    all_to_all x2, waiting for transfers between devices, exchange(): return lax.all_to_all(array, 'ctx', split_axis=0, concat_axis=0, tiled=True)  19.1 us
    all_to_all x2, starting transfers between devices, exchange(): return lax.all_to_all(array, 'ctx', split_axis=0, concat_axis=0, tiled=True)  10.5 us
    unnamed x36, local copies, waits for them, and re-layouts  3.85 us
  transfers between devices with their start and end apart: 6, of which 5 were waited for; matrix products, arithmetic and copies ran while one was open for 0% of the time, Pallas kernels for 14%

profile of v3, /device:TPU:0, one launch (start us, length us, event | category | flops | bytes accessed | tf_op | source)
XLA Modules:
  0.0 142.4 jit_solution(8504627635150186468)
XLA Ops:
  0.6 1.1 multiply_reduce_fusion
  1.7 0.1 collective-permute-start
  1.8 1.1 collective-permute-done
  2.9 0.0 copy-done.8
  2.9 0.5 copy-done.11
  3.4 4.0 %shard_map.138 = bf16[64,160,128]{2,1,0:T(8,128)(2,1)} custom-call(bf16[128,1024]{1,0:T(8,128)(2,1)} %h.3, bf16[128,1024]{1,0:T(8,128)(2,1)} %g.3, f32[1,128]{1,0:T(1,128)} %bitcast.11, f32[1,128]{1,0:T(1,128)} %bitcast.15, f32[1,1024]{1,0:T(1,128)} %bitcast.9, s32[4,128]{1,0:T(4,128)} %bitcast.13, f32[4,128]{1,0:T(4,128)} %bitcast.20), custom_call_target="tpu_custom_call" | custom-call | flops 16777216 | bytes 4096 | tf_op jit(solution)/shard_map/pallas_call | solution.py:34
  7.4 47.6 %all_to_all.20.raw_ref = bf16[64,160,128]{2,1,0:T(8,128)(2,1)} all-to-all(bf16[64,160,128]{2,1,0:T(8,128)(2,1)} %shard_map.138), channel_id=1, replica_groups=mesh['ctx'=64,'tp'=2] {'ctx'}, dimensions={0} | all-to-all | bytes 5242880 | tf_op jit(solution)/shard_map/all_to_all | solution.py:486
  55.0 0.0 collective-permute-start.1
  55.0 8.1 %shard_map.139 = (f32[640,768]{1,0:T(8,128)S(1)}, f32[640,768]{1,0:T(8,128)S(1)}, f32[640,768]{1,0:T(8,128)S(1)}, bf16[1024,768]{1,0:T(8,128)(2,1)S(1)}, bf16[10...) custom-call(s32[1]{0:T(128)} %bitcast.5.core_ref, ...), custom_call_target="tpu_custom_call" | custom-call | flops 3019898880 | bytes 13631488 | tf_op jit(solution)/shard_map/pallas_call | solution.py:34
  63.1 0.0 collective-permute-done.1.raw_ref
  63.1 5.9 %shard_map.140 = (bf16[640,1024]{1,0:T(8,128)(2,1)S(1)}, bf16[640,768]{1,0:T(8,128)(2,1)S(1)}, bf16[640,768]{1,0:T(8,128)(2,1)S(1)}) custom-call(bf16[64,160,128]{2,1,0:T(8,128)(2,1)S(1)} %collective-permute-done.1.raw_ref, f32[640,768]{1,0:T(8,128)S(1)} %get-tuple-element.30.part_0, f32[640,768]{1,0:T(8,128)S(1)} %get-tuple-element.31.part_1, ...), custom_call_target="tpu_custom_call" | custom-call | flops 5033164800 | bytes 16777216 | tf_op jit(solution)/shard_map/pallas_call | solution.py:34
  68.9 0.6 collective-permute-start.2
  69.5 2.2 %shard_map.141.keep_ref = f32[640,1024]{1,0:T(8,128)S(1)} custom-call(bf16[640,768]{1,0:T(8,128)(2,1)S(1)} %get-tuple-element.36.dg, bf16[640,768]{1,0:T(8,128)(2,1)S(1)} %get-tuple-element.37.du, bf16[1024,768]{1,0:T(8,128)(2,1)S(1)} %get-tuple-element.38.gate, bf16[1024,768]{1,0:T(8,128)(2,1)S(1)} %get-tuple-element.39.up), custom_call_target="tpu_custom_call" | custom-call | flops 2013265920 | bytes 8388608 | tf_op jit(solution)/shard_map/pallas_call | solution.py:34
  71.8 0.4 collective-permute-done.2.got_ref
  72.2 1.7 %shard_map.142 = bf16[64,80,128]{2,1,0:T(8,128)(2,1)} custom-call(f32[640,1024]{1,0:T(8,128)S(1)} %shard_map.141.keep_ref, bf16[640,1024]{1,0:T(8,128)(2,1)S(1)} %collective-permute-done.2.got_ref), custom_call_target="tpu_custom_call" | custom-call | flops 67108864 | bytes 6291456 | tf_op jit(solution)/shard_map/pallas_call | solution.py:34
  73.9 5.6 %all-to-all-start.1 = ((bf16[64,80,128]{2,1,0:T(8,128)(2,1)}), bf16[64,80,128]{2,1,0:T(8,128)(2,1)S(1)}, u32[]{:S(2)}, u32[]{:S(2)}) async-start(bf16[64,80,128]{2,1,0:T(8,128)(2,1)} %shard_map.142), calls=%async_computation.1 | async-start | bytes 2621440 | tf_op jit(solution)/shard_map/all_to_all | solution.py:486
  79.5 0.0 copy-done.10
  79.5 0.0 copy-start.13
  79.5 0.9 copy-done.13
  80.5 0.9 copy-done.15
  81.4 2.0 %shard_map.143 = (bf16[256,1024]{1,0:T(8,128)(2,1)S(1)}, bf16[128,1024]{1,0:T(8,128)(2,1)S(1)}, f32[128,1024]{1,0:T(8,128)S(1)}, f32[64,8,128]{2,1,0:T(8,128)S(1)}, bf16[64,16,128]{2,1,0:T(8,128)(2,1)S(1)}) custom-call(s32[4,128]{1,0:T(4,128)S(1)} %bitcast.14, bf16[128,1024]{1,0:T(8,128)(2,1)S(1)} %copy-done.13, bf16[128,1024]{1,0:T(8,128)(2,1)S(1)} %copy-done.15), custom_call_target="tpu_custom_call" | custom-call | flops 1073741824 | bytes 4194304 | tf_op jit(solution)/shard_map/pallas_call | solution.py:34
  83.4 0.0 copy-start.3
  83.4 0.7 copy-done.3
  84.1 0.7 copy-done.5
  84.8 16.5 %all-to-all-done.1.back_ref = bf16[64,80,128]{2,1,0:T(8,128)(2,1)S(1)} async-done(((bf16[64,80,128]{2,1,0:T(8,128)(2,1)}), bf16[64,80,128]{2,1,0:T(8,128)(2,1)S(1)}, u32[]{:S(2)}, u32[]{:S(2)}) %all-to-all-start.1) | async-done | bytes 1310752 | tf_op jit(solution)/shard_map/all_to_all | solution.py:486
  101.3 0.0 copy-done
  101.3 0.0 copy-done.7
  101.3 1.1 shard_map.144
  102.4 0.1 collective-permute-start.3
  102.5 1.1 collective-permute-done.3.e
  103.6 0.0 copy-done.1
  103.6 0.0 copy-done.2
  103.6 0.0 copy-done.9
  103.6 0.0 copy-done.12
  103.6 0.0 copy-done.4
  103.6 0.0 copy-done.6
  103.6 0.0 copy-start.14
  103.6 0.0 copy-start.16
  103.6 1.1 shard_map.145
  104.8 17.9 %all_to_all.21.piece_ref = bf16[64,32,128]{2,1,0:T(8,128)(2,1)S(1)} all-to-all(bf16[64,32,128]{2,1,0:T(8,128)(2,1)S(1)} %get-tuple-element.52), channel_id=1, replica_groups=mesh['ctx'=64,'tp'=2] {'ctx'}, dimensions={0} | all-to-all | bytes 1048576 | tf_op jit(solution)/shard_map/all_to_all | solution.py:486
  122.7 0.8 shard_map.147
  123.5 4.9 %all-to-all-start.3 = ((bf16[64,16,128]{2,1,0:T(8,128)(2,1)}), bf16[64,16,128]{2,1,0:T(8,128)(2,1)S(1)}, u32[]{:S(2)}, u32[]{:S(2)}) async-start(bf16[64,16,128]{2,1,0:T(8,128)(2,1)} %shard_map.147), calls=%async_computation.3 | async-start | bytes 524288 | tf_op jit(solution)/shard_map/all_to_all | solution.py:486
  128.4 0.0 copy-done.14
  128.5 0.0 copy-done.16
  128.5 0.0 copy-done.17
  128.5 7.8 %shard_map.146 = (f32[128,1024]{1,0:T(8,128)S(1)}, f32[128,1024]{1,0:T(8,128)S(1)}, bf16[128,1024]{1,0:T(8,128)(2,1)S(1)}) custom-call(bf16[128,1024]{1,0:T(8,128)(2,1)S(1)} %copy-done.2, bf16[128,1024]{1,0:T(8,128)(2,1)S(1)} %copy-done.14, bf16[128,1024]{1,0:T(8,128)(2,1)S(1)} %copy-done.16, f32[128,1024]{1,0:T(8,128)S(1)} %get-tuple-element.45.t.total_ref, ...), custom_call_target="tpu_custom_call" | custom-call | flops 4294967296 | bytes 4194304 | tf_op jit(solution)/shard_map/pallas_call | solution.py:34
  136.3 2.6 %all-to-all-done.3.carried_ref = bf16[64,16,128]{2,1,0:T(8,128)(2,1)S(1)} async-done(((bf16[64,16,128]{2,1,0:T(8,128)(2,1)}), bf16[64,16,128]{2,1,0:T(8,128)(2,1)S(1)}, u32[]{:S(2)}, u32[]{:S(2)}) %all-to-all-start.3) | async-done | bytes 262176 | tf_op jit(solution)/shard_map/all_to_all | solution.py:486
  138.9 3.5 %shard_map.148 = (bf16[128,1024]{1,0:T(8,128)(2,1)}, bf16[128,1024]{1,0:T(8,128)(2,1)}, bf16[128,1024]{1,0:T(8,128)(2,1)}) custom-call(bf16[128,1024]{1,0:T(8,128)(2,1)S(1)} %copy-done.2, bf16[128,1024]{1,0:T(8,128)(2,1)S(1)} %copy-done.14, bf16[128,1024]{1,0:T(8,128)(2,1)S(1)} %copy-done.16, bf16[128,1024]{1,0:T(8,128)(2,1)S(1)} %copy-done.17, ...), custom_call_target="tpu_custom_call" | custom-call | flops 1073741824 | bytes 4194304 | tf_op jit(solution)/shard_map/pallas_call | solution.py:34
  (14 shorter events, 0.0 us)
Async XLA Ops:
  1.7 1.2 copy-start.8
  1.7 1.2 collective-permute-start
  2.9 0.5 copy-start.11
  55.0 8.1 %collective-permute-start.1 = (bf16[64,160,128]{2,1,0:T(8,128)(2,1)}, bf16[64,160,128]{2,1,0:T(8,128)(2,1)S(1)}, u32[]{:S(2)}, u32[]{:S(2)}) collective-permute-start(bf16[64,160,128]{2,1,0:T(8,128)(2,1)} %all_to_all.20.raw_ref), channel_id=1, source_target_pairs={{0,1},{1,0},{2,3},{3,2},{4,5},{5,4},{6,7},{7,6},{8,9},{9,8},{10,11... | collective-permute-start | bytes 7864328 | tf_op jit(solution)/shard_map/ppermute | solution.py:533
  68.9 3.2 %collective-permute-start.2 = (bf16[640,1024]{1,0:T(8,128)(2,1)S(1)}, bf16[640,1024]{1,0:T(8,128)(2,1)S(1)}, u32[]{:S(2)}, u32[]{:S(2)}) collective-permute-start(bf16[640,1024]{1,0:T(8,128)(2,1)S(1)} %get-tuple-element.40), channel_id=1, source_target_pairs={{0,1},{1,0},{2,3},{3,2},{4,5},{5,4},{6,7},{7,6},{8,9},{9,8},{10,11... | collective-permute-start | bytes 3932168 | tf_op jit(solution)/shard_map/ppermute | solution.py:569
  73.9 5.6 %copy-start.10 = (s32[128,4]{0,1:T(4,128)S(1)}, s32[128,4]{0,1:T(4,128)}, u32[]{:S(2)}) copy-start(s32[128,4]{0,1:T(4,128)} %param.13) | copy-start | bytes 6148
  73.9 27.4 %all-to-all-start.1 = ((bf16[64,80,128]{2,1,0:T(8,128)(2,1)}), bf16[64,80,128]{2,1,0:T(8,128)(2,1)S(1)}, u32[]{:S(2)}, u32[]{:S(2)}) async-start(bf16[64,80,128]{2,1,0:T(8,128)(2,1)} %shard_map.142), calls=%async_computation.1 | async-start | bytes 2621440 | tf_op jit(solution)/shard_map/all_to_all | solution.py:486
  79.5 1.0 copy-start.13
  80.5 0.9 copy-start.15
  81.4 19.9 %copy-start = (bf16[128,1024]{1,0:T(8,128)(2,1)S(1)}, bf16[128,1024]{1,0:T(8,128)(2,1)}, u32[]{:S(2)}) copy-start(bf16[128,1024]{1,0:T(8,128)(2,1)} %h.3) | copy-start | bytes 786436
  81.4 19.9 %copy-start.7 = (f32[1024]{0:T(1024)S(1)}, f32[1024]{0:T(1024)}, u32[]{:S(2)}) copy-start(f32[1024]{0:T(1024)} %param.15) | copy-start | bytes 12292
  83.4 0.7 copy-start.3
  84.1 0.7 copy-start.5
  84.8 18.8 %copy-start.1 = (bf16[128,1024]{1,0:T(8,128)(2,1)S(1)}, bf16[128,1024]{1,0:T(8,128)(2,1)}, u32[]{:S(2)}) copy-start(bf16[128,1024]{1,0:T(8,128)(2,1)} %g.3) | copy-start | bytes 786436
  84.8 18.8 %copy-start.2 = (bf16[128,1024]{1,0:T(8,128)(2,1)S(1)}, bf16[128,1024]{1,0:T(8,128)(2,1)}, u32[]{:S(2)}) copy-start(bf16[128,1024]{1,0:T(8,128)(2,1)} %query_ref.3) | copy-start | bytes 786436
  84.8 18.8 %copy-start.9 = (f32[128]{0:T(128)S(1)}, f32[128]{0:T(128)}, u32[]{:S(2)}) copy-start(f32[128]{0:T(128)} %copy-done.8) | copy-start | bytes 1540
  84.8 18.8 %copy-start.12 = (f32[128]{0:T(128)S(1)}, f32[128]{0:T(128)}, u32[]{:S(2)}) copy-start(f32[128]{0:T(128)} %copy-done.11) | copy-start | bytes 1540
  101.3 2.3 %copy-start.4 = (f32[64,8,128]{2,1,0:T(8,128)S(1)}, f32[64,8,128]{2,1,0:T(8,128)}, u32[]{:S(2)}) copy-start(f32[64,8,128]{2,1,0:T(8,128)} %copy-done.3) | copy-start | bytes 786436
  101.3 2.3 %copy-start.6 = (bf16[64,16,128]{2,1,0:T(8,128)(2,1)S(1)}, bf16[64,16,128]{2,1,0:T(8,128)(2,1)}, u32[]{:S(2)}) copy-start(bf16[64,16,128]{2,1,0:T(8,128)(2,1)} %copy-done.5) | copy-start | bytes 786436
  102.4 1.2 collective-permute-start.3
  103.6 24.8 %copy-start.14 = (bf16[128,1024]{1,0:T(8,128)(2,1)S(1)}, bf16[128,1024]{1,0:T(8,128)(2,1)}, u32[]{:S(2)}) copy-start(bf16[128,1024]{1,0:T(8,128)(2,1)} %logit_ref.5) | copy-start | bytes 786436
  103.6 24.8 %copy-start.16 = (bf16[128,1024]{1,0:T(8,128)(2,1)S(1)}, bf16[128,1024]{1,0:T(8,128)(2,1)}, u32[]{:S(2)}) copy-start(bf16[128,1024]{1,0:T(8,128)(2,1)} %value_ref.5) | copy-start | bytes 786436
  104.8 23.7 %copy-start.17 = (bf16[128,1024]{1,0:T(8,128)(2,1)S(1)}, bf16[128,1024]{1,0:T(8,128)(2,1)}, u32[]{:S(2)}) copy-start(bf16[128,1024]{1,0:T(8,128)(2,1)} %get-tuple-element.26.upstream_ref) | copy-start | bytes 786436
  123.5 15.3 %all-to-all-start.3 = ((bf16[64,16,128]{2,1,0:T(8,128)(2,1)}), bf16[64,16,128]{2,1,0:T(8,128)(2,1)S(1)}, u32[]{:S(2)}, u32[]{:S(2)}) async-start(bf16[64,16,128]{2,1,0:T(8,128)(2,1)} %shard_map.147), calls=%async_computation.3 | async-start | bytes 524288 | tf_op jit(solution)/shard_map/all_to_all | solution.py:486

commit v4 on v3

--- a/solution.py
+++ b/solution.py
@@ -74,53 +74,99 @@
 
 
 def dispatch_kernel(
-    hidden_ref, cot_ref, own_sq_ref, peer_sq_ref, gain_ref, ids_ref, weight_ref, width, out_hbm, out_ref, rhs, rhs_rem, sems
+    hidden_hbm,
+    cot_hbm,
+    own_sq_hbm,
+    peer_sq_hbm,
+    gain_hbm,
+    ids_hbm,
+    weight_hbm,
+    width,
+    out_hbm,
+    out_ref,
+    hidden,
+    rhs,
+    rhs_rem,
+    own_sq,
+    peer_sq,
+    gain,
+    ids,
+    weight_in,
+    in_sems,
+    sems,
 ):
-    rows = hidden_ref.shape[0]
+    rows = hidden.shape[0]
     count = out_ref.shape[0]
-    row_scale = row_scale_of(own_sq_ref, peer_sq_ref, width)
-    normed = (hidden_ref[...].astype(F32) * row_scale * gain_ref[...]).astype(BF16)
-    rhs[0:rows, :] = normed
-    rhs[rows : 2 * rows, :] = cot_ref[...]
+    loads = start_copies(
+        (
+            (ids_hbm, ids),
+            (weight_hbm, weight_in),
+            (own_sq_hbm, own_sq),
+            (peer_sq_hbm, peer_sq),
+            (gain_hbm, gain),
+            (hidden_hbm, hidden),
+            (cot_hbm, rhs.at[pl.ds(rows, rows), :]),
+        ),
+        in_sems,
+    )
+    loads[0].wait()
+    rank_b = ranked(ids, count).astype(BF16)
+    loads[1].wait()
+    weight = named_by(ids, count, weight_in)
+    for load in loads[2:]:
+        load.wait()
+    row_scale = row_scale_of(own_sq, peer_sq, width)
+    rhs[0:rows, :] = (hidden[...].astype(F32) * row_scale * gain[...]).astype(BF16)
     for j in range(8):
         lo, col = 2 * rows * (j % 4), LANES * (j // 4)
-        rhs_rem[lo : lo + rows, col : col + LANES] = normed[:, j * LANES : (j + 1) * LANES]
-        rhs_rem[lo + rows : lo + 2 * rows, col : col + LANES] = cot_ref[:, j * LANES : (j + 1) * LANES]
-    rank_b = ranked(ids_ref, count).astype(BF16)
-    weight = named_by(ids_ref, count, weight_ref)
+        rhs_rem[lo : lo + 2 * rows, col : col + LANES] = rhs[:, j * LANES : (j + 1) * LANES]
+    slots = count * 16
+    inner = iota((slots, LANES), 0) % 16
+    main_cot = inner >= 8
+    rest_cot = (inner // 2) % 2 == 1
+    expand = (iota((slots, count), 0) // 16 == iota((slots, count), 1)).astype(BF16)
+    ranks = fast_dot(expand, rank_b)
+    weights = fast_dot(expand, jnp.concatenate(three_parts(weight), axis=1))
+    weights = weights[:, 0:rows] + weights[:, rows : 2 * rows] + weights[:, 2 * rows :]
+
+    def scale_of(hit, is_cot):
+        scale = jnp.sum(jnp.where(hit & is_cot, weights, 0.0), axis=1, keepdims=True)
+        return jnp.where(is_cot[:, :1], scale, 1.0)
+
+    hit = ranks == (inner % 8).astype(F32)
+    hit_b = hit.astype(BF16)
+    left = jnp.concatenate([hit_b * mask.astype(BF16) for mask in (~main_cot, main_cot)], axis=1)
+    scale = scale_of(hit, main_cot)
     copies = []
-    for group in range(count // 8):
-        expand = (iota((128, count), 0) // 16 + group * 8 == iota((128, count), 1)).astype(BF16)
-        ranks = fast_dot(expand, rank_b)
-        weights = exact_dot(expand.astype(F32), weight)
-        inner = iota((128, LANES), 0) % 16
-        hit = ranks == (inner % 8).astype(F32)
-        is_cot = inner >= 8
-        left = jnp.concatenate([hit & ~is_cot, hit & is_cot], axis=1).astype(BF16)
-        scale = jnp.sum(jnp.where(hit & is_cot, weights, 0.0), axis=1, keepdims=True)
-        scale = jnp.where(is_cot[:, :1], scale, 1.0)
-        main = (fast_dot(left, rhs[...]) * scale).astype(BF16)
-        for j in range(8):
-            out_ref[group * 8 : group * 8 + 8, j * 16 : (j + 1) * 16, :] = main[
-                :, j * LANES : (j + 1) * LANES
-            ].reshape(8, 16, LANES)
-        hit = ranks == (8 + inner % 2).astype(F32)
-        is_cot = (inner // 2) % 2 == 1
-        parts = []
-        for j in range(4):
-            here = hit & (inner // 4 == j)
-            parts += [here & ~is_cot, here & is_cot]
-        left = jnp.concatenate(parts, axis=1).astype(BF16)
-        scale = jnp.sum(jnp.where(hit & is_cot, weights, 0.0), axis=1, keepdims=True)
-        scale = jnp.where(is_cot[:, :1], scale, 1.0)
-        rest = (fast_dot(left, rhs_rem[...]) * scale).astype(BF16)
+
+    def send(first, last):
+        span = pl.ds(first, last - first)
+        copies.append(
+            pltpu.make_async_copy(out_ref.at[:, span, :], out_hbm.at[:, span, :], sems.at[len(copies)])
+        )
+        copies[-1].start()
+
+    for pair in range(4):
+        value = (fast_dot(left, rhs[:, pair * 256 : (pair + 1) * 256]) * scale).astype(BF16)
         for half in range(2):
-            out_ref[group * 8 : group * 8 + 8, 128 + 16 * half : 144 + 16 * half, :] = rest[
-                :, half * LANES : (half + 1) * LANES
-            ].reshape(8, 16, LANES)
-        eight = slice(group * 8, group * 8 + 8)
-        copies.append(pltpu.make_async_copy(out_ref.at[eight], out_hbm.at[eight], sems.at[group]))
-        copies[-1].start()
+            first = pair * 32 + half * 16
+            out_ref[:, first : first + 16, :] = value[:, half * LANES : (half + 1) * LANES].reshape(count, 16, LANES)
+        send(pair * 32, pair * 32 + 32)
+    hit = ranks == (8 + inner % 2).astype(F32)
+    hit_b = hit.astype(BF16)
+    left = jnp.concatenate(
+        [
+            hit_b * ((inner // 4 == j) & kind).astype(BF16)
+            for j in range(4)
+            for kind in (~rest_cot, rest_cot)
+        ],
+        axis=1,
+    )
+    value = (fast_dot(left, rhs_rem[...]) * scale_of(hit, rest_cot)).astype(BF16)
+    for half in range(2):
+        first = 128 + half * 16
+        out_ref[:, first : first + 16, :] = value[:, half * LANES : (half + 1) * LANES].reshape(count, 16, LANES)
+    send(128, 160)
     for copy in copies:
         copy.wait()
 
@@ -182,7 +228,7 @@
 
 def own_kernel(
     core_ref,
-    raw_ref,
+    raw_hbm,
     gate_hbm,
     up_hbm,
     down_hbm,
@@ -194,6 +240,7 @@
     peer_gate,
     peer_up,
     peer_down,
+    raw,
     x,
     c,
     down,
@@ -202,23 +249,19 @@
 ):
     mine = half_of(core_ref[0], x.shape[1])
     other = half_of(1 - core_ref[0], x.shape[1])
-    copies = start_copies(
-        ((gate_hbm.at[mine, :], gate), (up_hbm.at[mine, :], up), (down_hbm.at[:, mine], down)), sems
-    )
-    later = [
-        pltpu.make_async_copy(source, target, peer_sems.at[number])
-        for number, (source, target) in enumerate(
-            ((gate_hbm.at[other, :], peer_gate), (up_hbm.at[other, :], peer_up), (down_hbm.at[:, other], peer_down))
-        )
-    ]
-    unpack(raw_ref, x, c)
-    for copy in later:
-        copy.start()
-    copies[0].wait()
+    first = start_copies(((raw_hbm, raw), (gate_hbm.at[mine, :], gate)), sems)
+    first[0].wait()
+    second = start_copies(((up_hbm.at[mine, :], up), (down_hbm.at[:, mine], down)), sems.at[pl.ds(2, 2)])
+    unpack(raw, x, c)
+    first[1].wait()
+    later = start_copies(
+        ((gate_hbm.at[other, :], peer_gate), (up_hbm.at[other, :], peer_up), (down_hbm.at[:, other], peer_down)),
+        peer_sems,
+    )
     part_0[...] = fast_dot(x[...], gate[...])
-    copies[1].wait()
+    second[0].wait()
     part_1[...] = fast_dot(x[...], up[...])
-    copies[2].wait()
+    second[1].wait()
     part_2[...] = fast_dot(c[...], down[...], NT)
     for copy in later:
         copy.wait()
@@ -283,9 +326,9 @@
         [back_ref[:, m * 16 : (m + 1) * 16, :].reshape(count * 16, LANES) for m in range(4)], axis=1
     )
     main = fast_dot(main_ref[...], main)
-    block = iota((1, count * 16), 1) % 16 // 2
-    left = jnp.concatenate([jnp.where(block == j, rest_ref[...], 0.0) for j in range(8)], axis=0)
-    rest = fast_dot(left.astype(BF16), back_ref[:, 64:80, :].reshape(count * 16, LANES))
+    block = iota((rows, count * 16), 1) % 16 // 2
+    left = jnp.concatenate([rest_ref[...] * (block == j).astype(BF16) for j in range(8)], axis=0)
+    rest = fast_dot(left, back_ref[:, 64:80, :].reshape(count * 16, LANES))
     total = jnp.zeros((rows, LANES), F32)
     for j in range(8):
         cols = slice(j * LANES, (j + 1) * LANES)
@@ -304,6 +347,12 @@
 def two_parts(array):
     high = array.astype(BF16)
     return high, (array - high.astype(F32)).astype(BF16)
+
+
+def three_parts(array):
+    high = array.astype(BF16)
+    middle, low = two_parts(array - high.astype(F32))
+    return high, middle, low
 
 
 def head_mask():
@@ -380,7 +429,8 @@
     for pair in range(hidden_ref.shape[1] // LANES):
         cols = slice(pair * LANES, (pair + 1) * LANES)
         eight = slice(pair * 8, (pair + 1) * 8)
-        elem = exact_dot(query[:, cols], upstream[:, cols].astype(F32), TN)
+        high, low = two_parts(query[:, cols])
+        elem = fast_dot(high, upstream[:, cols], TN) + fast_dot(low, upstream[:, cols], TN)
         elem = jnp.where(same, elem, 0.0)
         elem = (elem[:HEAD_DIM] + elem[HEAD_DIM:]).reshape(8, 8, LANES)
         piece_ref[eight, 0:16, :] = jnp.concatenate([elem, local_ref[eight]], axis=1).astype(BF16)
@@ -434,15 +484,15 @@
     rows, feats = query_ref.shape
     upper = (iota((rows, rows), 0) <= iota((rows, rows), 1)).astype(BF16)
     lower = (iota((rows, rows), 0) >= iota((rows, rows), 1)).astype(BF16)
+    ones = jnp.ones((16, LANES), BF16)
     same = head_mask()
 
     def spread(array):
         return jnp.where(same, jnp.concatenate([array, array], axis=0), 0.0)
 
     def summed(mask, array):
-        high, rest = two_parts(array)
-        middle, low = two_parts(array - high.astype(F32))
-        return fast_dot(mask, high) + fast_dot(mask, middle) + fast_dot(mask, low)
+        high, low = two_parts(array)
+        return fast_dot(mask, high) + fast_dot(mask, low)
 
     for pair in range(feats // LANES):
         cols = slice(pair * LANES, (pair + 1) * LANES)
@@ -461,7 +511,8 @@
         key_grad = key_in[:, cols] + key_back
         high, low = two_parts(key * tail)
         value_grad = value_in[:, cols].astype(F32) + fast_dot(high, incoming_b) + fast_dot(low, incoming_b)
-        past = exact_dot(jnp.ones((8, LANES), F32), spread(start * incoming), NT)[0:1, :]
+        high, low = two_parts(spread(start * incoming))
+        past = (fast_dot(ones, high, NT) + fast_dot(ones, low, NT))[0:1, :]
         past = jnp.exp(end) * past + jnp.sum(key * key_back, axis=0, keepdims=True)
         suffix = summed(upper, query_ref[:, cols].astype(F32) * query_grad - key * key_grad) + past
         logit_grad = suffix * key - key_grad * key * (1.0 - key)
@@ -494,7 +545,7 @@
     squares = (squares.reshape(1, rows), lax.ppermute(squares, "tp", swap).reshape(1, rows))
 
     sent = call(
-        lambda h, g, s, z, n, i, w, o, v, a, b, m: dispatch_kernel(h, g, s, z, n, i, w, width, o, v, a, b, m),
+        lambda h, g, s, z, n, i, w, *rest: dispatch_kernel(h, g, s, z, n, i, w, width, *rest),
         shape_of((ctx, 160, LANES), BF16),
         hidden,
         grad_out,
@@ -502,12 +553,20 @@
         gain,
         ids,
         weights,
+        in_specs=[hbm] * 7,
         out_specs=hbm,
         scratch=(
             pltpu.VMEM((ctx, 160, LANES), BF16),
+            pltpu.VMEM((rows, feats), BF16),
             pltpu.VMEM((2 * rows, feats), BF16),
             pltpu.VMEM((8 * rows, 2 * LANES), BF16),
-            pltpu.SemaphoreType.DMA((ctx // 8,)),
+            pltpu.VMEM((1, rows), F32),
+            pltpu.VMEM((1, rows), F32),
+            pltpu.VMEM((1, feats), F32),
+            pltpu.VMEM(ids.shape, jnp.int32),
+            pltpu.VMEM(weights.shape, F32),
+            pltpu.SemaphoreType.DMA((7,)),
+            pltpu.SemaphoreType.DMA((5,)),
         ),
         mib=60,
         flops=1 << 24,
@@ -541,12 +600,13 @@
         w_gate[0],
         w_up[0],
         w_down[0],
-        in_specs=[smem, vmem, hbm, hbm, hbm],
+        in_specs=[smem, hbm, hbm, hbm, hbm],
         scratch=(
+            pltpu.VMEM((ctx, 160, LANES), BF16),
             pltpu.VMEM((slots, feats), BF16),
             pltpu.VMEM((slots, feats), BF16),
             pltpu.VMEM((units, feats), BF16),
-            pltpu.SemaphoreType.DMA((3,)),
+            pltpu.SemaphoreType.DMA((4,)),
             pltpu.SemaphoreType.DMA((3,)),
         ),
         mib=40,

time: 143 us -> 141 us (0.986)
  Pallas kernels: 38.2 us -> 36.6 us
    pallas_call x11, Pallas kernels: 38.2 us -> 36.6 us  [call(): pl.pallas_call(kernel, out_shape=out_shape, in_specs=in_specs or [pl.Bloc...]
  transfers between devices with their start and end apart: 6 -> 6, of which waited for: 5 -> 5; matrix products, arithmetic and copies ran while one was open for 0% -> 0% of each run, Pallas kernels for 14% -> 13%
where the time goes in v4:
time: 141 us
  blocking collectives  65.5 us (46%)
  Pallas kernels  36.6 us (26%)
  waiting for transfers between devices  21.7 us (15%)
  starting transfers between devices  11.3 us (8%)
  local copies, waits for them, and re-layouts  3.85 us (3%)
    all_to_all x2, blocking collectives, exchange(): return lax.all_to_all(array, 'ctx', split_axis=0, concat_axis=0, tiled=True)  65.5 us
    pallas_call x11, Pallas kernels, call(): pl.pallas_call(kernel, out_shape=out_shape, in_specs=in_specs or [pl.Bloc...  36.6 us
    all_to_all x2, waiting for transfers between devices, exchange(): return lax.all_to_all(array, 'ctx', split_axis=0, concat_axis=0, tiled=True)  19.1 us
    all_to_all x2, starting transfers between devices, exchange(): return lax.all_to_all(array, 'ctx', split_axis=0, concat_axis=0, tiled=True)  10.5 us
    unnamed x36, local copies, waits for them, and re-layouts  3.85 us
  transfers between devices with their start and end apart: 6, of which 5 were waited for; matrix products, arithmetic and copies ran while one was open for 0% of the time, Pallas kernels for 13%

profile of v4, /device:TPU:0, one launch (start us, length us, event | category | flops | bytes accessed | tf_op | source)
XLA Modules:
  0.0 140.8 jit_solution(15206758447230652446)
XLA Ops:
  0.6 1.1 multiply_reduce_fusion
  1.7 0.1 collective-permute-start
  1.8 1.1 collective-permute-done
  2.9 0.0 copy-done.8
  2.9 0.5 copy-done.11
  3.4 4.0 %shard_map.138 = bf16[64,160,128]{2,1,0:T(8,128)(2,1)} custom-call(bf16[128,1024]{1,0:T(8,128)(2,1)} %h.3, bf16[128,1024]{1,0:T(8,128)(2,1)} %g.3, f32[1,128]{1,0:T(1,128)} %bitcast.11, f32[1,128]{1,0:T(1,128)} %bitcast.15, f32[1,1024]{1,0:T(1,128)} %bitcast.9, s32[4,128]{1,0:T(4,128)} %bitcast.13, f32[4,128]{1,0:T(4,128)} %bitcast.20), custom_call_target="tpu_custom_call" | custom-call | flops 16777216 | bytes 4096 | tf_op jit(solution)/shard_map/pallas_call | solution.py:34
  7.4 47.6 %all_to_all.20.raw_hbm = bf16[64,160,128]{2,1,0:T(8,128)(2,1)} all-to-all(bf16[64,160,128]{2,1,0:T(8,128)(2,1)} %shard_map.138), channel_id=1, replica_groups=mesh['ctx'=64,'tp'=2] {'ctx'}, dimensions={0} | all-to-all | bytes 5242880 | tf_op jit(solution)/shard_map/all_to_all | solution.py:537
  55.0 0.0 collective-permute-start.1
  55.0 6.9 %shard_map.139 = (f32[640,768]{1,0:T(8,128)S(1)}, f32[640,768]{1,0:T(8,128)S(1)}, f32[640,768]{1,0:T(8,128)S(1)}, bf16[1024,768]{1,0:T(8,128)(2,1)S(1)}, bf16[10...) custom-call(s32[1]{0:T(128)} %bitcast.5.core_ref, ...), custom_call_target="tpu_custom_call" | custom-call | flops 3019898880 | bytes 13631488 | tf_op jit(solution)/shard_map/pallas_call | solution.py:34
  61.9 0.0 collective-permute-done.1.raw_ref
  61.9 5.9 %shard_map.140 = (bf16[640,1024]{1,0:T(8,128)(2,1)S(1)}, bf16[640,768]{1,0:T(8,128)(2,1)S(1)}, bf16[640,768]{1,0:T(8,128)(2,1)S(1)}) custom-call(bf16[64,160,128]{2,1,0:T(8,128)(2,1)S(1)} %collective-permute-done.1.raw_ref, f32[640,768]{1,0:T(8,128)S(1)} %get-tuple-element.30.part_0, f32[640,768]{1,0:T(8,128)S(1)} %get-tuple-element.31.part_1, ...), custom_call_target="tpu_custom_call" | custom-call | flops 5033164800 | bytes 16777216 | tf_op jit(solution)/shard_map/pallas_call | solution.py:34
  67.8 0.6 collective-permute-start.2
  68.4 2.2 %shard_map.141.keep_ref = f32[640,1024]{1,0:T(8,128)S(1)} custom-call(bf16[640,768]{1,0:T(8,128)(2,1)S(1)} %get-tuple-element.36.dg, bf16[640,768]{1,0:T(8,128)(2,1)S(1)} %get-tuple-element.37.du, bf16[1024,768]{1,0:T(8,128)(2,1)S(1)} %get-tuple-element.38.gate, bf16[1024,768]{1,0:T(8,128)(2,1)S(1)} %get-tuple-element.39.up), custom_call_target="tpu_custom_call" | custom-call | flops 2013265920 | bytes 8388608 | tf_op jit(solution)/shard_map/pallas_call | solution.py:34
  70.6 0.4 collective-permute-done.2.got_ref
  71.1 1.7 %shard_map.142 = bf16[64,80,128]{2,1,0:T(8,128)(2,1)} custom-call(f32[640,1024]{1,0:T(8,128)S(1)} %shard_map.141.keep_ref, bf16[640,1024]{1,0:T(8,128)(2,1)S(1)} %collective-permute-done.2.got_ref), custom_call_target="tpu_custom_call" | custom-call | flops 67108864 | bytes 6291456 | tf_op jit(solution)/shard_map/pallas_call | solution.py:34
  72.8 5.6 %all-to-all-start.1 = ((bf16[64,80,128]{2,1,0:T(8,128)(2,1)}), bf16[64,80,128]{2,1,0:T(8,128)(2,1)S(1)}, u32[]{:S(2)}, u32[]{:S(2)}) async-start(bf16[64,80,128]{2,1,0:T(8,128)(2,1)} %shard_map.142), calls=%async_computation.1 | async-start | bytes 2621440 | tf_op jit(solution)/shard_map/all_to_all | solution.py:537
  78.4 0.0 copy-done.10
  78.4 0.0 copy-start.13
  78.4 0.9 copy-done.13
  79.4 0.9 copy-done.15
  80.3 2.0 %shard_map.143 = (bf16[256,1024]{1,0:T(8,128)(2,1)S(1)}, bf16[128,1024]{1,0:T(8,128)(2,1)S(1)}, f32[128,1024]{1,0:T(8,128)S(1)}, f32[64,8,128]{2,1,0:T(8,128)S(1)}, bf16[64,16,128]{2,1,0:T(8,128)(2,1)S(1)}) custom-call(s32[4,128]{1,0:T(4,128)S(1)} %bitcast.14, bf16[128,1024]{1,0:T(8,128)(2,1)S(1)} %copy-done.13, bf16[128,1024]{1,0:T(8,128)(2,1)S(1)} %copy-done.15), custom_call_target="tpu_custom_call" | custom-call | flops 1073741824 | bytes 4194304 | tf_op jit(solution)/shard_map/pallas_call | solution.py:34
  82.3 0.0 copy-start.3
  82.3 0.7 copy-done.3
  83.0 0.7 copy-done.5
  83.7 16.5 %all-to-all-done.1.back_ref = bf16[64,80,128]{2,1,0:T(8,128)(2,1)S(1)} async-done(((bf16[64,80,128]{2,1,0:T(8,128)(2,1)}), bf16[64,80,128]{2,1,0:T(8,128)(2,1)S(1)}, u32[]{:S(2)}, u32[]{:S(2)}) %all-to-all-start.1) | async-done | bytes 1310752 | tf_op jit(solution)/shard_map/all_to_all | solution.py:537
  100.2 0.0 copy-done
  100.2 0.0 copy-done.7
  100.2 1.1 shard_map.144
  101.3 0.1 collective-permute-start.3
  101.3 1.1 collective-permute-done.3.e
  102.5 0.0 copy-done.1
  102.5 0.0 copy-done.2
  102.5 0.0 copy-done.9
  102.5 0.0 copy-done.12
  102.5 0.0 copy-done.4
  102.5 0.0 copy-done.6
  102.5 0.0 copy-start.14
  102.5 0.0 copy-start.16
  102.5 1.1 shard_map.145
  103.6 17.9 %all_to_all.21.piece_ref = bf16[64,32,128]{2,1,0:T(8,128)(2,1)S(1)} all-to-all(bf16[64,32,128]{2,1,0:T(8,128)(2,1)S(1)} %get-tuple-element.52), channel_id=1, replica_groups=mesh['ctx'=64,'tp'=2] {'ctx'}, dimensions={0} | all-to-all | bytes 1048576 | tf_op jit(solution)/shard_map/all_to_all | solution.py:537
  121.5 0.8 shard_map.147
  122.3 4.9 %all-to-all-start.3 = ((bf16[64,16,128]{2,1,0:T(8,128)(2,1)}), bf16[64,16,128]{2,1,0:T(8,128)(2,1)S(1)}, u32[]{:S(2)}, u32[]{:S(2)}) async-start(bf16[64,16,128]{2,1,0:T(8,128)(2,1)} %shard_map.147), calls=%async_computation.3 | async-start | bytes 524288 | tf_op jit(solution)/shard_map/all_to_all | solution.py:537
  127.3 0.0 copy-done.14
  127.3 0.0 copy-done.16
  127.3 0.0 copy-done.17
  127.3 7.8 %shard_map.146 = (f32[128,1024]{1,0:T(8,128)S(1)}, f32[128,1024]{1,0:T(8,128)S(1)}, bf16[128,1024]{1,0:T(8,128)(2,1)S(1)}) custom-call(bf16[128,1024]{1,0:T(8,128)(2,1)S(1)} %copy-done.2, bf16[128,1024]{1,0:T(8,128)(2,1)S(1)} %copy-done.14, bf16[128,1024]{1,0:T(8,128)(2,1)S(1)} %copy-done.16, f32[128,1024]{1,0:T(8,128)S(1)} %get-tuple-element.45.t.total_ref, ...), custom_call_target="tpu_custom_call" | custom-call | flops 4294967296 | bytes 4194304 | tf_op jit(solution)/shard_map/pallas_call | solution.py:34
  135.1 2.6 %all-to-all-done.3.carried_ref = bf16[64,16,128]{2,1,0:T(8,128)(2,1)S(1)} async-done(((bf16[64,16,128]{2,1,0:T(8,128)(2,1)}), bf16[64,16,128]{2,1,0:T(8,128)(2,1)S(1)}, u32[]{:S(2)}, u32[]{:S(2)}) %all-to-all-start.3) | async-done | bytes 262176 | tf_op jit(solution)/shard_map/all_to_all | solution.py:537
  137.7 3.1 %shard_map.148 = (bf16[128,1024]{1,0:T(8,128)(2,1)}, bf16[128,1024]{1,0:T(8,128)(2,1)}, bf16[128,1024]{1,0:T(8,128)(2,1)}) custom-call(bf16[128,1024]{1,0:T(8,128)(2,1)S(1)} %copy-done.2, bf16[128,1024]{1,0:T(8,128)(2,1)S(1)} %copy-done.14, bf16[128,1024]{1,0:T(8,128)(2,1)S(1)} %copy-done.16, bf16[128,1024]{1,0:T(8,128)(2,1)S(1)} %copy-done.17, ...), custom_call_target="tpu_custom_call" | custom-call | flops 1073741824 | bytes 4194304 | tf_op jit(solution)/shard_map/pallas_call | solution.py:34
  (14 shorter events, 0.0 us)
Async XLA Ops:
  1.7 1.2 copy-start.8
  1.7 1.2 collective-permute-start
  2.9 0.5 copy-start.11
  55.0 7.0 %collective-permute-start.1 = (bf16[64,160,128]{2,1,0:T(8,128)(2,1)}, bf16[64,160,128]{2,1,0:T(8,128)(2,1)S(1)}, u32[]{:S(2)}, u32[]{:S(2)}) collective-permute-start(bf16[64,160,128]{2,1,0:T(8,128)(2,1)} %all_to_all.20.raw_hbm), channel_id=1, source_target_pairs={{0,1},{1,0},{2,3},{3,2},{4,5},{5,4},{6,7},{7,6},{8,9},{9,8},{10,11... | collective-permute-start | bytes 7864328 | tf_op jit(solution)/shard_map/ppermute | solution.py:592
  67.8 3.3 %collective-permute-start.2 = (bf16[640,1024]{1,0:T(8,128)(2,1)S(1)}, bf16[640,1024]{1,0:T(8,128)(2,1)S(1)}, u32[]{:S(2)}, u32[]{:S(2)}) collective-permute-start(bf16[640,1024]{1,0:T(8,128)(2,1)S(1)} %get-tuple-element.40), channel_id=1, source_target_pairs={{0,1},{1,0},{2,3},{3,2},{4,5},{5,4},{6,7},{7,6},{8,9},{9,8},{10,11... | collective-permute-start | bytes 3932168 | tf_op jit(solution)/shard_map/ppermute | solution.py:629
  72.8 5.6 %copy-start.10 = (s32[128,4]{0,1:T(4,128)S(1)}, s32[128,4]{0,1:T(4,128)}, u32[]{:S(2)}) copy-start(s32[128,4]{0,1:T(4,128)} %param.13) | copy-start | bytes 6148
  72.8 27.4 %all-to-all-start.1 = ((bf16[64,80,128]{2,1,0:T(8,128)(2,1)}), bf16[64,80,128]{2,1,0:T(8,128)(2,1)S(1)}, u32[]{:S(2)}, u32[]{:S(2)}) async-start(bf16[64,80,128]{2,1,0:T(8,128)(2,1)} %shard_map.142), calls=%async_computation.1 | async-start | bytes 2621440 | tf_op jit(solution)/shard_map/all_to_all | solution.py:537
  78.4 1.0 copy-start.13
  79.4 0.9 copy-start.15
  80.3 19.9 %copy-start = (bf16[128,1024]{1,0:T(8,128)(2,1)S(1)}, bf16[128,1024]{1,0:T(8,128)(2,1)}, u32[]{:S(2)}) copy-start(bf16[128,1024]{1,0:T(8,128)(2,1)} %h.3) | copy-start | bytes 786436
  80.3 19.9 %copy-start.7 = (f32[1024]{0:T(1024)S(1)}, f32[1024]{0:T(1024)}, u32[]{:S(2)}) copy-start(f32[1024]{0:T(1024)} %param.15) | copy-start | bytes 12292
  82.3 0.7 copy-start.3
  83.0 0.7 copy-start.5
  83.7 18.8 %copy-start.1 = (bf16[128,1024]{1,0:T(8,128)(2,1)S(1)}, bf16[128,1024]{1,0:T(8,128)(2,1)}, u32[]{:S(2)}) copy-start(bf16[128,1024]{1,0:T(8,128)(2,1)} %g.3) | copy-start | bytes 786436
  83.7 18.8 %copy-start.2 = (bf16[128,1024]{1,0:T(8,128)(2,1)S(1)}, bf16[128,1024]{1,0:T(8,128)(2,1)}, u32[]{:S(2)}) copy-start(bf16[128,1024]{1,0:T(8,128)(2,1)} %query_ref.3) | copy-start | bytes 786436
  83.7 18.8 %copy-start.9 = (f32[128]{0:T(128)S(1)}, f32[128]{0:T(128)}, u32[]{:S(2)}) copy-start(f32[128]{0:T(128)} %copy-done.8) | copy-start | bytes 1540
  83.7 18.8 %copy-start.12 = (f32[128]{0:T(128)S(1)}, f32[128]{0:T(128)}, u32[]{:S(2)}) copy-start(f32[128]{0:T(128)} %copy-done.11) | copy-start | bytes 1540
  100.2 2.3 %copy-start.4 = (f32[64,8,128]{2,1,0:T(8,128)S(1)}, f32[64,8,128]{2,1,0:T(8,128)}, u32[]{:S(2)}) copy-start(f32[64,8,128]{2,1,0:T(8,128)} %copy-done.3) | copy-start | bytes 786436
  100.2 2.3 %copy-start.6 = (bf16[64,16,128]{2,1,0:T(8,128)(2,1)S(1)}, bf16[64,16,128]{2,1,0:T(8,128)(2,1)}, u32[]{:S(2)}) copy-start(bf16[64,16,128]{2,1,0:T(8,128)(2,1)} %copy-done.5) | copy-start | bytes 786436
  101.3 1.2 collective-permute-start.3
  102.5 24.8 %copy-start.14 = (bf16[128,1024]{1,0:T(8,128)(2,1)S(1)}, bf16[128,1024]{1,0:T(8,128)(2,1)}, u32[]{:S(2)}) copy-start(bf16[128,1024]{1,0:T(8,128)(2,1)} %logit_ref.5) | copy-start | bytes 786436
  102.5 24.8 %copy-start.16 = (bf16[128,1024]{1,0:T(8,128)(2,1)S(1)}, bf16[128,1024]{1,0:T(8,128)(2,1)}, u32[]{:S(2)}) copy-start(bf16[128,1024]{1,0:T(8,128)(2,1)} %value_ref.5) | copy-start | bytes 786436
  103.6 23.7 %copy-start.17 = (bf16[128,1024]{1,0:T(8,128)(2,1)S(1)}, bf16[128,1024]{1,0:T(8,128)(2,1)}, u32[]{:S(2)}) copy-start(bf16[128,1024]{1,0:T(8,128)(2,1)} %get-tuple-element.26.upstream_ref) | copy-start | bytes 786436
  122.3 15.3 %all-to-all-start.3 = ((bf16[64,16,128]{2,1,0:T(8,128)(2,1)}), bf16[64,16,128]{2,1,0:T(8,128)(2,1)S(1)}, u32[]{:S(2)}, u32[]{:S(2)}) async-start(bf16[64,16,128]{2,1,0:T(8,128)(2,1)} %shard_map.147), calls=%async_computation.3 | async-start | bytes 524288 | tf_op jit(solution)/shard_map/all_to_all | solution.py:537

commit v5 on v4

--- a/solution.py
+++ b/solution.py
@@ -37,7 +37,7 @@
         in_specs=in_specs or [pl.BlockSpec(memory_space=pltpu.VMEM)] * len(args),
         out_specs=out_specs or jax.tree.map(lambda _: pl.BlockSpec(memory_space=pltpu.VMEM), out_shape),
         scratch_shapes=list(scratch),
-        compiler_params=pltpu.CompilerParams(vmem_limit_bytes=mib << 20),
+        compiler_params=pltpu.CompilerParams(vmem_limit_bytes=int(mib * 2**20)),
         cost_estimate=pl.CostEstimate(flops=flops, bytes_accessed=nbytes, transcendentals=0),
     )(*args)
 
@@ -191,27 +191,31 @@
     rest_ref[...] = hit.astype(BF16)
 
 
-def unpack(raw_ref, x_ref, c_ref):
-    count = raw_ref.shape[0]
+def unpack(raw_ref, x_ref, c_ref, first=0, last=None):
+    blocks = raw_ref.shape[0]
+    last = blocks if last is None else last
+    count = last - first
+    main = slice(first * 8, last * 8)
+    every = slice(blocks * 8 + first * 2, blocks * 8 + last * 2)
     for j in range(8):
-        tile = raw_ref[:, j * 16 : (j + 1) * 16, :].astype(F32).reshape(count, 2, 8, LANES)
+        tile = raw_ref[first:last, j * 16 : (j + 1) * 16, :].astype(F32).reshape(count, 2, 8, LANES)
         cols = slice(j * LANES, (j + 1) * LANES)
-        x_ref[0 : count * 8, cols] = tile[:, 0].reshape(count * 8, LANES).astype(BF16)
-        c_ref[0 : count * 8, cols] = tile[:, 1].reshape(count * 8, LANES).astype(BF16)
+        x_ref[main, cols] = tile[:, 0].reshape(count * 8, LANES).astype(BF16)
+        c_ref[main, cols] = tile[:, 1].reshape(count * 8, LANES).astype(BF16)
     row = iota((128, 128), 0)
     source = (row // 2) % 4 * 32 + row // 16 * 4 + (row // 8) % 2 * 2 + row % 2
     perm = (iota((128, 128), 1) == source).astype(BF16)
-    groups = count // 4
+    groups = range(first // 4, last // 4)
     rest = jnp.concatenate(
-        [raw_ref[g * 4 : (g + 1) * 4, 128:160, :].reshape(128, LANES) for g in range(groups)], axis=1
+        [raw_ref[g * 4 : (g + 1) * 4, 128:160, :].reshape(128, LANES) for g in groups], axis=1
     )
     rest = fast_dot(perm, rest)
     for j in range(8):
         cols = slice(j * LANES, (j + 1) * LANES)
         for kind, ref in enumerate((x_ref, c_ref)):
             lo = j * 16 + kind * 8
-            ref[count * 8 : count * 10, cols] = jnp.concatenate(
-                [rest[lo : lo + 8, g * LANES : (g + 1) * LANES] for g in range(groups)], axis=0
+            ref[every, cols] = jnp.concatenate(
+                [rest[lo : lo + 8, g * LANES : (g + 1) * LANES] for g in range(len(groups))], axis=0
             ).astype(BF16)
 
 
@@ -244,16 +248,21 @@
     x,
     c,
     down,
+    raw_sems,
     sems,
     peer_sems,
 ):
     mine = half_of(core_ref[0], x.shape[1])
     other = half_of(1 - core_ref[0], x.shape[1])
-    first = start_copies(((raw_hbm, raw), (gate_hbm.at[mine, :], gate)), sems)
+    quarter = raw.shape[0] // 4
+    quarters = [slice(q * quarter, (q + 1) * quarter) for q in range(4)]
+    rows = start_copies([(raw_hbm.at[span], raw.at[span]) for span in quarters], raw_sems)
+    first = start_copies(((gate_hbm.at[mine, :], gate),), sems)
+    for copy, span in zip(rows, quarters):
+        copy.wait()
+        unpack(raw, x, c, span.start, span.stop)
+    second = start_copies(((up_hbm.at[mine, :], up), (down_hbm.at[:, mine], down)), sems.at[pl.ds(1, 2)])
     first[0].wait()
-    second = start_copies(((up_hbm.at[mine, :], up), (down_hbm.at[:, mine], down)), sems.at[pl.ds(2, 2)])
-    unpack(raw, x, c)
-    first[1].wait()
     later = start_copies(
         ((gate_hbm.at[other, :], peer_gate), (up_hbm.at[other, :], peer_up), (down_hbm.at[:, other], peer_down)),
         peer_sems,
@@ -291,15 +300,8 @@
     project(dg, du, gate, up, keep_ref)
 
 
-def pack_kernel(keep_ref, got_ref, out_ref):
+def pack_kernel(keep_ref, got_ref, out_hbm, out_ref, sems):
     count = out_ref.shape[0]
-    for pair in range(4):
-        tiles = []
-        for j in (2 * pair, 2 * pair + 1):
-            cols = slice(j * LANES, (j + 1) * LANES)
-            value = keep_ref[0 : count * 8, cols] + got_ref[0 : count * 8, cols].astype(F32)
-            tiles.append(value.reshape(count, 8, LANES))
-        out_ref[:, pair * 16 : (pair + 1) * 16, :] = jnp.concatenate(tiles, axis=1).astype(BF16)
     rest = (keep_ref[count * 8 :, :] + got_ref[count * 8 :, :].astype(F32)).astype(BF16)
     row = iota((128, 128), 0)
     source = (row // 2) % 8 * 16 + row // 16 * 2 + row % 2
@@ -317,6 +319,26 @@
     moved = fast_dot(perm, stacked).astype(BF16)
     for g in range(groups):
         out_ref[g * 8 : (g + 1) * 8, 64:80, :] = moved[:, g * LANES : (g + 1) * LANES].reshape(8, 16, LANES)
+    copies = []
+
+    def send(first, last):
+        span = pl.ds(first, last - first)
+        copies.append(
+            pltpu.make_async_copy(out_ref.at[:, span, :], out_hbm.at[:, span, :], sems.at[len(copies)])
+        )
+        copies[-1].start()
+
+    send(64, 80)
+    for pair in range(4):
+        tiles = []
+        for j in (2 * pair, 2 * pair + 1):
+            cols = slice(j * LANES, (j + 1) * LANES)
+            value = keep_ref[0 : count * 8, cols] + got_ref[0 : count * 8, cols].astype(F32)
+            tiles.append(value.reshape(count, 8, LANES))
+        out_ref[:, pair * 16 : (pair + 1) * 16, :] = jnp.concatenate(tiles, axis=1).astype(BF16)
+        send(pair * 16, pair * 16 + 16)
+    for copy in copies:
+        copy.wait()
 
 
 def combine_kernel(back_ref, main_ref, rest_ref, hidden_ref, gain_ref, gained_ref, dot_ref):
@@ -608,8 +630,9 @@
             pltpu.VMEM((units, feats), BF16),
             pltpu.SemaphoreType.DMA((4,)),
             pltpu.SemaphoreType.DMA((3,)),
+            pltpu.SemaphoreType.DMA((3,)),
         ),
-        mib=40,
+        mib=39.5,
         flops=6 * slots * feats * units,
         nbytes=13 << 20,
     )
@@ -637,7 +660,16 @@
         flops=4 * slots * feats * units,
         nbytes=8 << 20,
     )
-    packed = call(pack_kernel, shape_of((ctx, 80, LANES), BF16), keep, got, flops=1 << 26, nbytes=6 << 20)
+    packed = call(
+        pack_kernel,
+        shape_of((ctx, 80, LANES), BF16),
+        keep,
+        got,
+        out_specs=hbm,
+        scratch=(pltpu.VMEM((ctx, 80, LANES), BF16), pltpu.SemaphoreType.DMA((5,))),
+        flops=1 << 26,
+        nbytes=6 << 20,
+    )
     back = exchange(packed)
     gained, dots = call(
         combine_kernel,

time: 141 us -> 141 us (level)
  no operation moved by 1% of the time
where the time goes in v5:
time: 141 us; the launch traced here: 140 us
  blocking collectives  65.5 us (46%)
  Pallas kernels  36.2 us (26%)
  waiting for transfers between devices  21.7 us (15%)
  starting transfers between devices  11.2 us (8%)
  local copies, waits for them, and re-layouts  3.86 us (3%)
    all_to_all x2, blocking collectives, exchange(): return lax.all_to_all(array, 'ctx', split_axis=0, concat_axis=0, tiled=True)  65.5 us
    pallas_call x11, Pallas kernels, call(): pl.pallas_call(kernel, out_shape=out_shape, in_specs=in_specs or [pl.Bloc...  36.2 us
    all_to_all x2, waiting for transfers between devices, exchange(): return lax.all_to_all(array, 'ctx', split_axis=0, concat_axis=0, tiled=True)  19.1 us
    all_to_all x2, starting transfers between devices, exchange(): return lax.all_to_all(array, 'ctx', split_axis=0, concat_axis=0, tiled=True)  10.4 us
    unnamed x36, local copies, waits for them, and re-layouts  3.86 us
  transfers between devices with their start and end apart: 6, of which 5 were waited for; matrix products, arithmetic and copies ran while one was open for 0% of the time, Pallas kernels for 13%

profile of v5, /device:TPU:0, one launch (start us, length us, event | category | flops | bytes accessed | tf_op | source)
XLA Modules:
  0.0 140.3 jit_solution(3997303326624693777)
XLA Ops:
  0.6 1.1 multiply_reduce_fusion
  1.7 0.1 collective-permute-start
  1.8 1.1 collective-permute-done
  2.9 0.0 copy-done.8
  2.9 0.5 copy-done.11
  3.4 4.0 %shard_map.138 = bf16[64,160,128]{2,1,0:T(8,128)(2,1)} custom-call(bf16[128,1024]{1,0:T(8,128)(2,1)} %h.3, bf16[128,1024]{1,0:T(8,128)(2,1)} %g.3, f32[1,128]{1,0:T(1,128)} %bitcast.11, f32[1,128]{1,0:T(1,128)} %bitcast.15, f32[1,1024]{1,0:T(1,128)} %bitcast.9, s32[4,128]{1,0:T(4,128)} %bitcast.13, f32[4,128]{1,0:T(4,128)} %bitcast.20), custom_call_target="tpu_custom_call" | custom-call | flops 16777216 | bytes 4096 | tf_op jit(solution)/shard_map/pallas_call | solution.py:34
  7.4 47.6 %all_to_all.20.raw_hbm = bf16[64,160,128]{2,1,0:T(8,128)(2,1)} all-to-all(bf16[64,160,128]{2,1,0:T(8,128)(2,1)} %shard_map.138), channel_id=1, replica_groups=mesh['ctx'=64,'tp'=2] {'ctx'}, dimensions={0} | all-to-all | bytes 5242880 | tf_op jit(solution)/shard_map/all_to_all | solution.py:559
  55.0 0.0 collective-permute-start.1
  55.0 6.7 %shard_map.139 = (f32[640,768]{1,0:T(8,128)S(1)}, f32[640,768]{1,0:T(8,128)S(1)}, f32[640,768]{1,0:T(8,128)S(1)}, bf16[1024,768]{1,0:T(8,128)(2,1)S(1)}, bf16[10...) custom-call(s32[1]{0:T(128)} %bitcast.5.core_ref, ...), custom_call_target="tpu_custom_call" | custom-call | flops 3019898880 | bytes 13631488 | tf_op jit(solution)/shard_map/pallas_call | solution.py:34
  61.7 0.0 collective-permute-done.1.raw_ref
  61.7 5.9 %shard_map.140 = (bf16[640,1024]{1,0:T(8,128)(2,1)S(1)}, bf16[640,768]{1,0:T(8,128)(2,1)S(1)}, bf16[640,768]{1,0:T(8,128)(2,1)S(1)}) custom-call(bf16[64,160,128]{2,1,0:T(8,128)(2,1)S(1)} %collective-permute-done.1.raw_ref, f32[640,768]{1,0:T(8,128)S(1)} %get-tuple-element.30.part_0, f32[640,768]{1,0:T(8,128)S(1)} %get-tuple-element.31.part_1, ...), custom_call_target="tpu_custom_call" | custom-call | flops 5033164800 | bytes 16777216 | tf_op jit(solution)/shard_map/pallas_call | solution.py:34
  67.6 0.6 collective-permute-start.2
  68.2 2.2 %shard_map.141.keep_ref = f32[640,1024]{1,0:T(8,128)S(1)} custom-call(bf16[640,768]{1,0:T(8,128)(2,1)S(1)} %get-tuple-element.36.dg, bf16[640,768]{1,0:T(8,128)(2,1)S(1)} %get-tuple-element.37.du, bf16[1024,768]{1,0:T(8,128)(2,1)S(1)} %get-tuple-element.38.gate, bf16[1024,768]{1,0:T(8,128)(2,1)S(1)} %get-tuple-element.39.up), custom_call_target="tpu_custom_call" | custom-call | flops 2013265920 | bytes 8388608 | tf_op jit(solution)/shard_map/pallas_call | solution.py:34
  70.4 0.4 collective-permute-done.2.got_ref
  70.9 1.5 %shard_map.142 = bf16[64,80,128]{2,1,0:T(8,128)(2,1)} custom-call(f32[640,1024]{1,0:T(8,128)S(1)} %shard_map.141.keep_ref, bf16[640,1024]{1,0:T(8,128)(2,1)S(1)} %collective-permute-done.2.got_ref), custom_call_target="tpu_custom_call" | custom-call | flops 67108864 | bytes 6291456 | tf_op jit(solution)/shard_map/pallas_call | solution.py:34
  72.4 0.0 copy-start.10
  72.4 5.5 %all-to-all-start.1 = ((bf16[64,80,128]{2,1,0:T(8,128)(2,1)}), bf16[64,80,128]{2,1,0:T(8,128)(2,1)S(1)}, u32[]{:S(2)}, u32[]{:S(2)}) async-start(bf16[64,80,128]{2,1,0:T(8,128)(2,1)} %shard_map.142), calls=%async_computation.1 | async-start | bytes 2621440 | tf_op jit(solution)/shard_map/all_to_all | solution.py:559
  77.9 0.0 copy-done.10
  77.9 0.0 copy-start.13
  77.9 0.9 copy-done.13
  78.8 0.9 copy-done.15
  79.8 2.0 %shard_map.143 = (bf16[256,1024]{1,0:T(8,128)(2,1)S(1)}, bf16[128,1024]{1,0:T(8,128)(2,1)S(1)}, f32[128,1024]{1,0:T(8,128)S(1)}, f32[64,8,128]{2,1,0:T(8,128)S(1)}, bf16[64,16,128]{2,1,0:T(8,128)(2,1)S(1)}) custom-call(s32[4,128]{1,0:T(4,128)S(1)} %bitcast.14, bf16[128,1024]{1,0:T(8,128)(2,1)S(1)} %copy-done.13, bf16[128,1024]{1,0:T(8,128)(2,1)S(1)} %copy-done.15), custom_call_target="tpu_custom_call" | custom-call | flops 1073741824 | bytes 4194304 | tf_op jit(solution)/shard_map/pallas_call | solution.py:34
  81.8 0.0 copy-start.3
  81.8 0.7 copy-done.3
  82.5 0.7 copy-done.5
  83.2 16.5 %all-to-all-done.1.back_ref = bf16[64,80,128]{2,1,0:T(8,128)(2,1)S(1)} async-done(((bf16[64,80,128]{2,1,0:T(8,128)(2,1)}), bf16[64,80,128]{2,1,0:T(8,128)(2,1)S(1)}, u32[]{:S(2)}, u32[]{:S(2)}) %all-to-all-start.1) | async-done | bytes 1310752 | tf_op jit(solution)/shard_map/all_to_all | solution.py:559
  99.6 0.0 copy-done
  99.7 0.0 copy-done.7
  99.7 1.1 shard_map.144
  100.7 0.1 collective-permute-start.3
  100.8 1.1 collective-permute-done.3.e
  101.9 0.0 copy-done.1
  101.9 0.0 copy-done.2
  101.9 0.0 copy-done.9
  101.9 0.0 copy-done.12
  102.0 0.0 copy-done.4
  102.0 0.0 copy-done.6
  102.0 0.0 copy-start.14
  102.0 0.0 copy-start.16
  102.0 1.1 shard_map.145
  103.1 17.9 %all_to_all.21.piece_ref = bf16[64,32,128]{2,1,0:T(8,128)(2,1)S(1)} all-to-all(bf16[64,32,128]{2,1,0:T(8,128)(2,1)S(1)} %get-tuple-element.52), channel_id=1, replica_groups=mesh['ctx'=64,'tp'=2] {'ctx'}, dimensions={0} | all-to-all | bytes 1048576 | tf_op jit(solution)/shard_map/all_to_all | solution.py:559
  121.0 0.8 shard_map.147
  121.8 4.9 %all-to-all-start.3 = ((bf16[64,16,128]{2,1,0:T(8,128)(2,1)}), bf16[64,16,128]{2,1,0:T(8,128)(2,1)S(1)}, u32[]{:S(2)}, u32[]{:S(2)}) async-start(bf16[64,16,128]{2,1,0:T(8,128)(2,1)} %shard_map.147), calls=%async_computation.3 | async-start | bytes 524288 | tf_op jit(solution)/shard_map/all_to_all | solution.py:559
  126.7 0.0 copy-done.14
  126.7 0.0 copy-done.16
  126.8 7.8 %shard_map.146 = (f32[128,1024]{1,0:T(8,128)S(1)}, f32[128,1024]{1,0:T(8,128)S(1)}, bf16[128,1024]{1,0:T(8,128)(2,1)S(1)}) custom-call(bf16[128,1024]{1,0:T(8,128)(2,1)S(1)} %copy-done.2, bf16[128,1024]{1,0:T(8,128)(2,1)S(1)} %copy-done.14, bf16[128,1024]{1,0:T(8,128)(2,1)S(1)} %copy-done.16, f32[128,1024]{1,0:T(8,128)S(1)} %get-tuple-element.45.t.total_ref, ...), custom_call_target="tpu_custom_call" | custom-call | flops 4294967296 | bytes 4194304 | tf_op jit(solution)/shard_map/pallas_call | solution.py:34
  134.6 2.6 %all-to-all-done.3.carried_ref = bf16[64,16,128]{2,1,0:T(8,128)(2,1)S(1)} async-done(((bf16[64,16,128]{2,1,0:T(8,128)(2,1)}), bf16[64,16,128]{2,1,0:T(8,128)(2,1)S(1)}, u32[]{:S(2)}, u32[]{:S(2)}) %all-to-all-start.3) | async-done | bytes 262176 | tf_op jit(solution)/shard_map/all_to_all | solution.py:559
  137.2 3.1 %shard_map.148 = (bf16[128,1024]{1,0:T(8,128)(2,1)}, bf16[128,1024]{1,0:T(8,128)(2,1)}, bf16[128,1024]{1,0:T(8,128)(2,1)}) custom-call(bf16[128,1024]{1,0:T(8,128)(2,1)S(1)} %copy-done.2, bf16[128,1024]{1,0:T(8,128)(2,1)S(1)} %copy-done.14, bf16[128,1024]{1,0:T(8,128)(2,1)S(1)} %copy-done.16, bf16[128,1024]{1,0:T(8,128)(2,1)S(1)} %copy-done.17, ...), custom_call_target="tpu_custom_call" | custom-call | flops 1073741824 | bytes 4194304 | tf_op jit(solution)/shard_map/pallas_call | solution.py:34
  (14 shorter events, 0.0 us)
Async XLA Ops:
  1.7 1.2 copy-start.8
  1.7 1.2 collective-permute-start
  2.9 0.5 copy-start.11
  55.0 6.8 %collective-permute-start.1 = (bf16[64,160,128]{2,1,0:T(8,128)(2,1)}, bf16[64,160,128]{2,1,0:T(8,128)(2,1)S(1)}, u32[]{:S(2)}, u32[]{:S(2)}) collective-permute-start(bf16[64,160,128]{2,1,0:T(8,128)(2,1)} %all_to_all.20.raw_hbm), channel_id=1, source_target_pairs={{0,1},{1,0},{2,3},{3,2},{4,5},{5,4},{6,7},{7,6},{8,9},{9,8},{10,11... | collective-permute-start | bytes 7864328 | tf_op jit(solution)/shard_map/ppermute | solution.py:614
  67.6 3.3 %collective-permute-start.2 = (bf16[640,1024]{1,0:T(8,128)(2,1)S(1)}, bf16[640,1024]{1,0:T(8,128)(2,1)S(1)}, u32[]{:S(2)}, u32[]{:S(2)}) collective-permute-start(bf16[640,1024]{1,0:T(8,128)(2,1)S(1)} %get-tuple-element.40), channel_id=1, source_target_pairs={{0,1},{1,0},{2,3},{3,2},{4,5},{5,4},{6,7},{7,6},{8,9},{9,8},{10,11... | collective-permute-start | bytes 3932168 | tf_op jit(solution)/shard_map/ppermute | solution.py:652
  72.4 5.5 %copy-start.10 = (s32[128,4]{0,1:T(4,128)S(1)}, s32[128,4]{0,1:T(4,128)}, u32[]{:S(2)}) copy-start(s32[128,4]{0,1:T(4,128)} %param.13) | copy-start | bytes 6148
  72.4 27.3 %all-to-all-start.1 = ((bf16[64,80,128]{2,1,0:T(8,128)(2,1)}), bf16[64,80,128]{2,1,0:T(8,128)(2,1)S(1)}, u32[]{:S(2)}, u32[]{:S(2)}) async-start(bf16[64,80,128]{2,1,0:T(8,128)(2,1)} %shard_map.142), calls=%async_computation.1 | async-start | bytes 2621440 | tf_op jit(solution)/shard_map/all_to_all | solution.py:559
  77.9 1.0 copy-start.13
  78.8 0.9 copy-start.15
  79.8 19.9 %copy-start = (bf16[128,1024]{1,0:T(8,128)(2,1)S(1)}, bf16[128,1024]{1,0:T(8,128)(2,1)}, u32[]{:S(2)}) copy-start(bf16[128,1024]{1,0:T(8,128)(2,1)} %h.3) | copy-start | bytes 786436
  79.8 19.9 %copy-start.7 = (f32[1024]{0:T(1024)S(1)}, f32[1024]{0:T(1024)}, u32[]{:S(2)}) copy-start(f32[1024]{0:T(1024)} %param.15) | copy-start | bytes 12292
  81.8 0.7 copy-start.3
  82.5 0.7 copy-start.5
  83.2 18.8 %copy-start.1 = (bf16[128,1024]{1,0:T(8,128)(2,1)S(1)}, bf16[128,1024]{1,0:T(8,128)(2,1)}, u32[]{:S(2)}) copy-start(bf16[128,1024]{1,0:T(8,128)(2,1)} %g.3) | copy-start | bytes 786436
  83.2 18.8 %copy-start.2 = (bf16[128,1024]{1,0:T(8,128)(2,1)S(1)}, bf16[128,1024]{1,0:T(8,128)(2,1)}, u32[]{:S(2)}) copy-start(bf16[128,1024]{1,0:T(8,128)(2,1)} %query_ref.3) | copy-start | bytes 786436
  83.2 18.8 %copy-start.9 = (f32[128]{0:T(128)S(1)}, f32[128]{0:T(128)}, u32[]{:S(2)}) copy-start(f32[128]{0:T(128)} %copy-done.8) | copy-start | bytes 1540
  83.2 18.8 %copy-start.12 = (f32[128]{0:T(128)S(1)}, f32[128]{0:T(128)}, u32[]{:S(2)}) copy-start(f32[128]{0:T(128)} %copy-done.11) | copy-start | bytes 1540
  99.6 2.3 %copy-start.4 = (f32[64,8,128]{2,1,0:T(8,128)S(1)}, f32[64,8,128]{2,1,0:T(8,128)}, u32[]{:S(2)}) copy-start(f32[64,8,128]{2,1,0:T(8,128)} %copy-done.3) | copy-start | bytes 786436
  99.6 2.3 %copy-start.6 = (bf16[64,16,128]{2,1,0:T(8,128)(2,1)S(1)}, bf16[64,16,128]{2,1,0:T(8,128)(2,1)}, u32[]{:S(2)}) copy-start(bf16[64,16,128]{2,1,0:T(8,128)(2,1)} %copy-done.5) | copy-start | bytes 786436
  100.7 1.2 collective-permute-start.3
  102.0 24.8 %copy-start.14 = (bf16[128,1024]{1,0:T(8,128)(2,1)S(1)}, bf16[128,1024]{1,0:T(8,128)(2,1)}, u32[]{:S(2)}) copy-start(bf16[128,1024]{1,0:T(8,128)(2,1)} %logit_ref.5) | copy-start | bytes 786436
  102.0 24.8 %copy-start.16 = (bf16[128,1024]{1,0:T(8,128)(2,1)S(1)}, bf16[128,1024]{1,0:T(8,128)(2,1)}, u32[]{:S(2)}) copy-start(bf16[128,1024]{1,0:T(8,128)(2,1)} %value_ref.5) | copy-start | bytes 786436
  103.1 23.7 %copy-start.17 = (bf16[128,1024]{1,0:T(8,128)(2,1)S(1)}, bf16[128,1024]{1,0:T(8,128)(2,1)}, u32[]{:S(2)}) copy-start(bf16[128,1024]{1,0:T(8,128)(2,1)} %get-tuple-element.26.upstream_ref) | copy-start | bytes 786436
  121.8 15.3 %all-to-all-start.3 = ((bf16[64,16,128]{2,1,0:T(8,128)(2,1)}), bf16[64,16,128]{2,1,0:T(8,128)(2,1)S(1)}, u32[]{:S(2)}, u32[]{:S(2)}) async-start(bf16[64,16,128]{2,1,0:T(8,128)(2,1)} %shard_map.147), calls=%async_computation.3 | async-start | bytes 524288 | tf_op jit(solution)/shard_map/all_to_all | solution.py:559

commit v6 on v5

--- a/solution.py
+++ b/solution.py
@@ -113,13 +113,6 @@
     rank_b = ranked(ids, count).astype(BF16)
     loads[1].wait()
     weight = named_by(ids, count, weight_in)
-    for load in loads[2:]:
-        load.wait()
-    row_scale = row_scale_of(own_sq, peer_sq, width)
-    rhs[0:rows, :] = (hidden[...].astype(F32) * row_scale * gain[...]).astype(BF16)
-    for j in range(8):
-        lo, col = 2 * rows * (j % 4), LANES * (j // 4)
-        rhs_rem[lo : lo + 2 * rows, col : col + LANES] = rhs[:, j * LANES : (j + 1) * LANES]
     slots = count * 16
     inner = iota((slots, LANES), 0) % 16
     main_cot = inner >= 8
@@ -146,12 +139,19 @@
         )
         copies[-1].start()
 
+    for load in loads[2:]:
+        load.wait()
+    row_scale = row_scale_of(own_sq, peer_sq, width)
+    rhs[0:rows, :] = (hidden[...].astype(F32) * row_scale * gain[...]).astype(BF16)
     for pair in range(4):
         value = (fast_dot(left, rhs[:, pair * 256 : (pair + 1) * 256]) * scale).astype(BF16)
         for half in range(2):
             first = pair * 32 + half * 16
             out_ref[:, first : first + 16, :] = value[:, half * LANES : (half + 1) * LANES].reshape(count, 16, LANES)
         send(pair * 32, pair * 32 + 32)
+    for j in range(8):
+        lo, col = 2 * rows * (j % 4), LANES * (j // 4)
+        rhs_rem[lo : lo + 2 * rows, col : col + LANES] = rhs[:, j * LANES : (j + 1) * LANES]
     hit = ranks == (8 + inner % 2).astype(F32)
     hit_b = hit.astype(BF16)
     left = jnp.concatenate(

time: 141 us -> 141 us (level)
  no operation moved by 1% of the time
where the time goes in v6:
time: 141 us; the launch traced here: 140 us
  blocking collectives  65.5 us (46%)
  Pallas kernels  36.2 us (26%)
  waiting for transfers between devices  21.7 us (15%)
  starting transfers between devices  11.2 us (8%)
  local copies, waits for them, and re-layouts  3.86 us (3%)
    all_to_all x2, blocking collectives, exchange(): return lax.all_to_all(array, 'ctx', split_axis=0, concat_axis=0, tiled=True)  65.5 us
    pallas_call x11, Pallas kernels, call(): pl.pallas_call(kernel, out_shape=out_shape, in_specs=in_specs or [pl.Bloc...  36.2 us
    all_to_all x2, waiting for transfers between devices, exchange(): return lax.all_to_all(array, 'ctx', split_axis=0, concat_axis=0, tiled=True)  19.1 us
    all_to_all x2, starting transfers between devices, exchange(): return lax.all_to_all(array, 'ctx', split_axis=0, concat_axis=0, tiled=True)  10.4 us
    unnamed x36, local copies, waits for them, and re-layouts  3.86 us
  transfers between devices with their start and end apart: 6, of which 5 were waited for; matrix products, arithmetic and copies ran while one was open for 0% of the time, Pallas kernels for 13%

profile of v6, /device:TPU:0, one launch (start us, length us, event | category | flops | bytes accessed | tf_op | source)
XLA Modules:
  0.0 140.3 jit_solution(14407289418301839712)
XLA Ops:
  0.6 1.1 multiply_reduce_fusion
  1.7 0.1 collective-permute-start
  1.8 1.1 collective-permute-done
  2.9 0.0 copy-done.8
  2.9 0.5 copy-done.11
  3.4 4.0 %shard_map.138 = bf16[64,160,128]{2,1,0:T(8,128)(2,1)} custom-call(bf16[128,1024]{1,0:T(8,128)(2,1)} %h.3, bf16[128,1024]{1,0:T(8,128)(2,1)} %g.3, f32[1,128]{1,0:T(1,128)} %bitcast.11, f32[1,128]{1,0:T(1,128)} %bitcast.15, f32[1,1024]{1,0:T(1,128)} %bitcast.9, s32[4,128]{1,0:T(4,128)} %bitcast.13, f32[4,128]{1,0:T(4,128)} %bitcast.20), custom_call_target="tpu_custom_call" | custom-call | flops 16777216 | bytes 4096 | tf_op jit(solution)/shard_map/pallas_call | solution.py:34
  7.4 47.6 %all_to_all.20.raw_hbm = bf16[64,160,128]{2,1,0:T(8,128)(2,1)} all-to-all(bf16[64,160,128]{2,1,0:T(8,128)(2,1)} %shard_map.138), channel_id=1, replica_groups=mesh['ctx'=64,'tp'=2] {'ctx'}, dimensions={0} | all-to-all | bytes 5242880 | tf_op jit(solution)/shard_map/all_to_all | solution.py:559
  55.0 0.0 collective-permute-start.1
  55.0 6.7 %shard_map.139 = (f32[640,768]{1,0:T(8,128)S(1)}, f32[640,768]{1,0:T(8,128)S(1)}, f32[640,768]{1,0:T(8,128)S(1)}, bf16[1024,768]{1,0:T(8,128)(2,1)S(1)}, bf16[10...) custom-call(s32[1]{0:T(128)} %bitcast.5.core_ref, ...), custom_call_target="tpu_custom_call" | custom-call | flops 3019898880 | bytes 13631488 | tf_op jit(solution)/shard_map/pallas_call | solution.py:34
  61.7 0.0 collective-permute-done.1.raw_ref
  61.7 5.9 %shard_map.140 = (bf16[640,1024]{1,0:T(8,128)(2,1)S(1)}, bf16[640,768]{1,0:T(8,128)(2,1)S(1)}, bf16[640,768]{1,0:T(8,128)(2,1)S(1)}) custom-call(bf16[64,160,128]{2,1,0:T(8,128)(2,1)S(1)} %collective-permute-done.1.raw_ref, f32[640,768]{1,0:T(8,128)S(1)} %get-tuple-element.30.part_0, f32[640,768]{1,0:T(8,128)S(1)} %get-tuple-element.31.part_1, ...), custom_call_target="tpu_custom_call" | custom-call | flops 5033164800 | bytes 16777216 | tf_op jit(solution)/shard_map/pallas_call | solution.py:34
  67.6 0.6 collective-permute-start.2
  68.2 2.2 %shard_map.141.keep_ref = f32[640,1024]{1,0:T(8,128)S(1)} custom-call(bf16[640,768]{1,0:T(8,128)(2,1)S(1)} %get-tuple-element.36.dg, bf16[640,768]{1,0:T(8,128)(2,1)S(1)} %get-tuple-element.37.du, bf16[1024,768]{1,0:T(8,128)(2,1)S(1)} %get-tuple-element.38.gate, bf16[1024,768]{1,0:T(8,128)(2,1)S(1)} %get-tuple-element.39.up), custom_call_target="tpu_custom_call" | custom-call | flops 2013265920 | bytes 8388608 | tf_op jit(solution)/shard_map/pallas_call | solution.py:34
  70.4 0.4 collective-permute-done.2.got_ref
  70.9 1.5 %shard_map.142 = bf16[64,80,128]{2,1,0:T(8,128)(2,1)} custom-call(f32[640,1024]{1,0:T(8,128)S(1)} %shard_map.141.keep_ref, bf16[640,1024]{1,0:T(8,128)(2,1)S(1)} %collective-permute-done.2.got_ref), custom_call_target="tpu_custom_call" | custom-call | flops 67108864 | bytes 6291456 | tf_op jit(solution)/shard_map/pallas_call | solution.py:34
  72.4 0.0 copy-start.10
  72.4 5.5 %all-to-all-start.1 = ((bf16[64,80,128]{2,1,0:T(8,128)(2,1)}), bf16[64,80,128]{2,1,0:T(8,128)(2,1)S(1)}, u32[]{:S(2)}, u32[]{:S(2)}) async-start(bf16[64,80,128]{2,1,0:T(8,128)(2,1)} %shard_map.142), calls=%async_computation.1 | async-start | bytes 2621440 | tf_op jit(solution)/shard_map/all_to_all | solution.py:559
  77.9 0.0 copy-done.10
  77.9 0.0 copy-start.13
  77.9 0.9 copy-done.13
  78.9 0.9 copy-done.15
  79.8 2.0 %shard_map.143 = (bf16[256,1024]{1,0:T(8,128)(2,1)S(1)}, bf16[128,1024]{1,0:T(8,128)(2,1)S(1)}, f32[128,1024]{1,0:T(8,128)S(1)}, f32[64,8,128]{2,1,0:T(8,128)S(1)}, bf16[64,16,128]{2,1,0:T(8,128)(2,1)S(1)}) custom-call(s32[4,128]{1,0:T(4,128)S(1)} %bitcast.14, bf16[128,1024]{1,0:T(8,128)(2,1)S(1)} %copy-done.13, bf16[128,1024]{1,0:T(8,128)(2,1)S(1)} %copy-done.15), custom_call_target="tpu_custom_call" | custom-call | flops 1073741824 | bytes 4194304 | tf_op jit(solution)/shard_map/pallas_call | solution.py:34
  81.8 0.0 copy-start.3
  81.8 0.7 copy-done.3
  82.5 0.7 copy-done.5
  83.2 16.5 %all-to-all-done.1.back_ref = bf16[64,80,128]{2,1,0:T(8,128)(2,1)S(1)} async-done(((bf16[64,80,128]{2,1,0:T(8,128)(2,1)}), bf16[64,80,128]{2,1,0:T(8,128)(2,1)S(1)}, u32[]{:S(2)}, u32[]{:S(2)}) %all-to-all-start.1) | async-done | bytes 1310752 | tf_op jit(solution)/shard_map/all_to_all | solution.py:559
  99.7 0.0 copy-done
  99.7 0.0 copy-done.7
  99.7 1.1 shard_map.144
  100.8 0.1 collective-permute-start.3
  100.8 1.1 collective-permute-done.3.e
  102.0 0.0 copy-done.1
  102.0 0.0 copy-done.2
  102.0 0.0 copy-done.9
  102.0 0.0 copy-done.12
  102.0 0.0 copy-done.4
  102.0 0.0 copy-done.6
  102.0 0.0 copy-start.14
  102.0 0.0 copy-start.16
  102.0 1.1 shard_map.145
  103.1 17.9 %all_to_all.21.piece_ref = bf16[64,32,128]{2,1,0:T(8,128)(2,1)S(1)} all-to-all(bf16[64,32,128]{2,1,0:T(8,128)(2,1)S(1)} %get-tuple-element.52), channel_id=1, replica_groups=mesh['ctx'=64,'tp'=2] {'ctx'}, dimensions={0} | all-to-all | bytes 1048576 | tf_op jit(solution)/shard_map/all_to_all | solution.py:559
  121.0 0.8 shard_map.147
  121.8 4.9 %all-to-all-start.3 = ((bf16[64,16,128]{2,1,0:T(8,128)(2,1)}), bf16[64,16,128]{2,1,0:T(8,128)(2,1)S(1)}, u32[]{:S(2)}, u32[]{:S(2)}) async-start(bf16[64,16,128]{2,1,0:T(8,128)(2,1)} %shard_map.147), calls=%async_computation.3 | async-start | bytes 524288 | tf_op jit(solution)/shard_map/all_to_all | solution.py:559
  126.7 0.0 copy-done.14
  126.8 0.0 copy-done.16
  126.8 7.8 %shard_map.146 = (f32[128,1024]{1,0:T(8,128)S(1)}, f32[128,1024]{1,0:T(8,128)S(1)}, bf16[128,1024]{1,0:T(8,128)(2,1)S(1)}) custom-call(bf16[128,1024]{1,0:T(8,128)(2,1)S(1)} %copy-done.2, bf16[128,1024]{1,0:T(8,128)(2,1)S(1)} %copy-done.14, bf16[128,1024]{1,0:T(8,128)(2,1)S(1)} %copy-done.16, f32[128,1024]{1,0:T(8,128)S(1)} %get-tuple-element.45.t.total_ref, ...), custom_call_target="tpu_custom_call" | custom-call | flops 4294967296 | bytes 4194304 | tf_op jit(solution)/shard_map/pallas_call | solution.py:34
  134.6 2.6 %all-to-all-done.3.carried_ref = bf16[64,16,128]{2,1,0:T(8,128)(2,1)S(1)} async-done(((bf16[64,16,128]{2,1,0:T(8,128)(2,1)}), bf16[64,16,128]{2,1,0:T(8,128)(2,1)S(1)}, u32[]{:S(2)}, u32[]{:S(2)}) %all-to-all-start.3) | async-done | bytes 262176 | tf_op jit(solution)/shard_map/all_to_all | solution.py:559
  137.2 3.1 %shard_map.148 = (bf16[128,1024]{1,0:T(8,128)(2,1)}, bf16[128,1024]{1,0:T(8,128)(2,1)}, bf16[128,1024]{1,0:T(8,128)(2,1)}) custom-call(bf16[128,1024]{1,0:T(8,128)(2,1)S(1)} %copy-done.2, bf16[128,1024]{1,0:T(8,128)(2,1)S(1)} %copy-done.14, bf16[128,1024]{1,0:T(8,128)(2,1)S(1)} %copy-done.16, bf16[128,1024]{1,0:T(8,128)(2,1)S(1)} %copy-done.17, ...), custom_call_target="tpu_custom_call" | custom-call | flops 1073741824 | bytes 4194304 | tf_op jit(solution)/shard_map/pallas_call | solution.py:34
  (14 shorter events, 0.0 us)
Async XLA Ops:
  1.7 1.2 copy-start.8
  1.7 1.2 collective-permute-start
  2.9 0.5 copy-start.11
  55.0 6.8 %collective-permute-start.1 = (bf16[64,160,128]{2,1,0:T(8,128)(2,1)}, bf16[64,160,128]{2,1,0:T(8,128)(2,1)S(1)}, u32[]{:S(2)}, u32[]{:S(2)}) collective-permute-start(bf16[64,160,128]{2,1,0:T(8,128)(2,1)} %all_to_all.20.raw_hbm), channel_id=1, source_target_pairs={{0,1},{1,0},{2,3},{3,2},{4,5},{5,4},{6,7},{7,6},{8,9},{9,8},{10,11... | collective-permute-start | bytes 7864328 | tf_op jit(solution)/shard_map/ppermute | solution.py:614
  67.6 3.2 %collective-permute-start.2 = (bf16[640,1024]{1,0:T(8,128)(2,1)S(1)}, bf16[640,1024]{1,0:T(8,128)(2,1)S(1)}, u32[]{:S(2)}, u32[]{:S(2)}) collective-permute-start(bf16[640,1024]{1,0:T(8,128)(2,1)S(1)} %get-tuple-element.40), channel_id=1, source_target_pairs={{0,1},{1,0},{2,3},{3,2},{4,5},{5,4},{6,7},{7,6},{8,9},{9,8},{10,11... | collective-permute-start | bytes 3932168 | tf_op jit(solution)/shard_map/ppermute | solution.py:652
  72.4 5.5 %copy-start.10 = (s32[128,4]{0,1:T(4,128)S(1)}, s32[128,4]{0,1:T(4,128)}, u32[]{:S(2)}) copy-start(s32[128,4]{0,1:T(4,128)} %param.13) | copy-start | bytes 6148
  72.4 27.3 %all-to-all-start.1 = ((bf16[64,80,128]{2,1,0:T(8,128)(2,1)}), bf16[64,80,128]{2,1,0:T(8,128)(2,1)S(1)}, u32[]{:S(2)}, u32[]{:S(2)}) async-start(bf16[64,80,128]{2,1,0:T(8,128)(2,1)} %shard_map.142), calls=%async_computation.1 | async-start | bytes 2621440 | tf_op jit(solution)/shard_map/all_to_all | solution.py:559
  77.9 1.0 copy-start.13
  78.9 0.9 copy-start.15
  79.8 19.9 %copy-start = (bf16[128,1024]{1,0:T(8,128)(2,1)S(1)}, bf16[128,1024]{1,0:T(8,128)(2,1)}, u32[]{:S(2)}) copy-start(bf16[128,1024]{1,0:T(8,128)(2,1)} %h.3) | copy-start | bytes 786436
  79.8 19.9 %copy-start.7 = (f32[1024]{0:T(1024)S(1)}, f32[1024]{0:T(1024)}, u32[]{:S(2)}) copy-start(f32[1024]{0:T(1024)} %param.15) | copy-start | bytes 12292
  81.8 0.7 copy-start.3
  82.5 0.7 copy-start.5
  83.2 18.8 %copy-start.1 = (bf16[128,1024]{1,0:T(8,128)(2,1)S(1)}, bf16[128,1024]{1,0:T(8,128)(2,1)}, u32[]{:S(2)}) copy-start(bf16[128,1024]{1,0:T(8,128)(2,1)} %g.3) | copy-start | bytes 786436
  83.2 18.8 %copy-start.2 = (bf16[128,1024]{1,0:T(8,128)(2,1)S(1)}, bf16[128,1024]{1,0:T(8,128)(2,1)}, u32[]{:S(2)}) copy-start(bf16[128,1024]{1,0:T(8,128)(2,1)} %query_ref.3) | copy-start | bytes 786436
  83.2 18.8 %copy-start.9 = (f32[128]{0:T(128)S(1)}, f32[128]{0:T(128)}, u32[]{:S(2)}) copy-start(f32[128]{0:T(128)} %copy-done.8) | copy-start | bytes 1540
  83.2 18.8 %copy-start.12 = (f32[128]{0:T(128)S(1)}, f32[128]{0:T(128)}, u32[]{:S(2)}) copy-start(f32[128]{0:T(128)} %copy-done.11) | copy-start | bytes 1540
  99.7 2.3 %copy-start.4 = (f32[64,8,128]{2,1,0:T(8,128)S(1)}, f32[64,8,128]{2,1,0:T(8,128)}, u32[]{:S(2)}) copy-start(f32[64,8,128]{2,1,0:T(8,128)} %copy-done.3) | copy-start | bytes 786436
  99.7 2.3 %copy-start.6 = (bf16[64,16,128]{2,1,0:T(8,128)(2,1)S(1)}, bf16[64,16,128]{2,1,0:T(8,128)(2,1)}, u32[]{:S(2)}) copy-start(bf16[64,16,128]{2,1,0:T(8,128)(2,1)} %copy-done.5) | copy-start | bytes 786436
  100.8 1.2 collective-permute-start.3
  102.0 24.8 %copy-start.14 = (bf16[128,1024]{1,0:T(8,128)(2,1)S(1)}, bf16[128,1024]{1,0:T(8,128)(2,1)}, u32[]{:S(2)}) copy-start(bf16[128,1024]{1,0:T(8,128)(2,1)} %logit_ref.5) | copy-start | bytes 786436
  102.0 24.8 %copy-start.16 = (bf16[128,1024]{1,0:T(8,128)(2,1)S(1)}, bf16[128,1024]{1,0:T(8,128)(2,1)}, u32[]{:S(2)}) copy-start(bf16[128,1024]{1,0:T(8,128)(2,1)} %value_ref.5) | copy-start | bytes 786436
  103.1 23.7 %copy-start.17 = (bf16[128,1024]{1,0:T(8,128)(2,1)S(1)}, bf16[128,1024]{1,0:T(8,128)(2,1)}, u32[]{:S(2)}) copy-start(bf16[128,1024]{1,0:T(8,128)(2,1)} %get-tuple-element.26.upstream_ref) | copy-start | bytes 786436
  121.8 15.3 %all-to-all-start.3 = ((bf16[64,16,128]{2,1,0:T(8,128)(2,1)}), bf16[64,16,128]{2,1,0:T(8,128)(2,1)S(1)}, u32[]{:S(2)}, u32[]{:S(2)}) async-start(bf16[64,16,128]{2,1,0:T(8,128)(2,1)} %shard_map.147), calls=%async_computation.3 | async-start | bytes 524288 | tf_op jit(solution)/shard_map/all_to_all | solution.py:559
